TPU v7x, 32 devices: a whole 2x2x4 slice. The times are simulated.
32 devices in a mesh: dp: 8 (over z, y), heads: 4 (over x, core).
Axes of the slice: x: 2, y: 2, z: 4, core: 2. Of those that a mesh axis runs over, the one named last changes fastest.
Arguments:
- tokens: bfloat16 [16384, 1024], P('dp', 'heads'), may hold values from -6 to 6
- cotangent: bfloat16 [16384, 1024], P('dp', 'heads'), may hold values from -6 to 6
- scan_block_starts: int32 [128], P('dp'), may hold values from 0 to 1, as said below
- scan_block_fill: int32 [128], P('dp'), may hold values from 32 to 128, as said below
- norm_gain: float32 [1024], replicated, may hold values from 0.1 to 1.9
- w_x: bfloat16 [1024, 2048], P('dp', 'heads'), may hold values from -0.1875 to 0.1875
- w_z: bfloat16 [1024, 2048], P('dp', 'heads'), may hold values from -0.1875 to 0.1875
- w_dt: bfloat16 [1024, 32], P('dp', 'heads'), may hold values from -0.1875 to 0.1875
- w_bc: bfloat16 [1024, 256], P('dp'), may hold values from -0.1875 to 0.1875
- conv_x: float32 [4, 2048], P(None, 'heads'), may hold values from -3 to 3
- conv_bc: float32 [4, 256], replicated, may hold values from -3 to 3
- dt_bias: float32 [32], P('heads'), may hold values from -6 to -2
- a_log: float32 [32], P('heads'), may hold values from 0 to 2.77
- skip: float32 [32], P('heads'), may hold values from 0.5 to 1.5
- gate_gain: float32 [2048], P('heads'), may hold values from 0.1 to 1.9
- w_out: bfloat16 [1024, 2048], P('dp', 'heads'), may hold values from -0.125 to 0.125
Outputs:
- block_out: bfloat16 [16384, 1024], P('dp', 'heads')
- grad_tokens: float32 [16384, 1024], P('dp', 'heads')
- grad_norm_gain: float32 [1024], P('heads')
- grad_w_x: float32 [1024, 2048], P('dp', 'heads')
- grad_w_z: float32 [1024, 2048], P('dp', 'heads')
- grad_w_dt: float32 [1024, 32], P('dp', 'heads')
- grad_w_bc: float32 [1024, 256], P('dp')
- grad_conv_x: float32 [4, 2048], P(None, 'heads')
- grad_conv_bc: float32 [4, 256], replicated
- grad_dt_bias: float32 [32], P('heads')
- grad_a_log: float32 [32], P('heads')
- grad_skip: float32 [32], P('heads')
- grad_gate_gain: float32 [2048], P('heads')
- grad_w_out: float32 [1024, 2048], P('dp', 'heads')
Inputs may be any that keep to these rules, and one draw needn't show every extreme that they name: `scan_block_starts`: scenes never span two indices of dp: the first block of each 2048 tokens always begins a scene and its second never does. `scan_block_fill`: only the last block of a scene may be partly padded; the first block of every 2048 tokens is full.
All inputs are finite; a program needn't handle non-finite values.
Results may differ from a plain program's by a relative error of at most 0.01.
Values may be sent and summed in bfloat16 or wider, within the bound.
A program may use at most 192 MiB of HBM per device.

v0:
```python
import jax
import jax.numpy as jnp
from jax import lax
from jax.sharding import PartitionSpec as P

HD = 64


eps_norm = 1e-05
highest = lax.Precision.HIGHEST


def embedding_index_arrays(environment_boundary_indices, padded_matrix_entries, length):
    blocks = environment_boundary_indices.shape[0]
    span = length // blocks
    inside_segment = jnp.arange(length, dtype=jnp.int32) % span
    environment_beginning = jnp.repeat(environment_boundary_indices, span)
    segment_boundaries = jnp.repeat(padded_matrix_entries, span)
    embedding_validity_mask = (inside_segment < segment_boundaries).astype(jnp.float32)
    return (environment_beginning, inside_segment, embedding_validity_mask)


def leftward_convolution_kernel(signal, kernel_coefficients, environment_beginning, inside_segment):
    taps = kernel_coefficients.shape[0]
    result = kernel_coefficients[taps - 1] * signal
    for distance in range(1, taps):
        moved = jnp.concatenate(
            [jnp.zeros((distance, signal.shape[1]), jnp.float32), signal[:-distance]], axis=0
        )
        allowed = 1.0 - ((environment_beginning == 1) & (inside_segment < distance)).astype(
            jnp.float32
        )
        result = result + kernel_coefficients[taps - 1 - distance] * moved * allowed[:, None]
    return result


def state_space(inputs, interval_widths, rates, b_mat, c_mat, environment_boundary_indices):
    total_rows, head_count, head_dim = inputs.shape
    blocks = environment_boundary_indices.shape[0]
    span = total_rows // blocks
    state_dim = b_mat.shape[1]
    x_blocks = inputs.reshape(blocks, span, head_count, head_dim)
    dt_blocks = interval_widths.reshape(blocks, span, head_count).transpose(0, 2, 1)
    b_blocks = b_mat.reshape(blocks, span, state_dim)
    c_blocks = c_mat.reshape(blocks, span, state_dim)
    running = jnp.cumsum(dt_blocks * rates[None, :, None], axis=2)
    lower = jnp.arange(span)[:, None] >= jnp.arange(span)[None, :]
    spread = running[:, :, :, None] - running[:, :, None, :]
    fading = jnp.exp(jnp.where(lower, spread, -1e30))
    scores = jnp.einsum("cln,csn->cls", c_blocks, b_blocks, precision=highest)
    mixing = scores[:, None] * fading * dt_blocks[:, :, None, :]
    outputs = jnp.einsum("chls,cshp->clhp", mixing, x_blocks, precision=highest)
    closing = jnp.exp(running[:, :, -1:] - running) * dt_blocks
    weighted = x_blocks * closing.transpose(0, 2, 1)[..., None]
    block_states = jnp.einsum("clhp,cln->chpn", weighted, b_blocks, precision=highest)
    carried = jnp.exp(running[:, :, -1])
    resets = 1.0 - environment_boundary_indices.astype(jnp.float32)

    def advance(state, packed):
        keep_rate, fresh, reset_one = packed
        entering = state * reset_one
        return (keep_rate[:, None, None] * entering + fresh, entering)

    final_state, entering = lax.scan(
        advance,
        jnp.zeros((head_count, head_dim, state_dim), jnp.float32),
        (carried, block_states, resets),
    )
    reading = jnp.einsum("cln,chpn->clhp", c_blocks, entering, precision=highest)
    outputs = outputs + jnp.exp(running).transpose(0, 2, 1)[..., None] * reading
    return outputs.reshape(total_rows, head_count, head_dim)


def leading_state_matrices(
    mapped_state_matrices,
    kernel_coefficients_statewise,
    environment_beginning,
    inside_segment,
    embedding_validity_mask,
):
    return (
        jax.nn.silu(
            leftward_convolution_kernel(
                mapped_state_matrices,
                kernel_coefficients_statewise,
                environment_beginning,
                inside_segment,
            )
        )
        * embedding_validity_mask[:, None]
    )


def state_space_layer(
    mapped_input_vector,
    mapped_multiplier,
    mapped_interval_width,
    current_input_state_matrices,
    kernel_coefficients_inputwise,
    interval_offset_vector,
    forgetting_exponent_coefficients,
    direct_coupling_factors,
    environment_boundary_indices,
    environment_beginning,
    inside_segment,
    embedding_validity_mask,
):
    total_rows = mapped_input_vector.shape[0]
    current_input_vector = (
        jax.nn.silu(
            leftward_convolution_kernel(
                mapped_input_vector,
                kernel_coefficients_inputwise,
                environment_beginning,
                inside_segment,
            )
        )
        * embedding_validity_mask[:, None]
    )
    interval_widths = (
        jax.nn.softplus(mapped_interval_width + interval_offset_vector)
        * embedding_validity_mask[:, None]
    )
    rates = -jnp.exp(forgetting_exponent_coefficients)
    state_dim = current_input_state_matrices.shape[1] // 2
    x_heads = current_input_vector.reshape(total_rows, -1, HD)
    scanned = state_space(
        x_heads,
        interval_widths,
        rates,
        current_input_state_matrices[:, :state_dim],
        current_input_state_matrices[:, state_dim:],
        environment_boundary_indices,
    )
    scanned = scanned + direct_coupling_factors[None, :, None] * x_heads
    return scanned.reshape(total_rows, -1) * jax.nn.silu(mapped_multiplier)


def matmul(left, right):
    return jnp.dot(left, right, preferred_element_type=jnp.float32)


def contract_rows(left, right):
    return lax.dot_general(
        left, right, (((0,), (0,)), ((), ())), preferred_element_type=jnp.float32
    )


def contract_cols(left, right):
    return lax.dot_general(
        left, right, (((1,), (1,)), ((), ())), preferred_element_type=jnp.float32
    )


def body(
    tokens,
    cotangent,
    scan_block_starts,
    scan_block_fill,
    norm_gain,
    w_x,
    w_z,
    w_dt,
    w_bc,
    conv_x,
    conv_bc,
    dt_bias,
    a_log,
    skip,
    gate_gain,
    w_out,
):
    heads_n = lax.axis_size("heads")
    head_index = lax.axis_index("heads")
    whole = lax.all_gather(tokens, "heads", axis=1, tiled=True)
    carried_hidden_vector = whole.astype(jnp.float32)
    width = carried_hidden_vector.shape[1]
    inverse = lax.rsqrt(
        jnp.mean(carried_hidden_vector * carried_hidden_vector, axis=-1, keepdims=True) + eps_norm
    )
    normed = (carried_hidden_vector * inverse * norm_gain).astype(jnp.bfloat16)
    rows_x, rows_z, rows_dt, rows_bc, rows_out = (
        lax.all_gather(w_x, "dp", axis=0, tiled=True),
        lax.all_gather(w_z, "dp", axis=0, tiled=True),
        lax.all_gather(w_dt, "dp", axis=0, tiled=True),
        lax.all_gather(w_bc, "dp", axis=0, tiled=True),
        lax.all_gather(w_out, "dp", axis=0, tiled=True),
    )
    mapped_input_vector = matmul(normed, rows_x)
    mapped_multiplier = matmul(normed, rows_z)
    mapped_interval_width = matmul(normed, rows_dt)
    mapped_state_matrices = matmul(normed, rows_bc)
    environment_beginning, inside_segment, embedding_validity_mask = embedding_index_arrays(
        scan_block_starts, scan_block_fill, carried_hidden_vector.shape[0]
    )

    def front_piece(incoming_embeddings, kernel_coefficients):
        return leading_state_matrices(
            incoming_embeddings,
            kernel_coefficients,
            environment_beginning,
            inside_segment,
            embedding_validity_mask,
        )

    current_input_state_matrices, front_pull = jax.vjp(front_piece, mapped_state_matrices, conv_bc)

    def mixer_piece(
        source_x,
        source_z,
        source_dt,
        active_bc,
        kernel_coefficients_inputwise,
        interval_offset_vector,
        forgetting_exponent_coefficients,
        direct_coupling_factors,
    ):
        return state_space_layer(
            source_x,
            source_z,
            source_dt,
            active_bc,
            kernel_coefficients_inputwise,
            interval_offset_vector,
            forgetting_exponent_coefficients,
            direct_coupling_factors,
            scan_block_starts,
            environment_beginning,
            inside_segment,
            embedding_validity_mask,
        )

    multiplied_result_vector, mixer_pull = jax.vjp(
        mixer_piece,
        mapped_input_vector,
        mapped_multiplier,
        mapped_interval_width,
        current_input_state_matrices,
        conv_x,
        dt_bias,
        a_log,
        skip,
    )
    inner_total = multiplied_result_vector.shape[1] * heads_n
    squares = lax.psum(
        jnp.sum(multiplied_result_vector * multiplied_result_vector, axis=-1), "heads"
    )
    gate_inverse = lax.rsqrt(squares / inner_total + eps_norm)[:, None]
    gated_normed = (multiplied_result_vector * gate_inverse * gate_gain).astype(jnp.bfloat16)
    partial_out = contract_cols(gated_normed, rows_out)
    out_share = lax.psum_scatter(partial_out, "heads", scatter_dimension=1, tiled=True)
    block_out = (tokens.astype(jnp.float32) + out_share).astype(jnp.bfloat16)
    grad_full = lax.all_gather(cotangent, "heads", axis=1, tiled=True)
    rows_x, rows_z, rows_dt, rows_bc, rows_out = (
        lax.all_gather(w_x, "dp", axis=0, tiled=True),
        lax.all_gather(w_z, "dp", axis=0, tiled=True),
        lax.all_gather(w_dt, "dp", axis=0, tiled=True),
        lax.all_gather(w_bc, "dp", axis=0, tiled=True),
        lax.all_gather(w_out, "dp", axis=0, tiled=True),
    )
    grad_gated_normed = matmul(grad_full, rows_out)
    grad_w_out = contract_rows(grad_full, gated_normed)
    grad_gate_gain = jnp.sum(grad_gated_normed * multiplied_result_vector * gate_inverse, axis=0)
    scaled_grad = grad_gated_normed * gate_gain
    gate_dots = lax.psum(jnp.sum(scaled_grad * multiplied_result_vector, axis=-1), "heads")
    grad_gated = (
        gate_inverse * scaled_grad
        - multiplied_result_vector * gate_inverse**3 * (gate_dots / inner_total)[:, None]
    )
    grad_px, grad_pz, grad_pdt, grad_bc_part, grad_conv_x, grad_dt_bias, grad_a_log, grad_skip = (
        mixer_pull(grad_gated)
    )
    grad_bc_active = lax.psum(grad_bc_part, "heads")
    grad_pbc, grad_conv_bc = front_pull(grad_bc_active)
    low_px = grad_px.astype(jnp.bfloat16)
    low_pz = grad_pz.astype(jnp.bfloat16)
    low_pdt = grad_pdt.astype(jnp.bfloat16)
    low_pbc = grad_pbc.astype(jnp.bfloat16)
    grad_w_x = contract_rows(normed, low_px)
    grad_w_z = contract_rows(normed, low_pz)
    grad_w_dt = contract_rows(normed, low_pdt)
    grad_w_bc = contract_rows(normed, low_pbc)
    partial_in = (
        contract_cols(low_px, rows_x)
        + contract_cols(low_pz, rows_z)
        + contract_cols(low_pdt, rows_dt)
    )
    in_share = lax.psum_scatter(partial_in, "heads", scatter_dimension=1, tiled=True)
    columns = width // heads_n
    own_bc = lax.dynamic_slice_in_dim(rows_bc, head_index * columns, columns, 0)
    grad_normed = in_share + contract_cols(low_pbc, own_bc)
    own_residual = lax.dynamic_slice_in_dim(carried_hidden_vector, head_index * columns, columns, 1)
    own_gain = lax.dynamic_slice_in_dim(norm_gain, head_index * columns, columns, 0)
    gain_part = jnp.sum(grad_normed * own_residual * inverse, axis=0)
    norm_dots = lax.psum(jnp.sum(grad_normed * own_gain * own_residual, axis=-1), "heads")
    grad_tokens = (
        cotangent.astype(jnp.float32)
        + inverse * own_gain * grad_normed
        - own_residual * inverse**3 * (norm_dots / width)[:, None]
    )
    grad_w_x, grad_w_z, grad_w_dt, grad_w_bc, grad_w_out = (
        lax.psum_scatter(grad_w_x, "dp", scatter_dimension=0, tiled=True),
        lax.psum_scatter(grad_w_z, "dp", scatter_dimension=0, tiled=True),
        lax.psum_scatter(grad_w_dt, "dp", scatter_dimension=0, tiled=True),
        lax.psum_scatter(grad_w_bc, "dp", scatter_dimension=0, tiled=True),
        lax.psum_scatter(grad_w_out, "dp", scatter_dimension=0, tiled=True),
    )
    (
        grad_conv_x,
        grad_conv_bc,
        grad_dt_bias,
        grad_a_log,
        grad_skip,
        grad_gate_gain,
        grad_norm_gain,
    ) = lax.psum(
        (grad_conv_x, grad_conv_bc, grad_dt_bias, grad_a_log, grad_skip, grad_gate_gain, gain_part),
        "dp",
    )
    return (
        block_out,
        grad_tokens,
        grad_norm_gain,
        grad_w_x,
        grad_w_z,
        grad_w_dt,
        grad_w_bc,
        grad_conv_x,
        grad_conv_bc,
        grad_dt_bias,
        grad_a_log,
        grad_skip,
        grad_gate_gain,
        grad_w_out,
    )


def solution(mesh):
    placed = (
        P("dp", "heads"),
        P("dp", "heads"),
        P("dp"),
        P("dp"),
        P(),
        P("dp", "heads"),
        P("dp", "heads"),
        P("dp", "heads"),
        P("dp", None),
        P(None, "heads"),
        P(),
        P("heads"),
        P("heads"),
        P("heads"),
        P("heads"),
        P("dp", "heads"),
    )
    return jax.shard_map(
        body,
        mesh=mesh,
        in_specs=placed,
        out_specs=(
            P("dp", "heads"),
            P("dp", "heads"),
            P("heads"),
            P("dp", "heads"),
            P("dp", "heads"),
            P("dp", "heads"),
            P("dp", None),
            P(None, "heads"),
            P(),
            P("heads"),
            P("heads"),
            P("heads"),
            P("heads"),
            P("dp", "heads"),
        ),
        check_vma=False,
    )
```

profile of v0, /device:TPU:0, one launch (start us, length us, event | category | flops | bytes accessed | tf_op | source)
XLA Modules:
  0.0 999.0 jit_solution(2365328440459106176)
XLA Ops:
  16.5 27.9 %all_gather.29 = bf16[1024,8]{0,1:T(8,128)(2,1)S(1)} all-gather(bf16[128,8]{0,1:T(8,128)(2,1)} %param.27), channel_id=1, replica_groups=mesh['dp'=8,'heads'=4] {'dp'}, dimensions={0}, use_global_device_ids=true | all-gather | bytes 18432 | tf_op jit(solution)/shard_map/all_gather | solution.py:185
  44.5 31.5 %all_gather.28 = bf16[1024,256]{1,0:T(8,128)(2,1)S(1)} all-gather(bf16[128,256]{1,0:T(8,128)(2,1)} %param.28), channel_id=1, replica_groups=mesh['dp'=8,'heads'=4] {'dp'}, dimensions={0}, use_global_device_ids=true | all-gather | bytes 589824 | tf_op jit(solution)/shard_map/all_gather | solution.py:186
  76.0 3.3 multiply_reduce_fusion.2
  84.4 4.5 reduce_window_sum.22
  89.5 3.5 fusion.95
  93.1 3.5 multiply_multiply_fusion.1
  96.8 4.9 fusion.94
  101.7 6.2 multiply_multiply_fusion
  107.9 7.1 reshape.253
  115.0 6.9 copy.93
  121.9 6.9 fusion.35
  128.8 2.6 broadcast.229.clone
  131.4 77.5 %while.34 = (s32[]{:T(128)}, f32[8,64,128]{2,1,0:T(8,128)S(1)}, f32[16,8,64,128]{3,2,1,0:T(8,128)}, f32[16,8,1,1]{1,3,2,0:T(1,128)}, f32[16,8]{1,0:T(8,128)S(1)}...) while((s32[]{:T(128)}, f32[8,64,128]{2,1,0:T(8,128)S(1)}, ...), condition=%wide.region_3.4_spmd.clone, body=%wide.region_2.3_spmd.clone.sunk | while | flops 393219 | bytes 1312016 | solution.py:64
  209.0 2.3 fusion.96
  211.3 6.0 fusion.97
  219.4 17.9 %bitcast_add_fusion.3 = f32[16,128,8,64]{1,3,2,0:T(8,128)} fusion(f32[16,128,8,64]{1,3,2,0:T(8,128)S(1)} %fusion.97, f32[16,128,8]{1,2,0:T(8,128)S(1)} %exponential_bitcast_fusion, f32[16,128,8,64]{1,3,2,0:T(8,128)S(1)} %copy-done.7, f32[16,8,128]{2,1,0:T(8,128)S(1)} %get-tuple-element.420, f32[16,8,128]{2,1,0:T(8,128)S(1)} %reduce_window_sum.22, ...), kind=kOutput, calls=%fused_computation.37 | convolution fusion | flops 1621098496 | bytes 13844480 | tf_op jit(solution)/shard_map/jvp(chls,cshp->clhp)/dot_general | solution.py:52
  237.3 6.9 copy.121
  244.2 7.5 reshape.251
  251.7 11.5 %multiply_reduce_fusion.12 = (f32[2048]{0:T(1024)S(1)}, f32[2048,512]{1,0:T(8,128)}, f32[2048,512]{1,0:T(8,128)}) fusion(f32[2048,512]{1,0:T(8,128)} %reshape.251, f32[2048,512]{1,0:T(8,128)} %get-tuple-element.417, f32[512]{0:T(512)S(1)} %mul.750, bf16[2048,1024]{1,0:T(8,128)(2,1)} %copy-done.5, bf16[1024,512]{1,0:T(8,128)(2,1)} %all-gather.10.cloned.1.call-done), kind=kOutput, calls=%fused_computation.50 | convolution fusion | flops 2156918784 | bytes 22030336 | tf_op jit(solution)/shard_map/dot_general | solution.py:140
  263.2 5.7 psum.77
  269.0 9.2 multiply_reduce_fusion.3
  278.2 6.5 psum.78
  284.8 12.3 %multiply_reduce_fusion.4 = (f32[512]{0:T(512)}, f32[2048,512]{1,0:T(8,128)}, bf16[2048,512]{1,0:T(8,128)(2,1)}) fusion(f32[2048,512]{1,0:T(8,128)} %get-tuple-element.417, f32[2048,512]{1,0:T(8,128)} %get-tuple-element.451, f32[2048]{0:T(1024)S(1)} %broadcast_multiply_fusion.7, f32[2048,512]{1,0:T(8,128)} %get-tuple-element.416, ...), kind=kLoop, calls=%fused_computation.39 | loop fusion | flops 23068160 | bytes 27293696 | tf_op jit(solution)/shard_map/transpose(jvp())/reduce_sum | solution.py:135
  297.1 5.5 copy.100
  302.6 3.3 copy.129
  306.0 9.1 fusion.53
  315.1 6.8 fusion.38
  321.9 2.5 broadcast.229
  324.4 72.2 %while.35 = (s32[]{:T(128)}, f32[8,64,128]{2,1,0:T(8,128)S(1)}, f32[16,8]{1,0:T(8,128)S(1)}, f32[16,8,64,128]{3,2,1,0:T(8,128)}, f32[16,8,64,128]{3,2,1,0:T(8,12...) while((s32[]{:T(128)}, f32[8,64,128]{2,1,0:T(8,128)S(1)}, ...), condition=%wide.region_11.12_spmd.clone, body=%wide.region_9.11_spmd.clone.sunk | while | flops 458748 | bytes 1573228 | solution.py:64
  396.6 11.4 %fusion.54 = f32[16,128,128]{2,1,0:T(8,128)} fusion(f32[16,8,64,128]{3,2,1,0:T(8,128)} %get-tuple-element.215, f32[16,128,8,64]{1,3,2,0:T(8,128)} %copy.93, f32[16,128,8]{1,2,0:T(8,128)S(1)} %bitcast_multiply_fusion.5), kind=kOutput, calls=%fused_computation.111 | convolution fusion | flops 1611661312 | bytes 9502720 | tf_op jit(solution)/shard_map/transpose(jvp(clhp,cln->chpn))/dot_general | solution.py:55
  408.1 5.5 multiply_reduce_fusion.10
  413.7 20.5 %fusion.11 = (f32[16,8,128]{2,1,0:T(8,128)}, f32[16,8,128]{2,1,0:T(8,128)}, f32[16,8,128]{2,1,0:T(8,128)}, f32[16,128,128]{2,1,0:T(8,128)}) fusion(f32[16,8,128]{2,1,0:T(8,128)S(1)} %copy-done.35, f32[16,8,128]{2,1,0:T(8,128)S(1)} %reduce_window_sum.22, f32[16,128,128]{2,1,0:T(8,128)S(1)} %copy-done.33, pred[128,128]{1,0:T(8,128)(4,1)S(1)} %copy-done.73, ...), kind=kOutput, calls=%fused_computation.27 | convolution fusion | flops 1637564416 | bytes 10829824 | tf_op jit(solution)/shard_map/transpose(jvp(chls,cshp->clhp))/dot_general | solution.py:52
  435.0 2.5 convolution_add_fusion.3
  437.5 3.6 convolution_add_fusion.2
  441.2 12.5 %bitcast_add_fusion.2 = f32[16,128,8,64]{1,3,2,0:T(8,128)} fusion(f32[16,128,8,64]{1,3,2,0:T(8,128)S(1)} %copy-done.27, f32[16,128,8]{1,2,0:T(8,128)S(1)} %copy-done.40, f32[16,8,128]{2,1,0:T(8,128)S(1)} %copy-done.35, f32[16,8,128]{2,1,0:T(8,128)S(1)} %reduce_window_sum.22, f32[16,128,128]{2,1,0:T(8,128)} %copy-done.32, ...), kind=kOutput, calls=%fused_computation.36 | convolution fusion | flops 1621098496 | bytes 13844480 | tf_op jit(solution)/shard_map/transpose(jvp(chls,cshp->clhp))/dot_general | solution.py:52
  455.6 7.4 copy.122
  463.1 7.5 reshape.252
  470.6 9.1 multiply_reduce_fusion.8
  479.7 4.9 multiply_reduce_fusion.7
  491.2 3.9 convolution_bitcast_fusion
  495.3 7.1 fusion.99
  502.6 20.0 %reduce_window_sum.23 = f32[16,8,128]{2,1,0:T(8,128)S(1)} reduce-window(f32[16,8,128]{2,1,0:T(8,128)S(1)} %fusion.66, f32[]{:T(128)} %constant.123.clone.1), window={size=1x1x128 pad=0_0x0_0x0_127}, to_apply=%region_18.19 | reduce-window | flops 2080768 | bytes 131076 | tf_op jit(solution)/shard_map/transpose(jvp(jit(cumsum)))/reduce_window_sum | solution.py:46
  522.8 2.9 slice_multiply_fusion.2
  532.2 2.9 multiply_reduce_fusion.5
  535.1 4.4 fusion.98
  539.5 4.7 add_add_fusion
  545.4 7.9 fusion.83
  553.4 3.6 fusion.69
  557.2 3.1 multiply_reduce_fusion.16
  565.3 2.3 fusion.102
  567.7 5.9 fusion.101
  573.7 6.6 fusion.100
  581.3 7.6 convert_element_type.65
  590.9 60.9 %reduce-scatter.10.cloned.1.call-done = f32[2048,256]{1,0:T(8,128)} async-done(((f32[2048,1024]{1,0:T(8,128)}), f32[2048,256]{1,0:T(8,128)}) %reduce-scatter.10.cloned.1.call-update) | async-done | bytes 2097168 | tf_op jit(solution)/shard_map/reduce_scatter | solution.py:288
  651.8 3.5 multiply_reduce_fusion.17
  655.3 37.6 %all-reduce.24 = (f32[256]{0:T(256)}, f32[4,512]{1,0:T(4,128)}, f32[4,256]{1,0:T(4,128)}, f32[8]{0:T(128)}, f32[8]{0:T(128)}, /*index=5*/f32[8]{0:T(128)}, f32[512]{0:T(512)}) all-reduce(f32[256]{0:T(256)S(1)} %get-tuple-element.352, f32[4,512]{1,0:T(4,128)S(1)} %pad_add_fusion.1, ...), channel_id=1, replica_groups=mesh['dp'=8,'heads'=4] {'dp'}, use_global_device_ids=true, to_apply=%region_25.26 | all-reduce | flops 3864 | bytes 30912 | tf_op jit(solution)/shard_map/psum | solution.py:316
  693.0 6.5 psum.80
  699.5 26.9 %reduce-scatter.8.cloned.1.call-done = f32[2048,256]{1,0:T(8,128)} async-done(((f32[2048,1024]{1,0:T(8,128)}), f32[2048,256]{1,0:T(8,128)}) %reduce-scatter.8.cloned.1.call-update) | async-done | bytes 2097168 | tf_op jit(solution)/shard_map/reduce_scatter | solution.py:251
  726.4 3.1 add_convert_fusion.2
  729.4 3.2 multiply_subtract_fusion.1
  732.6 51.2 %reduce-scatter.16.cloned.1.call-done = f32[128,8]{0,1:T(8,128)} async-done(((f32[1024,8]{0,1:T(8,128)}), f32[128,8]{0,1:T(8,128)}) %reduce-scatter.16.cloned.1.call-update) | async-done | bytes 4112 | tf_op jit(solution)/shard_map/reduce_scatter | solution.py:304
  783.8 66.8 %reduce-scatter.18.cloned.1.call-done = f32[128,256]{1,0:T(8,128)} async-done(((f32[1024,256]{1,0:T(8,128)}), f32[128,256]{1,0:T(8,128)}) %reduce-scatter.18.cloned.1.call-update) | async-done | bytes 131088 | tf_op jit(solution)/shard_map/reduce_scatter | solution.py:305
  850.6 70.7 %reduce-scatter.14.cloned.1.call-done = f32[128,512]{1,0:T(8,128)} async-done(((f32[1024,512]{1,0:T(8,128)}), f32[128,512]{1,0:T(8,128)}) %reduce-scatter.14.cloned.1.call-update) | async-done | bytes 262160 | tf_op jit(solution)/shard_map/reduce_scatter | solution.py:303
  921.3 70.9 %reduce-scatter.12.cloned.1.call-done = f32[128,512]{1,0:T(8,128)} async-done(((f32[1024,512]{1,0:T(8,128)}), f32[128,512]{1,0:T(8,128)}) %reduce-scatter.12.cloned.1.call-update) | async-done | bytes 262160 | tf_op jit(solution)/shard_map/reduce_scatter | solution.py:302
  (431 shorter events, 191.9 us)
Async XLA Ops:
  7.2 72.8 %copy-start.83 = (f32[1024]{0:T(1024)S(1)}, f32[1024]{0:T(1024)}, u32[]{:S(2)}) copy-start(f32[1024]{0:T(1024)} %param.24) | copy-start | bytes 12292
  7.2 68.8 %all-gather.6.cloned.1.call-start = ((), (), s32[]{:S(2)}) async-start(), calls=%async_computation.7 | async-start | bytes 5242880 | tf_op jit(solution)/shard_map/all_gather | solution.py:175
  7.9 88.8 %all-gather.8.cloned.1.call-start = ((), (), s32[]{:S(2)}) async-start(), calls=%async_computation.8 | async-start | bytes 1179648 | tf_op jit(solution)/shard_map/all_gather | solution.py:183
  8.7 243.0 %all-gather.10.cloned.1.call-start = ((), (), s32[]{:S(2)}) async-start(), calls=%async_computation.9 | async-start | bytes 1179648 | tf_op jit(solution)/shard_map/all_gather | solution.py:184
  9.4 259.6 %all-gather.12.cloned.1.call-start = ((), (), s32[]{:S(2)}) async-start(), calls=%async_computation.10 | async-start | bytes 1179648 | tf_op jit(solution)/shard_map/all_gather | solution.py:187
  10.0 259.0 %all-gather.14.cloned.1.call-start = ((), (), s32[]{:S(2)}) async-start(), calls=%async_computation.12 | async-start | bytes 5242880 | tf_op jit(solution)/shard_map/all_gather | solution.py:253
  10.6 546.6 %all-reduce.27.cloned.1.call-start = ((), (), s32[]{:S(2)}) async-start(), calls=%async_computation.14 | async-start | bytes 4194304 | tf_op jit(solution)/shard_map/psum | solution.py:273
  12.5 204.8 %copy-start.72 = (pred[128,128]{1,0:T(8,128)(4,1)}, pred[128,128]{1,0:T(8,128)(4,1)S(1)}, u32[]{:S(2)}) copy-start(pred[128,128]{1,0:T(8,128)(4,1)S(1)} %iota_compare_fusion) | copy-start | bytes 49156
  13.2 71.2 %copy-start.85 = (f32[8]{0:T(128)}, f32[8]{0:T(128)S(1)}, u32[]{:S(2)}) copy-start(f32[8]{0:T(128)S(1)} %exponential_negate_fusion) | copy-start | bytes 100
  14.0 270.8 %copy-start.60 = (f32[512]{0:T(512)}, f32[512]{0:T(512)S(1)}, u32[]{:S(2)}) copy-start(f32[512]{0:T(512)S(1)} %mul.750) | copy-start | bytes 6148
  14.8 78.3 %copy-start.74 = (f32[1,256]{1,0:T(1,128)}, f32[1,256]{1,0:T(1,128)S(1)}, u32[]{:S(2)}) copy-start(f32[1,256]{1,0:T(1,128)S(1)} %get-tuple-element.444) | copy-start | bytes 3076
  14.8 78.3 %copy-start.76 = (f32[1,256]{1,0:T(1,128)}, f32[1,256]{1,0:T(1,128)S(1)}, u32[]{:S(2)}) copy-start(f32[1,256]{1,0:T(1,128)S(1)} %get-tuple-element.445) | copy-start | bytes 3076
  14.8 78.3 %copy-start.78 = (f32[1,256]{1,0:T(1,128)}, f32[1,256]{1,0:T(1,128)S(1)}, u32[]{:S(2)}) copy-start(f32[1,256]{1,0:T(1,128)S(1)} %get-tuple-element.447) | copy-start | bytes 3076
  14.8 78.3 %copy-start.80 = (f32[1,256]{1,0:T(1,128)}, f32[1,256]{1,0:T(1,128)S(1)}, u32[]{:S(2)}) copy-start(f32[1,256]{1,0:T(1,128)S(1)} %get-tuple-element.446) | copy-start | bytes 3076
  16.4 85.3 %copy-start.62 = (f32[1,512]{1,0:T(1,128)}, f32[1,512]{1,0:T(1,128)S(1)}, u32[]{:S(2)}) copy-start(f32[1,512]{1,0:T(1,128)S(1)} %get-tuple-element.440) | copy-start | bytes 6148
  16.4 85.3 %copy-start.64 = (f32[1,512]{1,0:T(1,128)}, f32[1,512]{1,0:T(1,128)S(1)}, u32[]{:S(2)}) copy-start(f32[1,512]{1,0:T(1,128)S(1)} %get-tuple-element.441) | copy-start | bytes 6148
  16.4 85.3 %copy-start.66 = (f32[1,512]{1,0:T(1,128)}, f32[1,512]{1,0:T(1,128)S(1)}, u32[]{:S(2)}) copy-start(f32[1,512]{1,0:T(1,128)S(1)} %get-tuple-element.443) | copy-start | bytes 6148
  16.5 85.3 %copy-start.68 = (f32[1,512]{1,0:T(1,128)}, f32[1,512]{1,0:T(1,128)S(1)}, u32[]{:S(2)}) copy-start(f32[1,512]{1,0:T(1,128)S(1)} %get-tuple-element.442) | copy-start | bytes 6148
  44.4 36.7 %copy-start.50 = (bf16[1024,8]{0,1:T(8,128)(2,1)}, bf16[1024,8]{0,1:T(8,128)(2,1)S(1)}, u32[]{:S(2)}) copy-start(bf16[1024,8]{0,1:T(8,128)(2,1)S(1)} %all_gather.29) | copy-start | bytes 49156
  44.5 57.3 %copy-start.42 = (f32[2048]{0:T(1024)}, f32[2048]{0:T(1024)S(1)}, u32[]{:S(2)}) copy-start(f32[2048]{0:T(1024)S(1)} %get-tuple-element.450) | copy-start | bytes 24580
  44.5 57.3 %copy-start.48 = (f32[2048]{0:T(1024)}, f32[2048]{0:T(1024)S(1)}, u32[]{:S(2)}) copy-start(f32[2048]{0:T(1024)S(1)} %get-tuple-element.449) | copy-start | bytes 24580
  76.0 13.5 %copy-start.38 = (bf16[1024,256]{1,0:T(8,128)(2,1)}, bf16[1024,256]{1,0:T(8,128)(2,1)S(1)}, u32[]{:S(2)}) copy-start(bf16[1024,256]{1,0:T(8,128)(2,1)S(1)} %all_gather.28) | copy-start | bytes 1572868
  84.4 132.9 %copy-start.34 = (f32[16,8,128]{2,1,0:T(8,128)}, f32[16,8,128]{2,1,0:T(8,128)S(1)}, u32[]{:S(2)}) copy-start(f32[16,8,128]{2,1,0:T(8,128)S(1)} %get-tuple-element.420) | copy-start | bytes 196612
  89.2 7.4 copy-start.57
  89.3 7.3 copy-start.46
  89.5 307.1 %copy-start.39 = (f32[16,128,8]{1,2,0:T(8,128)}, f32[16,128,8]{1,2,0:T(8,128)S(1)}, u32[]{:S(2)}) copy-start(f32[16,128,8]{1,2,0:T(8,128)S(1)} %bitcast_multiply_fusion.5) | copy-start | bytes 196612
  211.3 8.1 copy-start.7
  251.7 17.4 %copy-start.70 = (f32[512]{0:T(512)S(1)}, f32[512]{0:T(512)}, u32[]{:S(2)}) copy-start(f32[512]{0:T(512)} %param.34) | copy-start | bytes 6148
  269.0 15.8 %copy-start.44 = (f32[2048]{0:T(1024)}, f32[2048]{0:T(1024)S(1)}, u32[]{:S(2)}) copy-start(f32[2048]{0:T(1024)S(1)} %get-tuple-element.439) | copy-start | bytes 24580
  305.9 9.3 copy-start.9
  396.6 11.5 %copy-start.8 = (f32[16,128,8,64]{1,3,2,0:T(8,128)S(1)}, f32[16,128,8,64]{1,3,2,0:T(8,128)}, u32[]{:S(2)}) copy-start(f32[16,128,8,64]{1,3,2,0:T(8,128)} %copy.93) | copy-start | bytes 12582916
  396.6 11.4 %copy-start.15 = (f32[16,8,64,128]{3,2,1,0:T(8,128)S(1)}, f32[16,8,64,128]{3,2,1,0:T(8,128)}, u32[]{:S(2)}) copy-start(f32[16,8,64,128]{3,2,1,0:T(8,128)} %get-tuple-element.215) | copy-start | bytes 12582916
  413.6 41.6 %copy-start.30 = (f32[16,128,8]{1,2,0:T(8,128)}, f32[16,128,8]{1,2,0:T(8,128)S(1)}, u32[]{:S(2)}) copy-start(f32[16,128,8]{1,2,0:T(8,128)S(1)} %get-tuple-element.453) | copy-start | bytes 196612
  413.7 20.6 %copy-start.58 = (f32[16,8,1]{0,1,2:T(8,128)S(1)}, f32[16,8,1]{0,1,2:T(8,128)}, u32[]{:S(2)}) copy-start(f32[16,8,1]{0,1,2:T(8,128)} %copy-done.57) | copy-start | bytes 1540
  413.7 21.3 %copy-start.29 = (f32[16,128,128]{2,1,0:T(8,128)S(1)}, f32[16,128,128]{2,1,0:T(8,128)}, u32[]{:S(2)}) copy-start(f32[16,128,128]{2,1,0:T(8,128)} %fusion.53) | copy-start | bytes 3145732
  413.7 27.5 %copy-start.40 = (f32[16,128,8]{1,2,0:T(8,128)S(1)}, f32[16,128,8]{1,2,0:T(8,128)}, u32[]{:S(2)}) copy-start(f32[16,128,8]{1,2,0:T(8,128)} %copy-done.39) | copy-start | bytes 196612
  455.2 133.9 %reduce-scatter.20.cloned.1.call-start = ((), (), s32[]{:S(2)}) async-start(), calls=%async_computation.19 | async-start | bytes 2359296 | tf_op jit(solution)/shard_map/reduce_scatter | solution.py:306
  463.0 7.6 copy-start.49
  463.0 7.6 copy-start.61
  470.6 9.1 copy-start.1
  470.6 9.1 copy-start.43
  479.7 7.9 copy-start.22
  495.2 156.6 %reduce-scatter.10.cloned.1.call-start = ((), (), s32[]{:S(2)}) async-start(), calls=%async_computation.13 | async-start | bytes 10485760 | tf_op jit(solution)/shard_map/reduce_scatter | solution.py:288
  495.2 7.2 copy-start.31
  495.2 7.2 copy-start.36
  495.3 7.1 copy-start.41
  495.3 7.1 copy-start.54
  495.3 7.1 copy-start.55
  495.3 27.3 %copy-start.56 = (f32[16,8,128]{2,1,0:T(8,128)S(1)}, f32[16,8,128]{2,1,0:T(8,128)}, u32[]{:S(2)}) copy-start(f32[16,8,128]{2,1,0:T(8,128)} %get-tuple-element.356) | copy-start | bytes 196612
  495.3 27.3 %copy-start.86 = (f32[8]{0:T(128)S(1)}, f32[8]{0:T(128)}, u32[]{:S(2)}) copy-start(f32[8]{0:T(128)} %copy-done.85) | copy-start | bytes 100
  495.3 27.5 %copy-start.69 = (f32[1,512]{1,0:T(1,128)S(1)}, f32[1,512]{1,0:T(1,128)}, u32[]{:S(2)}) copy-start(f32[1,512]{1,0:T(1,128)} %copy-done.68) | copy-start | bytes 6148
  528.5 10.9 %slice-start = ((s8[8388608]{0:T(1024)(128)(4,1)}), s8[4194304]{0:T(1024)(128)(4,1)S(1)}, s32[]{:S(2)}) async-start(s8[8388608]{0:T(1024)(128)(4,1)} %bitcast.240), calls=%async_computation.20 | async-start | bytes 8388608
  532.2 7.3 slice-start.1
  544.2 182.2 %reduce-scatter.8.cloned.1.call-start = ((), (), s32[]{:S(2)}) async-start(), calls=%async_computation.11 | async-start | bytes 10485760 | tf_op jit(solution)/shard_map/reduce_scatter | solution.py:251
  553.4 230.4 %reduce-scatter.16.cloned.1.call-start = ((), (), s32[]{:S(2)}) async-start(), calls=%async_computation.17 | async-start | bytes 36864 | tf_op jit(solution)/shard_map/reduce_scatter | solution.py:304
  557.1 293.6 %reduce-scatter.18.cloned.1.call-start = ((), (), s32[]{:S(2)}) async-start(), calls=%async_computation.18 | async-start | bytes 1179648 | tf_op jit(solution)/shard_map/reduce_scatter | solution.py:305
  567.6 353.6 %reduce-scatter.14.cloned.1.call-start = ((), (), s32[]{:S(2)}) async-start(), calls=%async_computation.16 | async-start | bytes 2359296 | tf_op jit(solution)/shard_map/reduce_scatter | solution.py:303
  573.6 7.5 copy-start.82
  573.6 418.6 %reduce-scatter.12.cloned.1.call-start = ((), (), s32[]{:S(2)}) async-start(), calls=%async_computation.15 | async-start | bytes 2359296 | tf_op jit(solution)/shard_map/reduce_scatter | solution.py:302
  581.3 7.8 copy-start.89
  581.3 70.5 %copy-start.53 = (f32[2048]{0:T(1024)S(1)}, f32[2048]{0:T(1024)}, u32[]{:S(2)}) copy-start(f32[2048]{0:T(1024)} %copy-done.52) | copy-start | bytes 24580
  588.9 66.4 %copy-start.87 = (f32[512]{0:T(512)S(1)}, f32[512]{0:T(512)}, u32[]{:S(2)}) copy-start(f32[512]{0:T(512)} %get-tuple-element.358) | copy-start | bytes 6148
  590.9 138.5 %copy-start.26 = (bf16[2048,256]{1,0:T(8,128)(2,1)S(1)}, bf16[2048,256]{1,0:T(8,128)(2,1)}, u32[]{:S(2)}) copy-start(bf16[2048,256]{1,0:T(8,128)(2,1)} %param.21) | copy-start | bytes 3145732
  590.9 138.5 %copy-start.59 = (f32[2048]{0:T(1024)S(1)}, f32[2048]{0:T(1024)}, u32[]{:S(2)}) copy-start(f32[2048]{0:T(1024)} %get-tuple-element.436) | copy-start | bytes 24580
  (41 other events, 140.7 us)
Sparse Core Ops, SparseCore 0:
  9.6 37.7 all-gather.5
  49.5 41.0 all-gather.7
  92.6 38.9 all-gather.9
  133.6 38.9 all-gather.11
  174.0 33.7 all-gather.13
  455.3 50.4 all-reduce.26
  509.7 68.4 reduce-scatter.19
  581.0 70.7 reduce-scatter.9
  654.4 71.9 reduce-scatter.7
  730.2 53.4 reduce-scatter.15
  788.2 62.4 reduce-scatter.17
  854.6 66.6 reduce-scatter.13
  925.4 66.7 reduce-scatter.11
where the time goes:
time: 1020 us; the launch traced here: 999 us
  waiting for transfers between devices  351 us (34%)
  other arithmetic  190 us (19%)
  matrix products  185 us (18%)
  local copies, waits for them, and re-layouts  141 us (14%)
  blocking collectives  116 us (11%)
  between operations  15.3 us (2%)
    reduce_scatter x1, waiting for transfers between devices, body(): lax.psum_scatter(grad_w_x, 'dp', scatter_dimension=0, tiled=True)  70.9 us
    reduce_scatter x1, waiting for transfers between devices, body(): lax.psum_scatter(grad_w_z, 'dp', scatter_dimension=0, tiled=True)  70.7 us
    reduce_scatter x1, waiting for transfers between devices, body(): lax.psum_scatter(grad_w_bc, 'dp', scatter_dimension=0, tiled=True)  66.8 us
    reduce_scatter x1, waiting for transfers between devices, body(): lax.psum_scatter(partial_in, 'heads', scatter_dimension=1, tiled=True)  60.9 us
    reduce_scatter x1, waiting for transfers between devices, body(): lax.psum_scatter(grad_w_dt, 'dp', scatter_dimension=0, tiled=True)  51.2 us
    dot_general x3, matrix products, state_space(): outputs = jnp.einsum('chls,cshp->clhp', mixing, x_blocks, precision=highest)  50.9 us
    dynamic_slice x32, local copies, waits for them, and re-layouts, state_space(): lax.scan(advance, jnp.zeros((head_count, head_dim, state_dim), jnp.float3...  39.8 us
    psum x1, blocking collectives, body(): lax.psum((grad_conv_x, grad_conv_bc, grad_dt_bias, grad_a_log, grad_skip,...  37.6 us
  transfers between devices with their start and end apart: 13, of which 6 were waited for; matrix products, arithmetic and copies ran while one was open for 32% of the time, Pallas kernels for 0%

commit v1 on v0

v1 whole, which is shorter than its diff:
```python
import functools
import jax
import jax.numpy as jnp
import numpy as np
from jax import lax
from jax.experimental import pallas as pl
from jax.experimental.pallas import tpu as pltpu
from jax.sharding import PartitionSpec as P

HD = 64
EPS = 1e-05
F32 = jnp.float32
BF = jnp.bfloat16
NEG = -1e30


def nn(a, b):
    return lax.dot_general(a, b, (((1,), (0,)), ((), ())), preferred_element_type=F32)


def nt(a, b):
    return lax.dot_general(a, b, (((1,), (1,)), ((), ())), preferred_element_type=F32)


def tn(a, b):
    return lax.dot_general(a, b, (((0,), (0,)), ((), ())), preferred_element_type=F32)


def split2(v):
    hi = v.astype(BF).astype(F32)
    return hi, v - hi


def split3(v):
    hi = v.astype(BF).astype(F32)
    rest = v - hi
    mid = rest.astype(BF).astype(F32)
    return hi, mid, rest - mid


def softplus(v):
    return jnp.maximum(v, 0.0) + jnp.log1p(jnp.exp(-jnp.abs(v)))


def sigmoid(v):
    return 1.0 / (1.0 + jnp.exp(-v))


def iota2(rows, cols, axis):
    return lax.broadcasted_iota(jnp.int32, (rows, cols), axis)


def scan_constants(chunk, heads):
    inner = heads * HD
    t = np.arange(chunk)
    upper = (t[:, None] <= t[None, :]).astype(np.float32)
    head_of = np.arange(inner) // HD
    spread = np.zeros((chunk, 3 * inner), np.float32)
    for q in range(3):
        for part in range(2):
            base = heads * (1 + 2 * q + part)
            for h in range(heads):
                spread[base + h, q * inner : (q + 1) * inner] = head_of == h
    gather = np.zeros((3, inner, chunk), np.float32)
    for q in range(3):
        for h in range(heads):
            gather[q, :, q * heads + h] = head_of == h
    return jnp.asarray(upper, BF), jnp.asarray(spread, BF), jnp.asarray(gather, BF)


def conv_from(ext, taps, rows, halo):
    n = taps.shape[0]
    out = taps[n - 1 : n, :] * ext[pl.ds(halo, rows), :]
    for k in range(1, n):
        out = out + taps[n - 1 - k : n - k, :] * ext[pl.ds(halo - k, rows), :]
    return out


def dt_rows(pdt, bias, rate, fill, heads, upper):
    chunk = pdt.shape[0]
    pre = jnp.transpose(pdt)[:heads] + bias
    live = (iota2(heads, chunk, 1) < fill).astype(F32)
    dt = softplus(pre) * live
    hi, mid, low = split3(dt * rate)
    stacked = jnp.concatenate([hi, mid, low], axis=0).astype(BF)
    summed = nn(stacked, upper)
    run = summed[:heads] + summed[heads : 2 * heads] + summed[2 * heads :]
    return pre, live, dt, run


def spread_all(run, dt, heads, chunk, spread):
    last = run[:, chunk - 1 : chunk]
    e_in = jnp.exp(run)
    e_out = jnp.exp(last - run)
    parts = [run]
    for v in (dt, e_in, e_out):
        parts.extend(split2(v))
    used = heads * len(parts)
    if used < chunk:
        parts.append(jnp.zeros((chunk - used, chunk), F32))
    cols = jnp.transpose(jnp.concatenate(parts, axis=0))
    return cols, nn(cols.astype(BF), spread)


def pair_stack(v, low_lanes):
    zero = jnp.zeros_like(v)
    return jnp.concatenate([jnp.where(low_lanes, v, zero), jnp.where(low_lanes, zero, v)], axis=0)


def scan_fwd_kernel(
    heads, starts, fill, px, pbd, convx, convbc, bias, rate, skip, upper, spread,
    y_out, sin_out, state, extx, extb,
):
    c = pl.program_id(0)
    chunk, inner = px.shape
    bc = convbc.shape[1]
    ns = bc // 2
    keep = starts[c] == 0

    @pl.when(c == 0)
    def _():
        state[...] = jnp.zeros_like(state)
        extx[...] = jnp.zeros_like(extx)
        extb[...] = jnp.zeros_like(extb)

    state[...] = jnp.where(keep, state[...], 0.0)
    extx[0:8, :] = jnp.where(keep, extx[chunk : chunk + 8, :], 0.0)
    extb[0:8, :] = jnp.where(keep, extb[chunk : chunk + 8, :], 0.0)
    extx[8 : chunk + 8, :] = px[...]
    extb[8 : chunk + 8, :] = pbd[:, :bc]

    n_live = fill[c]
    u = conv_from(extx, convx[...], chunk, 8)
    x = u * sigmoid(u) * (iota2(chunk, inner, 0) < n_live).astype(F32)
    ub = conv_from(extb, convbc[...], chunk, 8)
    act = (ub * sigmoid(ub) * (iota2(chunk, bc, 0) < n_live).astype(F32)).astype(BF)
    b, cc = act[:, :ns], act[:, ns:]

    _, _, dt, run = dt_rows(pbd[:, bc:], bias[...], rate[...], n_live, heads, upper[...])
    cols, wide = spread_all(run, dt, heads, chunk, spread[...])
    dt_w, ein_w, eout_w = wide[:, :inner], wide[:, inner : 2 * inner], wide[:, 2 * inner :]

    xd = x * dt_w
    xdb = xd.astype(BF)
    scores = nt(cc, b)
    tri = iota2(chunk, chunk, 0) >= iota2(chunk, chunk, 1)
    low_lanes = iota2(chunk, 2 * HD, 1) < HD
    diag = []
    for j in range(heads // 2):
        mix = []
        for h in (2 * j, 2 * j + 1):
            spread_h = cols[:, h : h + 1] - run[h : h + 1, :]
            mix.append((scores * jnp.exp(jnp.where(tri, spread_h, NEG))).astype(BF))
        pair = pair_stack(xdb[:, 2 * HD * j : 2 * HD * (j + 1)], low_lanes)
        diag.append(nn(jnp.concatenate(mix, axis=1), pair))
    enter = state[...]
    enter_b = enter.astype(BF)
    sin_out[0] = enter_b
    y_out[...] = jnp.concatenate(diag, axis=1) + ein_w * nn(cc, enter_b) + skip[...] * x
    state[...] = ein_w[chunk - 1 : chunk, :] * enter + tn(b, (xd * eout_w).astype(BF))


def scan_forward(px, pbd, conv_x, conv_bc, dt_bias, a_log, skip, starts, fill):
    tokens, inner = px.shape
    blocks = starts.shape[0]
    chunk = tokens // blocks
    heads = inner // HD
    bc = conv_bc.shape[1]
    upper, spread, _ = scan_constants(chunk, heads)
    bias = jnp.broadcast_to(dt_bias[:, None], (heads, chunk))
    rate = jnp.broadcast_to(-jnp.exp(a_log)[:, None], (heads, chunk))
    skip_w = jnp.repeat(skip, HD)[None, :]
    fixed = lambda c, *_: (0, 0)
    whole = lambda a: pl.BlockSpec(a.shape, fixed)
    rows = lambda w: pl.BlockSpec((chunk, w), lambda c, *_: (c, 0))
    return pl.pallas_call(
        functools.partial(scan_fwd_kernel, heads),
        grid_spec=pltpu.PrefetchScalarGridSpec(
            num_scalar_prefetch=2,
            grid=(blocks,),
            in_specs=[rows(inner), rows(pbd.shape[1])]
            + [whole(a) for a in (conv_x, conv_bc, bias, rate, skip_w, upper, spread)],
            out_specs=[rows(inner), pl.BlockSpec((1, bc // 2, inner), lambda c, *_: (c, 0, 0))],
            scratch_shapes=[
                pltpu.VMEM((bc // 2, inner), F32),
                pltpu.VMEM((chunk + 8, inner), F32),
                pltpu.VMEM((chunk + 8, bc), F32),
            ],
        ),
        out_shape=[
            jax.ShapeDtypeStruct((tokens, inner), F32),
            jax.ShapeDtypeStruct((blocks, bc // 2, inner), BF),
        ],
        compiler_params=pltpu.CompilerParams(vmem_limit_bytes=48 * 2**20),
        name="scan_forward",
    )(starts, fill, px, pbd, conv_x, conv_bc, bias, rate, skip_w, upper, spread)


def scan_bwd_kernel(
    heads, total_inner, starts, fill, ggn, y, pz, px, px_halo, pbd, pbd_halo, sin, rows, gain, convx, convbc,
    bias, rate, skip, upper, spread, gather, ones_h,
    lpx, lpz, lpbd, acc_x, acc_bc, acc_s, dstate, extx, extb, dux, dub,
):
    i = pl.program_id(0)
    blocks = pl.num_programs(0)
    c = blocks - 1 - i
    chunk, inner = px.shape
    bc = convbc.shape[1]
    ns = bc // 2
    taps_n = convx.shape[0]
    keep = starts[c] == 0
    nxt = jnp.minimum(c + 1, blocks - 1)
    keep_next = jnp.logical_and(starts[nxt] == 0, i > 0)
    n_live = fill[c]

    @pl.when(i == 0)
    def _():
        for ref in (dstate, dux, dub, acc_x, acc_bc, acc_s):
            ref[...] = jnp.zeros_like(ref)

    moved = jnp.transpose(
        jnp.concatenate([rows[0], jnp.zeros((chunk - rows.shape[1], chunk), F32)], axis=0)
    )
    inv = lax.rsqrt(moved[:, 0:1] / total_inner + EPS)
    coef = inv * inv * inv * (moved[:, 1:2] / total_inner)
    z = pz[...]
    sz = sigmoid(z)
    silu_z = z * sz
    yv = y[...]
    gated = yv * silu_z
    g = ggn[...]
    d_gated = inv * (g * gain[...]) - gated * coef
    lpz[...] = (d_gated * yv * (sz * (1.0 + z * (1.0 - sz)))).astype(BF)
    dy = d_gated * silu_z
    acc_x[taps_n : taps_n + 1, :] += jnp.sum(g * gated * inv, axis=0, keepdims=True)

    extx[0:8, :] = jnp.where(keep, px_halo[...], 0.0)
    extb[0:8, :] = jnp.where(keep, pbd_halo[:, :bc], 0.0)
    extx[8 : chunk + 8, :] = px[...]
    extb[8 : chunk + 8, :] = pbd[:, :bc]
    taps = convx[...]
    taps_b = convbc[...]
    live_x = (iota2(chunk, inner, 0) < n_live).astype(F32)
    live_b = (iota2(chunk, bc, 0) < n_live).astype(F32)
    u = conv_from(extx, taps, chunk, 8)
    su = sigmoid(u)
    x = u * su * live_x
    dx_du = su * (1.0 + u * (1.0 - su)) * live_x
    ub = conv_from(extb, taps_b, chunk, 8)
    sb = sigmoid(ub)
    act = (ub * sb * live_b).astype(BF)
    db_du = sb * (1.0 + ub * (1.0 - sb)) * live_b
    b, cc = act[:, :ns], act[:, ns:]

    pre, live, dt, run = dt_rows(pbd[:, bc:], bias[...], rate[...], n_live, heads, upper[...])
    cols, wide = spread_all(run, dt, heads, chunk, spread[...])
    dt_w, ein_w, eout_w = wide[:, :inner], wide[:, inner : 2 * inner], wide[:, 2 * inner :]
    xd = x * dt_w
    xdb = xd.astype(BF)
    dyb = dy.astype(BF)
    acc_x[taps_n + 1 : taps_n + 2, :] += jnp.sum(dy * x, axis=0, keepdims=True)

    scores_t = nt(b, cc)
    tri = iota2(chunk, chunk, 0) <= iota2(chunk, chunk, 1)
    low_lanes = iota2(chunk, 2 * HD, 1) < HD
    d_scores_t = jnp.zeros((chunk, chunk), F32)
    dxd = []
    pulls = []
    read_sums = []
    for j in range(heads // 2):
        span = slice(2 * HD * j, 2 * HD * (j + 1))
        dy_pair = pair_stack(dyb[:, span], low_lanes)
        x_pair = pair_stack(xdb[:, span], low_lanes)
        d_mix = nt(x_pair, dyb[:, span])
        mix = []
        for k in (0, 1):
            h = 2 * j + k
            spread_h = run[h : h + 1, :] - cols[:, h : h + 1]
            fade = jnp.exp(jnp.where(tri, spread_h, NEG))
            m = scores_t * fade
            dm = d_mix[k * chunk : (k + 1) * chunk]
            d_scores_t = d_scores_t + dm * fade
            pull = (dm * m).astype(BF)
            pulls.append(pull)
            read_sums.append(jnp.sum(pull.astype(F32), axis=0, keepdims=True))
            mix.append(m.astype(BF))
        dxd.append(nn(jnp.concatenate(mix, axis=1), dy_pair))
    source_sums = nn(jnp.concatenate(pulls, axis=1), ones_h[...])
    read_rows = jnp.concatenate(read_sums, axis=0)

    d_state = jnp.where(keep_next, dstate[...], 0.0)
    d_state_b = d_state.astype(BF)
    enter_b = sin[0]
    edy = ein_w * dy
    edyb = edy.astype(BF)
    readings = nn(cc, enter_b)
    from_state = nn(b, d_state_b) * eout_w
    d_xd = jnp.concatenate(dxd, axis=1) + from_state
    q1 = edy * readings
    q2 = xd * from_state
    decay = ein_w[chunk - 1 : chunk, :]
    dstate[...] = decay * d_state + tn(cc, edyb)
    d_cb = tn(d_scores_t.astype(BF), b) + nt(edyb, enter_b)
    d_b = nn(d_scores_t.astype(BF), cc) + nt((xd * eout_w).astype(BF), d_state_b)

    sums = (
        nn((d_xd * x).astype(BF), gather[0])
        + nn((q1 - q2).astype(BF), gather[1])
        + nn(q2.astype(BF), gather[2])
        - source_sums
    )
    sums_t = jnp.transpose(sums)
    dt_direct = sums_t[:heads]
    d_run = sums_t[heads : 2 * heads] + read_rows
    whole_q2 = jnp.sum(sums_t[2 * heads : 3 * heads], axis=1, keepdims=True)
    kept = jnp.sum(enter_b.astype(F32) * d_state, axis=0, keepdims=True) * decay
    kept_hi, kept_lo = split2(kept)
    kept_two = jnp.concatenate([kept_hi, kept_lo, jnp.zeros((6, inner), F32)], axis=0).astype(BF)
    kept_cols = nt(gather[3][:, :inner], kept_two)
    d_last = whole_q2 + kept_cols[:heads, 0:1] + kept_cols[:heads, 1:2]
    hi, mid, low = split3(d_run)
    back = nt(jnp.concatenate([hi, mid, low], axis=0).astype(BF), upper[...])
    d_a = back[:heads] + back[heads : 2 * heads] + back[2 * heads :] + d_last
    d_dt = dt_direct + d_a * rate[...]
    d_pre = d_dt * live * sigmoid(pre)
    acc_s[0:heads, :] += d_pre
    acc_s[heads : 2 * heads, :] += d_a * dt * rate[...]

    def conv_back(d_u, du_ref, ext_ref, tap_values, acc):
        du_ref[chunk : chunk + 8, :] = jnp.where(keep_next, du_ref[0:8, :], 0.0)
        du_ref[0:chunk, :] = d_u
        out = tap_values[taps_n - 1 : taps_n, :] * d_u
        acc[taps_n - 1 : taps_n, :] += jnp.sum(d_u * ext_ref[8 : chunk + 8, :], axis=0, keepdims=True)
        for k in range(1, taps_n):
            row = taps_n - 1 - k
            out = out + tap_values[row : row + 1, :] * du_ref[pl.ds(k, chunk), :]
            acc[row : row + 1, :] += jnp.sum(
                d_u * ext_ref[pl.ds(8 - k, chunk), :], axis=0, keepdims=True
            )
        return out

    d_x = d_xd * dt_w + skip[...] * dy
    lpx[...] = conv_back(d_x * dx_du, dux, extx, taps, acc_x).astype(BF)
    d_act = jnp.concatenate([d_b, d_cb], axis=1)
    lpbd[:, :bc] = conv_back(d_act * db_du, dub, extb, taps_b, acc_bc).astype(BF)
    pad = jnp.concatenate([d_pre, jnp.zeros((chunk - heads, chunk), F32)], axis=0)
    lpbd[:, bc:] = jnp.transpose(pad).astype(BF)


def scan_backward(
    ggn, y, pz, px, pbd, sin, rows, gain, conv_x, conv_bc, dt_bias, a_log, skip, starts, fill, total_inner
):
    tokens, inner = px.shape
    blocks = starts.shape[0]
    chunk = tokens // blocks
    heads = inner // HD
    bc = conv_bc.shape[1]
    upper, spread, gather = scan_constants(chunk, heads)
    selector = np.zeros((1, inner, chunk), np.float32)
    lanes = np.zeros((chunk, inner), np.float32)
    for h in range(heads):
        lanes[h, h * HD : (h + 1) * HD] = 1.0
    ones_h = np.zeros((heads * chunk, chunk), np.float32)
    for h in range(heads):
        ones_h[h * chunk : (h + 1) * chunk, heads + h] = 1.0
    ones_h = jnp.asarray(ones_h, BF)
    lanes = jnp.asarray(lanes, BF)
    bias = jnp.broadcast_to(dt_bias[:, None], (heads, chunk))
    rate = jnp.broadcast_to(-jnp.exp(a_log)[:, None], (heads, chunk))
    skip_w = jnp.repeat(skip, HD)[None, :]
    whole = lambda a: pl.BlockSpec(a.shape, lambda i, *_: (0,) * a.ndim)
    back = lambda w: pl.BlockSpec((chunk, w), lambda i, *_: (blocks - 1 - i, 0))
    halo = lambda w: pl.BlockSpec(
        (8, w), lambda i, *_: (jnp.maximum((blocks - 1 - i) * (chunk // 8) - 1, 0), 0)
    )
    width = pbd.shape[1]
    consts = (gain[None, :], conv_x, conv_bc, bias, rate, skip_w, upper, spread, gather, lanes, ones_h)

    def kernel(*refs):
        n_in = 2 + 9
        ins, cons, rest = refs[:n_in], refs[n_in : n_in + 11], refs[n_in + 11 :]
        gain_r, cx, cb, bias_r, rate_r, skip_r, up, sp, ga, la, on = cons

        class Gather:
            def __getitem__(self, k):
                return la[...] if k == 3 else ga[k]

        scan_bwd_kernel(
            heads, total_inner, *ins, gain_r, cx, cb, bias_r, rate_r, skip_r, up, sp, Gather(), on, *rest
        )

    return pl.pallas_call(
        kernel,
        grid_spec=pltpu.PrefetchScalarGridSpec(
            num_scalar_prefetch=2,
            grid=(blocks,),
            in_specs=[
                back(inner), back(inner), back(inner), back(inner), halo(inner), back(width), halo(width),
                pl.BlockSpec((1, bc // 2, inner), lambda i, *_: (blocks - 1 - i, 0, 0)),
                pl.BlockSpec((1, 8, chunk), lambda i, *_: (blocks - 1 - i, 0, 0)),
            ]
            + [whole(a) for a in consts],
            out_specs=[
                back(inner), back(inner), back(width),
                pl.BlockSpec((8, inner), lambda i, *_: (0, 0)),
                pl.BlockSpec((8, bc), lambda i, *_: (0, 0)),
                pl.BlockSpec((2 * heads, chunk), lambda i, *_: (0, 0)),
            ],
            scratch_shapes=[
                pltpu.VMEM((bc // 2, inner), F32),
                pltpu.VMEM((chunk + 8, inner), F32),
                pltpu.VMEM((chunk + 8, bc), F32),
                pltpu.VMEM((chunk + 8, inner), F32),
                pltpu.VMEM((chunk + 8, bc), F32),
            ],
        ),
        out_shape=[
            jax.ShapeDtypeStruct((tokens, inner), BF),
            jax.ShapeDtypeStruct((tokens, inner), BF),
            jax.ShapeDtypeStruct((tokens, width), BF),
            jax.ShapeDtypeStruct((8, inner), F32),
            jax.ShapeDtypeStruct((8, bc), F32),
            jax.ShapeDtypeStruct((2 * heads, chunk), F32),
        ],
        compiler_params=pltpu.CompilerParams(vmem_limit_bytes=48 * 2**20),
        name="scan_backward",
    )(starts, fill, ggn, y, pz, px, px, pbd, pbd, sin, rows, *consts)


def body(
    tokens, cotangent, starts, fill, norm_gain, w_x, w_z, w_dt, w_bc, conv_x, conv_bc, dt_bias, a_log, skip,
    gate_gain, w_out,
):
    heads_n = lax.axis_size("heads")
    head_index = lax.axis_index("heads")
    count, columns = tokens.shape
    width = columns * heads_n
    blocks = starts.shape[0]
    chunk = count // blocks
    inner = w_x.shape[1]
    heads = w_dt.shape[1]
    bc = w_bc.shape[1]
    total_inner = inner * heads_n
    dt_pad = jnp.pad(w_dt, ((0, 0), (0, chunk - heads)))
    packed = jnp.concatenate([w_x, w_z, w_bc, dt_pad, w_out], axis=1)
    rows_all = lax.all_gather(packed, "dp", axis=0, tiled=True)
    rows_x, rows_z = rows_all[:, :inner], rows_all[:, inner : 2 * inner]
    rows_bd, rows_out = rows_all[:, 2 * inner : 2 * inner + bc + chunk], rows_all[:, 2 * inner + bc + chunk :]
    whole = lax.all_gather(tokens, "heads", axis=1, tiled=True).astype(F32)
    inverse = lax.rsqrt(jnp.mean(whole * whole, axis=-1, keepdims=True) + EPS)
    normed = (whole * inverse * norm_gain).astype(BF)
    px, pz, pbd = nn(normed, rows_x), nn(normed, rows_z), nn(normed, rows_bd)
    y, sin = scan_forward(px, pbd, conv_x, conv_bc, dt_bias, a_log, skip, starts, fill)
    g_full = lax.all_gather(cotangent, "heads", axis=1, tiled=True)
    ggn = nn(g_full, rows_out)
    gated = y * jax.nn.silu(pz)
    both = jnp.stack(
        [jnp.sum(gated * gated, axis=-1), jnp.sum(gated * gate_gain * ggn, axis=-1)], axis=0
    )
    both = lax.psum(both, "heads")
    rows = jnp.pad(jnp.transpose(both.reshape(2, blocks, chunk), (1, 0, 2)), ((0, 0), (0, 6), (0, 0)))
    gate_inverse = lax.rsqrt(both[0] / total_inner + EPS)[:, None]
    gated_normed = (gated * gate_inverse * gate_gain).astype(BF)
    partial_out = nt(gated_normed, rows_out)
    out_share = lax.psum_scatter(partial_out, "heads", scatter_dimension=1, tiled=True)
    block_out = (tokens.astype(F32) + out_share).astype(BF)
    lpx, lpz, lpbd, acc_x, acc_bc, acc_s = scan_backward(
        ggn, y, pz, px, pbd, sin, rows, gate_gain, conv_x, conv_bc, dt_bias, a_log, skip, starts, fill,
        total_inner,
    )
    partial_in = nt(lpx, rows_x) + nt(lpz, rows_z) + nt(lpbd, rows_bd)
    in_share = lax.psum_scatter(partial_in, "heads", scatter_dimension=1, tiled=True)
    own = tokens.astype(F32)
    own_gain = lax.dynamic_slice_in_dim(norm_gain, head_index * columns, columns, 0)
    gain_part = jnp.sum(in_share * own * inverse, axis=0)
    norm_dots = lax.psum(jnp.sum(in_share * own_gain * own, axis=-1), "heads")
    grad_tokens = (
        cotangent.astype(F32)
        + inverse * own_gain * in_share
        - own * inverse**3 * (norm_dots / width)[:, None]
    )
    grads = jnp.concatenate(
        [tn(normed, lpx), tn(normed, lpz), tn(normed, lpbd), tn(g_full, gated_normed)], axis=1
    )
    grads = lax.psum_scatter(grads, "dp", scatter_dimension=0, tiled=True)
    grad_w_x, grad_w_z = grads[:, :inner], grads[:, inner : 2 * inner]
    grad_bd = grads[:, 2 * inner : 2 * inner + bc + chunk]
    grad_w_bc = lax.psum(grad_bd[:, :bc], "heads")
    grad_w_dt = grad_bd[:, bc : bc + heads]
    grad_w_out = grads[:, 2 * inner + bc + chunk :]
    taps = conv_x.shape[0]
    small = jnp.concatenate([acc_x.reshape(-1), jnp.sum(acc_s, axis=1), gain_part])
    small = lax.psum(small, "dp")
    grad_conv_bc = lax.psum(acc_bc[:taps], ("dp", "heads"))
    acc_x = small[: acc_x.size].reshape(acc_x.shape)
    acc_s = small[acc_x.size : acc_x.size + 2 * heads]
    return (
        block_out, grad_tokens, small[acc_x.size + 2 * heads :], grad_w_x, grad_w_z, grad_w_dt, grad_w_bc,
        acc_x[:taps], grad_conv_bc, acc_s[:heads], acc_s[heads:],
        jnp.sum(acc_x[taps + 1].reshape(heads, HD), axis=1), acc_x[taps], grad_w_out,
    )


def solution(mesh):
    placed = (
        P("dp", "heads"),
        P("dp", "heads"),
        P("dp"),
        P("dp"),
        P(),
        P("dp", "heads"),
        P("dp", "heads"),
        P("dp", "heads"),
        P("dp", None),
        P(None, "heads"),
        P(),
        P("heads"),
        P("heads"),
        P("heads"),
        P("heads"),
        P("dp", "heads"),
    )
    return jax.shard_map(
        body,
        mesh=mesh,
        in_specs=placed,
        out_specs=(
            P("dp", "heads"),
            P("dp", "heads"),
            P("heads"),
            P("dp", "heads"),
            P("dp", "heads"),
            P("dp", "heads"),
            P("dp", None),
            P(None, "heads"),
            P(),
            P("heads"),
            P("heads"),
            P("heads"),
            P("heads"),
            P("dp", "heads"),
        ),
        check_vma=False,
    )
```

time: 1020 us -> 579 us (0.57); the launches traced: 999 us -> 574 us
  other arithmetic: 190 us -> 14.5 us
  local copies, waits for them, and re-layouts: 141 us -> 18.6 us
  matrix products: 185 us -> 76.6 us
  Pallas kernels: 0 us -> 62.5 us
  waiting for transfers between devices: 351 us -> 293 us
  blocking collectives: 116 us -> 93.3 us
    reduce_scatter x5 -> x1, waiting for transfers between devices: 260 us -> 124 us  [body(): grads = lax.psum_scatter(grads, 'dp', scatter_dimension=0, tiled=True)]
    dot_general x27 -> x12, matrix products: 185 us -> 76.6 us  [the longest x4 35 us: nt(): lax.dot_general(a, b, (((1,), (1,)), ((), ())), preferred_element_type=F32)]
    all_gather x5 -> x3, waiting for transfers between devices: 0.06 us -> 101 us  [the longest x1 69.8 us: body(): rows_all = lax.all_gather(packed, 'dp', axis=0, tiled=True)]
    reduce_sum x29 -> x4, other arithmetic: 69.8 us -> 6.53 us  [the longest x1 3.07 us: body(): inverse = lax.rsqrt(jnp.mean(whole * whole, axis=-1, keepdims=True) + EPS)]
    pallas_call x0 -> x2, Pallas kernels: none -> 62.5 us  [the longest x1 42.6 us: scan_backward(): pl.pallas_call(kernel, grid_spec=pltpu.PrefetchScalarGridSpec(num_scalar_...]
    all_gather x2 -> x0, blocking collectives: 59.5 us -> none  [the longest x1 31.5 us: body(): lax.all_gather(w_bc, 'dp', axis=0, tiled=True)]
    reshape x7 -> x0, local copies, waits for them, and re-layouts: 43.5 us -> none  [the longest x4 29 us: state_space(): x_blocks = inputs.reshape(blocks, span, head_count, head_dim)]
    dynamic_slice x32 -> x0, local copies, waits for them, and re-layouts: 39.8 us -> none  [state_space(): lax.scan(advance, jnp.zeros((head_count, head_dim, state_dim), jnp.float3...]
  transfers between devices with their start and end apart: 13 -> 7, of which waited for: 6 -> 5; matrix products, arithmetic and copies ran while one was open for 32% -> 13% of each run, Pallas kernels for 0% -> 3%
where the time goes in v1:
time: 579 us; the launch traced here: 574 us
  waiting for transfers between devices  293 us (51%)
  blocking collectives  93.3 us (16%)
  matrix products  76.6 us (13%)
  Pallas kernels  62.5 us (11%)
  local copies, waits for them, and re-layouts  18.6 us (3%)
  between operations  15 us (3%)
  other arithmetic  14.5 us (3%)
    reduce_scatter x1, waiting for transfers between devices, body(): grads = lax.psum_scatter(grads, 'dp', scatter_dimension=0, tiled=True)  124 us
    all_gather x1, waiting for transfers between devices, body(): rows_all = lax.all_gather(packed, 'dp', axis=0, tiled=True)  69.8 us
    pallas_call x1, Pallas kernels, scan_backward(): pl.pallas_call(kernel, grid_spec=pltpu.PrefetchScalarGridSpec(num_scalar_...  42.6 us
    reduce_scatter x1, waiting for transfers between devices, body(): lax.psum_scatter(partial_in, 'heads', scatter_dimension=1, tiled=True)  41.4 us
    psum x1, blocking collectives, body(): grad_conv_bc = lax.psum(acc_bc[:taps], ('dp', 'heads'))  39.4 us
    psum x1, blocking collectives, body(): small = lax.psum(small, 'dp')  37.1 us
    dot_general x4, matrix products, nt(): lax.dot_general(a, b, (((1,), (1,)), ((), ())), preferred_element_type=F32)  35 us
    all_gather x1, waiting for transfers between devices, body(): whole = lax.all_gather(tokens, 'heads', axis=1, tiled=True).astype(F32)  31.3 us
  transfers between devices with their start and end apart: 7, of which 5 were waited for; matrix products, arithmetic and copies ran while one was open for 13% of the time, Pallas kernels for 3%

profile of v1, /device:TPU:0, one launch (start us, length us, event | category | flops | bytes accessed | tf_op | source)
XLA Modules:
  0.0 573.7 jit_solution(5967382564057945219)
XLA Ops:
  7.2 0.7 all-gather.4.cloned.1.call-update
  8.0 0.8 copy.46
  8.8 0.9 constant_dynamic-update-slice_fusion.3
  9.7 0.9 constant_dynamic-update-slice_fusion.2
  10.6 0.8 constant_dynamic-update-slice_fusion.1
  11.5 0.9 constant_dynamic-update-slice_fusion
  12.4 0.8 copy-done.26
  13.2 0.0 all-gather.8.cloned.1.call-start
  13.2 0.7 all-gather.8.cloned.1.call-update
  13.9 0.0 reduce-scatter.8.cloned.1.call-start
  14.0 0.7 broadcast_in_dim.10
  14.7 0.7 broadcast_in_dim_reshape.4.skip.refs_16_
  15.4 0.7 exponential_negate_fusion
  16.0 31.3 %all-gather.4.cloned.1.call-done = bf16[2048,1024]{1,0:T(8,128)(2,1)} async-done(((bf16[2048,256]{1,0:T(8,128)(2,1)}), bf16[2048,1024]{1,0:T(8,128)(2,1)}) %all-gather.4.cloned.1.call-update) | async-done | bytes 4194320 | tf_op jit(solution)/shard_map/all_gather | solution.py:449
  47.3 3.1 fusion
  50.4 69.8 %all-gather.6.cloned.1.call-done = bf16[1024,1920]{1,0:T(8,128)(2,1)} async-done(((bf16[128,1920]{1,0:T(8,128)(2,1)}), bf16[1024,1920]{1,0:T(8,128)(2,1)}) %all-gather.6.cloned.1.call-update) | async-done | bytes 3932176 | tf_op jit(solution)/shard_map/all_gather | solution.py:446
  120.2 4.9 fusion.21.pbd.refs_7_.refs_8_
  125.3 6.9 %fusion.18.px.refs_5_.refs_6_ = f32[2048,512]{1,0:T(8,128)} fusion(bf16[1024,1920]{1,0:T(8,128)(2,1)} %all-gather.6.cloned.1.call-done, bf16[2048,1024]{1,0:T(8,128)(2,1)S(1)} %copy-done.23, f32[1024]{0:T(1024)S(1)} %copy-done.28, f32[2048]{0:T(1024)S(1)} %get-tuple-element.73), kind=kOutput, calls=%fused_computation.32 | convolution fusion | flops 2155872256 | bytes 9449472 | tf_op jit(solution)/shard_map/dot_general | solution.py:18
  132.2 0.1 broadcast_in_dim.9.rate.refs_15_
  132.3 0.1 broadcast_in_dim.8.bias.refs_14_
  132.4 19.8 %scan_forward.1 = (f32[2048,512]{1,0:T(8,128)}, bf16[16,128,512]{2,1,0:T(8,128)(2,1)S(1)}) custom-call(s32[16]{0:T(128)S(1)} %copy-done.14, s32[16]{0:T(128)S(1)} %copy-done.16, f32[2048,512]{1,0:T(8,128)} %fusion.18.px.refs_5_.refs_6_, f32[2048,384]{1,0:T(8,128)S(1)} %fusion.21.pbd.refs_7_.refs_8_, f32[4,512]{1,0:T(4,128)S(1)} %copy-done.8, ...), custom_call_target="tpu_custom_call" | custom-call | tf_op jit(solution)/shard_map/scan_forward/pallas_call | solution.py:176
  152.3 1.3 copy-done.1
  153.6 5.8 %fusion.14.refs_4_ = f32[2048,512]{1,0:T(8,128)} fusion(bf16[1024,1920]{1,0:T(8,128)(2,1)} %all-gather.6.cloned.1.call-done, bf16[2048,1024]{1,0:T(8,128)(2,1)S(1)} %copy-done.23, f32[1024]{0:T(1024)S(1)} %copy-done.28, f32[2048]{0:T(1024)S(1)} %get-tuple-element.73), kind=kOutput, calls=%fused_computation.28 | convolution fusion | flops 2155872256 | bytes 9449472 | tf_op jit(solution)/shard_map/dot_general | solution.py:18
  159.5 11.8 %multiply_reduce_fusion.1 = (f32[2048]{0:T(1024)S(1)}, f32[2048]{0:T(1024)S(1)}, f32[2048,512]{1,0:T(8,128)}, f32[2048,512]{1,0:T(8,128)}) fusion(f32[512]{0:T(512)S(1)} %copy-done.11, f32[2048,512]{1,0:T(8,128)} %get-tuple-element.22.refs_3_, f32[2048,512]{1,0:T(8,128)} %fusion.14.refs_4_, bf16[2048,1024]{1,0:T(8,128)(2,1)} %all-gather.8.cloned.1.call-done, ...), kind=kOutput, calls=%fused_computation.9 | convolution fusion | flops 2157965312 | bytes 22038528 | tf_op jit(solution)/shard_map/dot_general | solution.py:18
  171.3 10.3 %psum.35 = f32[2,2048]{1,0:T(2,128)S(1)} all-reduce(f32[2,2048]{1,0:T(2,128)S(1)} %pad_maximum_fusion.1), channel_id=1, replica_groups=mesh['dp'=8,'heads'=4] {'heads'}, use_global_device_ids=true, to_apply=%region_3.4 | all-reduce | flops 4096 | bytes 32768 | tf_op jit(solution)/shard_map/psum | solution.py:460
  181.8 42.6 %scan_backward.1 = (bf16[2048,512]{1,0:T(8,128)(2,1)S(1)}, bf16[2048,512]{1,0:T(8,128)(2,1)}, bf16[2048,384]{1,0:T(8,128)(2,1)S(1)}, f32[8,512]{1,0:T(8,128)S(1)...) custom-call(s32[16]{0:T(128)S(1)} %copy-done.15, s32[16]{0:T(128)S(1)} %copy-done.17, ...), custom_call_target="tpu_custom_call" | custom-call | tf_op jit(solution)/shard_map/scan_backward/pallas_call | solution.py:392
  224.5 4.9 fusion.27
  229.4 2.6 fusion.29
  232.0 2.1 fusion.25
  234.1 0.1 copy-done.22
  234.2 1.3 copy-done.29
  235.4 2.5 convolution_bitcast_fusion.1
  237.9 3.7 pad_maximum_fusion
  241.7 0.3 all-reduce.4.cloned.1.call-start
  242.0 7.8 %fusion.12 = f32[2048,1024]{1,0:T(8,128)} fusion(bf16[2048,512]{1,0:T(8,128)(2,1)} %get-tuple-element.25, bf16[1024,1920]{1,0:T(8,128)(2,1)} %all-gather.6.cloned.1.call-done), kind=kOutput, calls=%fused_computation.26 | convolution fusion | flops 2147483648 | bytes 11534336 | tf_op jit(solution)/shard_map/dot_general | solution.py:22
  249.8 7.0 %fusion.16 = f32[2048,1024]{1,0:T(8,128)} fusion(bf16[2048,512]{1,0:T(8,128)(2,1)S(1)} %copy-done.19, bf16[1024,1920]{1,0:T(8,128)(2,1)} %all-gather.6.cloned.1.call-done), kind=kOutput, calls=%fused_computation.30 | convolution fusion | flops 2147483648 | bytes 11534336 | tf_op jit(solution)/shard_map/dot_general | solution.py:22
  256.9 123.8 %reduce-scatter.8.cloned.1.call-done = f32[128,1920]{0,1:T(8,128)} async-done(((f32[1024,1920]{0,1:T(8,128)}), f32[128,1920]{0,1:T(8,128)}) %reduce-scatter.8.cloned.1.call-update) | async-done | bytes 983056 | tf_op jit(solution)/shard_map/reduce_scatter | solution.py:485
  380.7 1.6 slice.100
  382.3 0.0 reduce-scatter.6.cloned.1.call-start
  382.3 11.8 %add_add_fusion = f32[2048,1024]{1,0:T(8,128)} fusion(f32[2048,1024]{1,0:T(8,128)} %fusion.16, f32[2048,1024]{1,0:T(8,128)} %fusion.12, bf16[2048,384]{1,0:T(8,128)(2,1)S(1)} %get-tuple-element.26, bf16[1024,1920]{1,0:T(8,128)(2,1)} %all-gather.6.cloned.1.call-done), kind=kOutput, calls=%fused_computation.5 | convolution fusion | flops 1614807040 | bytes 27525120 | tf_op jit(solution)/shard_map/dot_general | solution.py:22
  394.2 0.0 reduce-scatter.4.cloned.1.call-start
  394.2 8.3 %fusion.9 = f32[2048,1024]{1,0:T(8,128)} fusion(bf16[1024,1920]{1,0:T(8,128)(2,1)} %all-gather.6.cloned.1.call-done, f32[2048,512]{1,0:T(8,128)} %get-tuple-element.62, f32[2048]{0:T(1024)S(1)} %bitcast.24, f32[512]{0:T(512)S(1)} %copy-done.11), kind=kOutput, calls=%fused_computation.23 | convolution fusion | flops 2150629376 | bytes 13641728 | tf_op jit(solution)/shard_map/dot_general | solution.py:22
  402.5 0.1 dynamic_slice.3
  402.6 0.1 reduce_sum.67
  402.7 39.4 %psum.39 = f32[4,256]{1,0:T(4,128)} all-reduce(f32[4,256]{1,0:T(4,128)S(1)} %slice.84), channel_id=1, replica_groups=mesh['dp'=8,'heads'=4] {'dp','heads'}, use_global_device_ids=true, to_apply=%region_13.14 | all-reduce | flops 1024 | bytes 8192 | tf_op jit(solution)/shard_map/psum | solution.py:494
  442.1 0.1 fusion.34
  442.2 0.8 copy.51
  443.0 0.8 copy.52
  443.8 0.8 copy.54
  444.7 0.6 slice.99
  445.3 1.7 copy.53
  446.9 41.4 %reduce-scatter.6.cloned.1.call-done = f32[2048,256]{1,0:T(8,128)} async-done(((f32[2048,1024]{1,0:T(8,128)}), f32[2048,256]{1,0:T(8,128)}) %reduce-scatter.6.cloned.1.call-update) | async-done | bytes 2097168 | tf_op jit(solution)/shard_map/reduce_scatter | solution.py:472
  488.3 2.7 fusion.8
  491.1 0.1 concatenate.10
  491.1 37.1 %psum.37 = f32[4368]{0:T(1024)S(1)} all-reduce(f32[4368]{0:T(1024)S(1)} %concatenate.10), channel_id=1, replica_groups=mesh['dp'=8,'heads'=4] {'dp'}, use_global_device_ids=true, to_apply=%region_10.11 | all-reduce | flops 4368 | bytes 34944 | tf_op jit(solution)/shard_map/psum | solution.py:493
  528.2 0.6 slice.96
  528.9 0.6 slice.83
  529.5 0.6 fusion.35
  530.0 0.1 slice.88
  530.1 0.6 reduce_sum.69
  530.7 6.5 %psum.36 = f32[2048]{0:T(1024)S(1)} all-reduce(f32[2048]{0:T(1024)S(1)} %get-tuple-element.61), channel_id=1, replica_groups=mesh['dp'=8,'heads'=4] {'heads'}, use_global_device_ids=true, to_apply=%region_7.8 | all-reduce | flops 2048 | bytes 16384 | tf_op jit(solution)/shard_map/psum | solution.py:476
  537.2 0.6 fusion.36
  537.8 25.1 %reduce-scatter.4.cloned.1.call-done = f32[2048,256]{1,0:T(8,128)} async-done(((f32[2048,1024]{1,0:T(8,128)}), f32[2048,256]{1,0:T(8,128)}) %reduce-scatter.4.cloned.1.call-update) | async-done | bytes 2097168 | tf_op jit(solution)/shard_map/reduce_scatter | solution.py:465
  563.0 3.5 fusion.5
  (74 shorter events, 0.4 us)
Async XLA Ops:
  7.2 113.1 %copy-start.28 = (f32[1024]{0:T(1024)S(1)}, f32[1024]{0:T(1024)}, u32[]{:S(2)}) copy-start(f32[1024]{0:T(1024)} %param.27) | copy-start | bytes 12292
  7.2 40.1 %all-gather.4.cloned.1.call-start = ((), (), s32[]{:S(2)}) async-start(), calls=%async_computation.3 | async-start | bytes 5242880 | tf_op jit(solution)/shard_map/all_gather | solution.py:449
  7.9 112.3 %all-gather.6.cloned.1.call-start = ((), (), s32[]{:S(2)}) async-start(), calls=%async_computation.4 | async-start | bytes 4423680 | tf_op jit(solution)/shard_map/all_gather | solution.py:446
  12.4 0.8 copy-start.26
  13.2 146.2 %all-gather.8.cloned.1.call-start = ((), (), s32[]{:S(2)}) async-start(), calls=%async_computation.5 | async-start | bytes 5242880 | tf_op jit(solution)/shard_map/all_gather | solution.py:454
  13.9 366.7 %reduce-scatter.8.cloned.1.call-start = ((), (), s32[]{:S(2)}) async-start(), calls=%async_computation.8 | async-start | bytes 8847360 | tf_op jit(solution)/shard_map/reduce_scatter | solution.py:485
  120.2 4.9 copy-start.23
  125.2 7.2 %copy-start = (f32[2048,384]{1,0:T(8,128)}, f32[2048,384]{1,0:T(8,128)S(1)}, u32[]{:S(2)}) copy-start(f32[2048,384]{1,0:T(8,128)S(1)} %fusion.21.pbd.refs_7_.refs_8_) | copy-start | bytes 9437188
  125.2 7.1 %copy-start.27 = (f32[8]{0:T(128)S(1)}, f32[8]{0:T(128)}, u32[]{:S(2)}) copy-start(f32[8]{0:T(128)} %param.34) | copy-start | bytes 100
  125.2 7.2 %copy-start.2 = (bf16[128,1536]{1,0:T(8,128)(2,1)S(1)}, bf16[128,1536]{1,0:T(8,128)(2,1)}, u32[]{:S(2)}) copy-start(bf16[128,1536]{1,0:T(8,128)(2,1)} %constant.40.clone.spread.refs_18_) | copy-start | bytes 1179652
  125.2 7.2 %copy-start.6 = (bf16[128,128]{1,0:T(8,128)(2,1)S(1)}, bf16[128,128]{1,0:T(8,128)(2,1)}, u32[]{:S(2)}) copy-start(bf16[128,128]{1,0:T(8,128)(2,1)} %constant.39.clone.upper.refs_17_) | copy-start | bytes 98308
  125.2 7.1 %copy-start.8 = (f32[4,512]{1,0:T(4,128)S(1)}, f32[4,512]{1,0:T(4,128)}, u32[]{:S(2)}) copy-start(f32[4,512]{1,0:T(4,128)} %refs_12_.1) | copy-start | bytes 24580
  125.2 7.1 %copy-start.9 = (f32[1,512]{1,0:T(1,128)S(1)}, f32[1,512]{1,0:T(1,128)}, u32[]{:S(2)}) copy-start(f32[1,512]{1,0:T(1,128)} %broadcast_in_dim_reshape.4.skip.refs_16_) | copy-start | bytes 6148
  125.3 7.1 %copy-start.12 = (f32[4,256]{1,0:T(4,128)S(1)}, f32[4,256]{1,0:T(4,128)}, u32[]{:S(2)}) copy-start(f32[4,256]{1,0:T(4,128)} %refs_13_.1) | copy-start | bytes 12292
  125.3 7.1 %copy-start.14 = (s32[16]{0:T(128)S(1)}, s32[16]{0:T(128)}, u32[]{:S(2)}) copy-start(s32[16]{0:T(128)} %refs_0_.1) | copy-start | bytes 196
  125.3 7.1 %copy-start.16 = (s32[16]{0:T(128)S(1)}, s32[16]{0:T(128)}, u32[]{:S(2)}) copy-start(s32[16]{0:T(128)} %refs_1_.1) | copy-start | bytes 196
  152.3 1.3 copy-start.1
  153.6 5.8 %copy-start.11 = (f32[512]{0:T(512)S(1)}, f32[512]{0:T(512)}, u32[]{:S(2)}) copy-start(f32[512]{0:T(512)} %param.37) | copy-start | bytes 6148
  159.4 22.3 %copy-start.3 = (bf16[3,512,128]{2,1,0:T(8,128)(2,1)S(1)}, bf16[3,512,128]{2,1,0:T(8,128)(2,1)}, u32[]{:S(2)}) copy-start(bf16[3,512,128]{2,1,0:T(8,128)(2,1)} %constant.41.clone.refs_19_) | copy-start | bytes 1179652
  159.4 22.3 %copy-start.4 = (bf16[1024,128]{1,0:T(8,128)(2,1)S(1)}, bf16[1024,128]{1,0:T(8,128)(2,1)}, u32[]{:S(2)}) copy-start(bf16[1024,128]{1,0:T(8,128)(2,1)} %constant.42.clone.refs_21_) | copy-start | bytes 786436
  159.4 22.3 %copy-start.5 = (bf16[128,512]{1,0:T(8,128)(2,1)S(1)}, bf16[128,512]{1,0:T(8,128)(2,1)}, u32[]{:S(2)}) copy-start(bf16[128,512]{1,0:T(8,128)(2,1)} %constant.43.clone.refs_20_) | copy-start | bytes 393220
  159.4 22.3 %copy-start.7 = (bf16[128,128]{1,0:T(8,128)(2,1)S(1)}, bf16[128,128]{1,0:T(8,128)(2,1)}, u32[]{:S(2)}) copy-start(bf16[128,128]{1,0:T(8,128)(2,1)} %constant.39.clone.upper.refs_17_) | copy-start | bytes 98308
  159.4 22.3 %copy-start.10 = (f32[1,512]{1,0:T(1,128)S(1)}, f32[1,512]{1,0:T(1,128)}, u32[]{:S(2)}) copy-start(f32[1,512]{1,0:T(1,128)} %broadcast_in_dim_reshape.4.skip.refs_16_) | copy-start | bytes 6148
  159.4 22.3 %copy-start.13 = (f32[4,256]{1,0:T(4,128)S(1)}, f32[4,256]{1,0:T(4,128)}, u32[]{:S(2)}) copy-start(f32[4,256]{1,0:T(4,128)} %refs_13_.1) | copy-start | bytes 12292
  159.5 22.3 %copy-start.15 = (s32[16]{0:T(128)S(1)}, s32[16]{0:T(128)}, u32[]{:S(2)}) copy-start(s32[16]{0:T(128)} %refs_0_.1) | copy-start | bytes 196
  159.5 22.3 %copy-start.17 = (s32[16]{0:T(128)S(1)}, s32[16]{0:T(128)}, u32[]{:S(2)}) copy-start(s32[16]{0:T(128)} %refs_1_.1) | copy-start | bytes 196
  181.8 42.7 %copy-start.24 = (bf16[2048,1024]{1,0:T(8,128)(2,1)S(1)}, bf16[2048,1024]{1,0:T(8,128)(2,1)}, u32[]{:S(2)}) copy-start(bf16[2048,1024]{1,0:T(8,128)(2,1)} %all-gather.4.cloned.1.call-done) | copy-start | bytes 12582916
  224.4 4.9 copy-start.18
  232.0 2.2 copy-start.22
  232.0 3.5 copy-start.29
  241.7 203.6 %all-reduce.4.cloned.1.call-start = ((), (), s32[]{:S(2)}) async-start(), calls=%async_computation.9 | async-start | bytes 262144 | tf_op jit(solution)/shard_map/psum | solution.py:488
  242.0 7.9 %copy-start.19 = (bf16[2048,512]{1,0:T(8,128)(2,1)S(1)}, bf16[2048,512]{1,0:T(8,128)(2,1)}, u32[]{:S(2)}) copy-start(bf16[2048,512]{1,0:T(8,128)(2,1)} %copy-done.18) | copy-start | bytes 6291460
  382.3 106.1 %reduce-scatter.6.cloned.1.call-start = ((), (), s32[]{:S(2)}) async-start(), calls=%async_computation.7 | async-start | bytes 10485760 | tf_op jit(solution)/shard_map/reduce_scatter | solution.py:472
  394.2 168.8 %reduce-scatter.4.cloned.1.call-start = ((), (), s32[]{:S(2)}) async-start(), calls=%async_computation.6 | async-start | bytes 10485760 | tf_op jit(solution)/shard_map/reduce_scatter | solution.py:465
  402.5 39.6 %copy-start.25 = (f32[128,1920]{0,1:T(8,128)S(1)}, f32[128,1920]{0,1:T(8,128)}, u32[]{:S(2)}) copy-start(f32[128,1920]{0,1:T(8,128)} %reduce-scatter.8.cloned.1.call-done) | copy-start | bytes 2949124
  402.5 85.8 %copy-start.20 = (bf16[2048,256]{1,0:T(8,128)(2,1)S(1)}, bf16[2048,256]{1,0:T(8,128)(2,1)}, u32[]{:S(2)}) copy-start(bf16[2048,256]{1,0:T(8,128)(2,1)} %param.23) | copy-start | bytes 3145732
  488.3 74.6 %copy-start.21 = (f32[2048,256]{1,0:T(8,128)S(1)}, f32[2048,256]{1,0:T(8,128)}, u32[]{:S(2)}) copy-start(f32[2048,256]{1,0:T(8,128)} %reduce-scatter.6.cloned.1.call-done) | copy-start | bytes 6291460
Sparse Core Ops, SparseCore 0:
  9.6 37.7 all-gather.3
  50.1 70.0 all-gather.5
  121.8 33.3 all-gather.7
  241.8 138.8 reduce-scatter.7
  383.4 30.4 all-reduce.3
  416.5 71.7 reduce-scatter.5
  490.9 71.9 reduce-scatter.3

commit v2 on v1

--- a/solution.py
+++ b/solution.py
@@ -12,6 +12,7 @@
 F32 = jnp.float32
 BF = jnp.bfloat16
 NEG = -1e30
+MESH = pl.DeviceIdType.MESH
 
 
 def nn(a, b):
@@ -425,6 +426,575 @@
         compiler_params=pltpu.CompilerParams(vmem_limit_bytes=48 * 2**20),
         name="scan_backward",
     )(starts, fill, ggn, y, pz, px, px, pbd, pbd, sin, rows, *consts)
+def peers(dp_n):
+    dp, hm = lax.axis_index("dp"), lax.axis_index("heads")
+    across, core = hm // 2, hm % 2
+    pair, line, lines = dp % 2, dp // 2, dp_n // 2
+    return dict(
+        sib=(dp, 2 * across + 1 - core),
+        xn=(dp, 2 * (1 - across) + core),
+        dg=(dp, 2 * (1 - across) + 1 - core),
+        yn=(2 * line + 1 - pair, hm),
+        line=lambda k: (2 * ((line + k) % lines) + pair, hm),
+        mine=hm,
+        other=2 * (1 - across) + core,
+        sib_mine=2 * across + 1 - core,
+        sib_other=2 * (1 - across) + 1 - core,
+        pair=pair, line_index=line, lines=lines, dp=dp, core=core,
+    )
+
+
+def meet(who):
+    barrier = pltpu.get_barrier_semaphore()
+    for name in ("sib", "xn", "dg", "yn"):
+        pl.semaphore_signal(barrier, inc=1, device_id=who[name], device_id_type=MESH)
+
+    def greet(k, carry):
+        pl.semaphore_signal(barrier, inc=1, device_id=who["line"](k), device_id_type=MESH)
+        return carry
+
+    lax.fori_loop(1, who["lines"], greet, 0)
+    pl.semaphore_wait(barrier, 4 + who["lines"] - 1)
+
+
+def push(src, dst, send, recv, to):
+    return pltpu.make_async_remote_copy(
+        src_ref=src, dst_ref=dst, send_sem=send, recv_sem=recv, device_id=to, device_id_type=MESH
+    )
+
+
+def tail_kernel(
+    dp_n, units,
+    grad_t_in, gn_in, rows_out_in, normed_t_in, lpz_in, rows_z_in, lpx_in, rows_x_in, lpbd_in, rows_bd_in, normed_in,
+    tokens, acc_x, acc_bc, acc_s,
+    block_out, in_share, row_sums, g_x, g_z, g_out, g_bc, small_out,
+    sib_send, sib_recv, x_send, x_recv, part, held,
+    y_send, y_recv, z_send, z_recv, g_own, yb_send, yb_recv, zb_send, zb_recv, gb_own, bh_send, bh_recv,
+    bx_send, bx_recv, bs_recv, h_send, h_recv, sy_send, sy_recv, sz_send, sz_recv, dy_send, dy_recv, dz_send, dz_recv,
+    grad_t, gn, rows_out, normed_t, lpz, rows_z, lpx, rows_x, lpbd, rows_bd, normed,
+    s_in, s_sib, r_sib, s_x, r_x, s_y, r_y, s_z, r_z, s_m, r_m, s_sl, r_sl,
+):
+    loads = [
+        pltpu.make_async_copy(src, dst, s_in.at[i])
+        for i, (src, dst) in enumerate((
+            (grad_t_in, grad_t), (gn_in, gn), (rows_out_in, rows_out), (normed_t_in, normed_t), (lpz_in, lpz),
+            (rows_z_in, rows_z), (lpx_in, lpx), (rows_x_in, rows_x), (lpbd_in, lpbd), (rows_bd_in, rows_bd),
+            (normed_in, normed),
+        ))
+    ]
+    for load in loads:
+        load.start()
+    who = peers(dp_n)
+    meet(who)
+    count = normed.shape[0]
+    width = normed.shape[1]
+    inner = lpx.shape[1]
+    bc = acc_bc.shape[1]
+    quarter = width // 4
+    span = count // units
+    block = width // dp_n
+    lines = who["lines"]
+    heads = acc_s.shape[0] // 2
+    taps_rows = acc_x.shape[0]
+
+    def copy_sib(u):
+        return push(sib_send.at[u], sib_recv.at[u], s_sib.at[u], r_sib.at[u], who["sib"])
+
+    def copy_x(u):
+        return push(x_send.at[u], x_recv.at[u], s_x.at[u], r_x.at[u], who["xn"])
+
+    def product(u, q):
+        cols = pl.ds(pl.multiple_of(q * quarter, quarter), quarter)
+        if u < units:
+            return nt(gn[u * span : (u + 1) * span, :], rows_out[cols, :])
+        at = slice((u - units) * span, (u - units + 1) * span)
+        return nt(lpx[at, :], rows_x[cols, :]) + nt(lpz[at, :], rows_z[cols, :]) + nt(lpbd[at, :], rows_bd[cols, :])
+
+    def head_a(u):
+        for k, q in enumerate(("sib_mine", "sib_other", "mine", "other")):
+            p = product(u, who[q])
+            if u >= units:
+                at = slice((u - units) * span, (u - units + 1) * span)
+                cols = pl.ds(pl.multiple_of(who[q] * quarter, quarter), quarter)
+                inner_p = p * normed[at, cols].astype(F32)
+                h_send[0:1, cols] += jnp.sum(inner_p, axis=0, keepdims=True)
+                first = (u - units) * span
+                lanes = slice(first % width, first % width + span)
+                h_send[2 + first // width : 3 + first // width, lanes] += nt(
+                    jnp.ones((8, quarter), BF), inner_p.astype(BF)
+                )[0:1]
+            if k < 2:
+                sib_send[u, k] = p.astype(BF)
+            else:
+                part[u % 2, k - 2] = p
+        copy_sib(u).start()
+
+    def head_b(u):
+        copy_sib(u).wait()
+        x_send[u] = (part[u % 2, 1] + sib_recv[u, 1].astype(F32)).astype(BF)
+        copy_x(u).start()
+        held[u] = part[u % 2, 0] + sib_recv[u, 0].astype(F32)
+
+    def head_c(u):
+        copy_x(u).wait()
+        total = held[u] + x_recv[u].astype(F32)
+        if u < units:
+            at = slice(u * span, (u + 1) * span)
+            block_out[at, :] = (tokens[at, :].astype(F32) + total).astype(BF)
+        else:
+            in_share[(u - units) * span : (u - units + 1) * span, :] = total
+
+    def rows_of(line, pair):
+        return pl.ds(pl.multiple_of((2 * line + pair) * block, block), block)
+
+    def grad_a(v):
+        left, right = ((grad_t, gn), (normed_t, lpz), (normed_t, lpx))[v // 2]
+        cols = slice((v % 2) * (inner // 2), (v % 2 + 1) * (inner // 2))
+        for side in (0, 1):
+            pair = (1 - who["pair"]) if side == 0 else who["pair"]
+            stacked = jnp.concatenate([left[rows_of(l, pair), :] for l in range(lines)], axis=0)
+            value = nn(stacked, right[:, cols])
+            if side == 0:
+                y_send[v] = value.astype(BF)
+                copy_y(v).start()
+            else:
+                g_own[v] = value
+
+    def copy_y(v):
+        return push(y_send.at[v], y_recv.at[v], s_y.at[v], r_y.at[v], who["yn"])
+
+    def copy_z(v, k):
+        to = (who["line_index"] + k) % lines
+        return push(
+            z_send.at[v, pl.ds(pl.multiple_of(to * block, block), block)],
+            z_recv.at[v, k - 1], s_z.at[v, k - 1], r_z.at[v, k - 1], who["line"](k),
+        )
+
+    def each_line(fn):
+        def step(k, carry):
+            fn(k)
+            return carry
+
+        lax.fori_loop(1, lines, step, 0)
+
+    def own_rows():
+        return pl.ds(pl.multiple_of(who["line_index"] * block, block), block)
+
+    def grad_b(v):
+        copy_y(v).wait()
+        g_own[v] = g_own[v] + y_recv[v].astype(F32)
+        z_send[v] = g_own[v].astype(BF)
+        each_line(lambda k: copy_z(v, k).start())
+
+    def grad_c(v):
+        each_line(lambda k: copy_z(v, k).wait())
+        total = g_own[v, own_rows(), :]
+        for k in range(lines - 1):
+            total = total + z_recv[v, k].astype(F32)
+        cols = slice((v % 2) * (inner // 2), (v % 2 + 1) * (inner // 2))
+        (g_out, g_z, g_x)[v // 2][:, cols] = total
+
+    half = bc // 2
+
+    def copy_bh():
+        return push(bh_send, bh_recv, s_m.at[0], r_m.at[0], who["sib"])
+
+    def copy_yb():
+        return push(yb_send, yb_recv, s_m.at[1], r_m.at[1], who["yn"])
+
+    def copy_zb(k):
+        to = (who["line_index"] + k) % lines
+        return push(
+            zb_send.at[pl.ds(pl.multiple_of(to * block, block), block)],
+            zb_recv.at[k - 1], s_sl.at[0, k - 1], r_sl.at[0, k - 1], who["line"](k),
+        )
+
+    def copy_bx():
+        return push(bx_send, bx_recv, s_m.at[2], r_m.at[2], who["xn"])
+
+    def copy_bs():
+        return push(bx_send, bs_recv, s_m.at[3], r_m.at[3], who["sib"])
+
+    def bc_a():
+        for side in (0, 1):
+            pair = (1 - who["pair"]) if side == 0 else who["pair"]
+            stacked = jnp.concatenate([normed_t[rows_of(l, pair), :] for l in range(lines)], axis=0)
+            value = nn(stacked, lpbd[:, :bc])
+            first = who["core"] == 0
+            lo, hi = value[:, :half], value[:, half:]
+            at = slice(side * lines * block, (side + 1) * lines * block)
+            bh_send[at, :] = jnp.where(first, hi, lo).astype(BF)
+            gb_own[at, :] = jnp.where(first, lo, hi)
+        copy_bh().start()
+
+    def bc_b():
+        copy_bh().wait()
+        rows = lines * block
+        gb_own[...] = gb_own[...] + bh_recv[...].astype(F32)
+        yb_send[...] = gb_own[:rows, :].astype(BF)
+        copy_yb().start()
+
+    def bc_c():
+        rows = lines * block
+        copy_yb().wait()
+        gb_own[rows:, :] = gb_own[rows:, :] + yb_recv[...].astype(F32)
+        zb_send[...] = gb_own[rows:, :].astype(BF)
+        each_line(lambda k: copy_zb(k).start())
+
+    def bc_d():
+        each_line(lambda k: copy_zb(k).wait())
+        at = pl.ds(pl.multiple_of(lines * block + who["line_index"] * block, block), block)
+        total = gb_own[at, :]
+        for k in range(lines - 1):
+            total = total + zb_recv[k].astype(F32)
+        bx_send[...] = total
+        copy_bx().start()
+
+    def bc_e():
+        copy_bx().wait()
+        bx_send[...] = bx_send[...] + bx_recv[...]
+        copy_bs().start()
+
+    def bc_f():
+        copy_bs().wait()
+        mine, theirs = bx_send[...], bs_recv[...]
+        first = who["core"] == 0
+        g_bc[:, :half] = jnp.where(first, mine, theirs)
+        g_bc[:, half:] = jnp.where(first, theirs, mine)
+
+    three = (("sib", 4), ("xn", 5), ("dg", 6))
+    taps = width // bc
+    token_rows = count // width
+
+    def copy_h(k):
+        name, sem = three[k]
+        return push(h_send, h_recv.at[k], s_m.at[sem], r_m.at[sem], who[name])
+
+    def small_a():
+        for k in range(taps):
+            h_send[1:2, k * bc : (k + 1) * bc] = acc_bc[k : k + 1, :]
+        for k in range(3):
+            copy_h(k).start()
+
+    def copy_sy():
+        return push(sy_send, sy_recv, s_m.at[7], r_m.at[7], who["yn"])
+
+    def copy_dy():
+        return push(dy_send, dy_recv, s_m.at[8], r_m.at[8], who["yn"])
+
+    def copy_sz(k):
+        return push(sz_send, sz_recv.at[k - 1], s_sl.at[1, k - 1], r_sl.at[1, k - 1], who["line"](k))
+
+    def copy_dz(k):
+        return push(dz_send, dz_recv.at[k - 1], s_sl.at[2, k - 1], r_sl.at[2, k - 1], who["line"](k))
+
+    def dt_a():
+        dy_send[...] = tn(lpbd[:, bc:], normed[...])[0:16, :].astype(BF)
+        copy_dy().start()
+
+    def dt_b():
+        copy_dy().wait()
+        dz_send[...] = (dy_send[...].astype(F32) + dy_recv[...].astype(F32)).astype(BF)
+        each_line(lambda k: copy_dz(k).start())
+
+    def dt_c():
+        each_line(lambda k: copy_dz(k).wait())
+        total = dz_send[...].astype(F32)
+        for k in range(lines - 1):
+            total = total + dz_recv[k].astype(F32)
+        small_out[8:24, :] = total
+
+    def small_b():
+        for k in range(3):
+            copy_h(k).wait()
+        over_heads = h_send[...] + h_recv[0] + h_recv[1] + h_recv[2]
+        row_sums[...] = over_heads[2 : 2 + token_rows, :]
+        sy_send[...] = jnp.zeros_like(sy_send)
+        sy_send[0:2, :] = over_heads[0:2, :]
+        per = width // inner
+        for k in range(taps + 2):
+            sy_send[2 + k // per : 3 + k // per, (k % per) * inner : (k % per + 1) * inner] = acc_x[k : k + 1, :]
+        lanes = acc_s.shape[1]
+        at = 2 + -(-(taps + 2) // per)
+        fit = width // lanes
+        for k in range(2 * heads):
+            sy_send[at + k // fit : at + k // fit + 1, (k % fit) * lanes : (k % fit + 1) * lanes] = acc_s[k : k + 1, :]
+        copy_sy().start()
+
+    def small_c():
+        copy_sy().wait()
+        sz_send[...] = sy_send[...] + sy_recv[...]
+        each_line(lambda k: copy_sz(k).start())
+
+    def small_d():
+        each_line(lambda k: copy_sz(k).wait())
+        total = sz_send[...]
+        for k in range(lines - 1):
+            total = total + sz_recv[k]
+        small_out[0:8, :] = total
+
+    h_send[...] = jnp.zeros_like(h_send)
+
+    def seq(*steps):
+        for fn, *args in steps:
+            fn(*args)
+
+    assert units == 4
+
+    def load(*which):
+        for i in which:
+            loads[i].wait()
+
+    load(0, 1)
+    seq((grad_a, 0), (grad_a, 1))
+    load(2)
+    seq((head_a, 0), (head_a, 1), (head_b, 0), (head_a, 2), (head_b, 1), (head_a, 3), (head_b, 2))
+    load(3, 8)
+    seq((bc_a,), (head_b, 3))
+    load(4)
+    seq((grad_a, 2), (bc_b,), (grad_a, 3))
+    load(5, 6, 7, 9, 10)
+    seq((grad_b, 0), (head_a, 4), (dt_a,), (grad_b, 1), (grad_a, 4), (head_b, 4), (head_a, 5), (bc_c,), (head_b, 5))
+    seq((grad_a, 5), (head_a, 6), (grad_b, 2), (head_b, 6), (head_a, 7), (small_a,), (grad_b, 3), (head_b, 7))
+    seq((dt_b,), (small_b,), (head_c, 0), (head_c, 1), (head_c, 2), (head_c, 3), (bc_d,), (grad_c, 0), (grad_c, 1))
+    seq((grad_b, 4), (small_c,), (grad_b, 5), (dt_c,), (bc_e,), (head_c, 4), (head_c, 5), (grad_c, 2), (grad_c, 3))
+    seq((small_d,), (head_c, 6), (grad_c, 4), (bc_f,), (head_c, 7), (grad_c, 5))
+
+
+def tail(dp_n, units, normed_t, normed, grad_t, gn, lpx, lpz, lpbd, rows_x, rows_z, rows_bd, rows_out, tokens, acc_x, acc_bc, acc_s):
+    count, width = normed.shape
+    inner = lpx.shape[1]
+    bc = acc_bc.shape[1]
+    quarter = width // 4
+    span = count // units
+    block = width // dp_n
+    lines = dp_n // 2
+    half_rows = lines * block
+    more = max(lines - 1, 1)
+    vm = pltpu.VMEM
+    dma = pltpu.SemaphoreType.DMA
+    operands = (
+        grad_t, gn, rows_out, normed_t, lpz, rows_z, lpx, rows_x, lpbd, rows_bd, normed, tokens, acc_x, acc_bc, acc_s,
+    )
+    sds = jax.ShapeDtypeStruct
+    spec = pl.BlockSpec(memory_space=pltpu.VMEM)
+    return pl.pallas_call(
+        functools.partial(tail_kernel, dp_n, units),
+        out_shape=[
+            sds((count, quarter), BF), sds((count, quarter), F32), sds((count // width, width), F32),
+            sds((block, inner), F32), sds((block, inner), F32), sds((block, inner), F32), sds((block, bc), F32),
+            sds((24, width), F32),
+        ],
+        in_specs=[pl.BlockSpec(memory_space=pl.ANY)] * 11 + [spec] * 4,
+        out_specs=[spec] * 8,
+        scratch_shapes=[
+            vm((2 * units, 2, span, quarter), BF), vm((2 * units, 2, span, quarter), BF),
+            vm((2 * units, span, quarter), BF), vm((2 * units, span, quarter), BF),
+            vm((2, 2, span, quarter), F32), vm((2 * units, span, quarter), F32),
+            vm((6, half_rows, inner // 2), BF), vm((6, half_rows, inner // 2), BF),
+            vm((6, half_rows, inner // 2), BF), vm((6, more, block, inner // 2), BF),
+            vm((6, half_rows, inner // 2), F32),
+            vm((half_rows, bc // 2), BF), vm((half_rows, bc // 2), BF),
+            vm((half_rows, bc // 2), BF), vm((more, block, bc // 2), BF),
+            vm((2 * half_rows, bc // 2), F32),
+            vm((2 * half_rows, bc // 2), BF), vm((2 * half_rows, bc // 2), BF),
+            vm((block, bc // 2), F32), vm((block, bc // 2), F32), vm((block, bc // 2), F32),
+            vm((8, width), F32), vm((3, 8, width), F32),
+            vm((8, width), F32), vm((8, width), F32), vm((8, width), F32), vm((more, 8, width), F32),
+            vm((16, width), BF), vm((16, width), BF), vm((16, width), BF), vm((more, 16, width), BF),
+        ]
+        + [vm(a.shape, a.dtype) for a in operands[:11]]
+        + [
+            dma((11,)), dma((2 * units,)), dma((2 * units,)), dma((2 * units,)), dma((2 * units,)),
+            dma((6,)), dma((6,)), dma((6, more)), dma((6, more)), dma((9,)), dma((9,)),
+            dma((3, more)), dma((3, more)),
+        ],
+        compiler_params=pltpu.CompilerParams(
+            collective_id=1, has_side_effects=True, vmem_limit_bytes=62 * 2**20
+        ),
+        name="tail",
+    )(*operands)
+def shares(ref_in, block_of, dp_n, width, send, recv, who):
+    rows = ref_in.shape[0]
+    lines = who["lines"]
+
+    def at(dp):
+        return block_of.at[pl.ds(pl.multiple_of(dp * rows, rows), rows), width]
+
+    def own():
+        return push(ref_in.at[:, width], at(who["dp"]), send.at[0], recv.at[0], who["yn"])
+
+    def along(k):
+        return push(ref_in.at[:, width], at(who["dp"]), send.at[k], recv.at[k], who["line"](k))
+
+    def onward(k):
+        source = at(2 * ((who["line_index"] - k + lines) % lines) + who["pair"])
+        return push(source, source, send.at[lines - 1 + k], recv.at[lines - 1 + k], who["yn"])
+
+    return own, along, onward
+
+
+def loop_line(lines, fn):
+    def step(k, carry):
+        fn(k)
+        return carry
+
+    lax.fori_loop(1, lines, step, 0)
+
+
+def front_kernel(
+    dp_n, units,
+    tokens, w_bd, w_x, gain,
+    px_out, pbd_out, normed_out, normed_t_out, q_out, rows_x, rows_bd,
+    tok, wx, wbd, px, pbd, normed, normed_t, q,
+    s_loc, s_sib, r_sib, s_x, r_x, s_f, r_f, s_b, r_b, s_w, r_w, s_out,
+):
+    who = peers(dp_n)
+    count, quarter = tokens.shape
+    width = 4 * quarter
+    span = count // units
+    lines = who["lines"]
+    block = w_x.shape[0]
+    here = pl.ds(pl.multiple_of(who["dp"] * block, block), block)
+    local = [
+        pltpu.make_async_copy(tokens, tok.at[who["mine"]], s_loc.at[0]),
+        pltpu.make_async_copy(w_bd, wbd.at[here], s_loc.at[1]),
+        pltpu.make_async_copy(w_x, wx.at[here], s_loc.at[2]),
+    ]
+    for copy in local:
+        copy.start()
+    meet(who)
+
+    def rows(s):
+        return pl.ds(s * span, span)
+
+    def to_x(s):
+        return push(tokens.at[rows(s)], tok.at[who["mine"], rows(s)], s_x.at[s], r_x.at[s], who["xn"])
+
+    def to_sib():
+        return push(tokens, tok.at[who["mine"]], s_sib.at[0], r_sib.at[0], who["sib"])
+
+    def forward(s):
+        here = tok.at[who["other"], rows(s)]
+        return push(here, here, s_f.at[s], r_f.at[s], who["sib"])
+
+    every = slice(None)
+    bd_own, bd_along, bd_onward = shares(w_bd, wbd, dp_n, every, s_b, r_b, who)
+    x_own, x_along, x_onward = shares(w_x, wx, dp_n, every, s_w, r_w, who)
+    to_x(0).start()
+    loop_line(lines, lambda k: bd_along(k).start())
+    bd_own().start()
+    for s in range(1, units):
+        to_x(s).start()
+    to_sib().start()
+    loop_line(lines, lambda k: x_along(k).start())
+    x_own().start()
+
+    def pass_on(along, onward, k):
+        along(k).wait()
+        onward(k).start()
+
+    def norm(s):
+        at = slice(s * span, (s + 1) * span)
+        parts = [tok[h, at, :].astype(F32) for h in range(4)]
+        total = sum(jnp.sum(p * p, axis=1, keepdims=True) for p in parts)
+        inv = lax.rsqrt(total / width + EPS)
+        q[at, :] = jnp.broadcast_to(inv, (span, q.shape[1]))
+        for h in range(4):
+            cols = slice(h * quarter, (h + 1) * quarter)
+            value = (parts[h] * inv * gain[:, cols]).astype(BF)
+            normed[at, cols] = value
+            normed_t[cols, at] = jnp.transpose(value)
+
+    def outward(ref, out, i, at):
+        return pltpu.make_async_copy(ref.at[at], out.at[at], s_out.at[i])
+
+    def send_norm(s):
+        at = (slice(s * span, (s + 1) * span),)
+        copies = [
+            outward(normed, normed_out, 3 * s, at),
+            outward(normed_t, normed_t_out, 3 * s + 1, (slice(None),) + at),
+            outward(q, q_out, 3 * s + 2, at),
+        ]
+        return copies
+
+    def project(s):
+        at = slice(s * span, (s + 1) * span)
+        pbd[at, :] = nn(normed[at, :], wbd[...])
+        px[at, :] = nn(normed[at, :], wx[...])
+
+    def send_proj(s):
+        at = (slice(s * span, (s + 1) * span),)
+        base = 3 * units + 2 * s
+        return [outward(px, px_out, base, at), outward(pbd, pbd_out, base + 1, at)]
+
+    outs = []
+
+    def go(copies):
+        for copy in copies:
+            copy.start()
+        outs.extend(copies)
+
+    local[0].wait()
+    to_x(0).wait()
+    forward(0).start()
+    loop_line(lines, lambda k: pass_on(bd_along, bd_onward, k))
+    to_sib().wait()
+    for s in range(units):
+        forward(s).wait()
+        norm(s)
+        go(send_norm(s))
+        if s + 1 < units:
+            to_x(s + 1).wait()
+            forward(s + 1).start()
+        if s == 1:
+            bd_own().wait()
+            loop_line(lines, lambda k: bd_onward(k).wait())
+            local[1].wait()
+            copy = pltpu.make_async_copy(wbd, rows_bd, s_out.at[5 * units])
+            go([copy])
+        if s == units - 2:
+            loop_line(lines, lambda k: pass_on(x_along, x_onward, k))
+    x_own().wait()
+    loop_line(lines, lambda k: x_onward(k).wait())
+    local[2].wait()
+    go([pltpu.make_async_copy(wx, rows_x, s_out.at[5 * units + 1])])
+    for s in range(units):
+        project(s)
+        go(send_proj(s))
+    for copy in outs:
+        copy.wait()
+
+
+def front(dp_n, units, tokens, w_bd, w_x, gain):
+    count, quarter = tokens.shape
+    width = 4 * quarter
+    inner, wide = w_x.shape[1], w_bd.shape[1]
+    vm, dma, sds = pltpu.VMEM, pltpu.SemaphoreType.DMA, jax.ShapeDtypeStruct
+    hbm = pl.BlockSpec(memory_space=pl.ANY)
+    lines = dp_n // 2
+    ways = 2 * lines - 1
+    outs = [
+        sds((count, inner), F32), sds((count, wide), F32), sds((count, width), BF), sds((width, count), BF),
+        sds((count, 128), F32), sds((width, inner), BF), sds((width, wide), BF),
+    ]
+    return pl.pallas_call(
+        functools.partial(front_kernel, dp_n, units),
+        out_shape=outs,
+        in_specs=[hbm] * 3 + [pl.BlockSpec(memory_space=pltpu.VMEM)],
+        out_specs=[hbm] * 7,
+        scratch_shapes=[
+            vm((4, count, quarter), BF), vm((width, inner), BF), vm((width, wide), BF),
+            vm((count, inner), F32), vm((count, wide), F32), vm((count, width), BF), vm((width, count), BF),
+            vm((count, 128), F32),
+            dma((3,)), dma((1,)), dma((1,)), dma((units,)), dma((units,)), dma((units,)), dma((units,)),
+            dma((ways,)), dma((ways,)), dma((ways,)), dma((ways,)), dma((5 * units + 2,)),
+        ],
+        compiler_params=pltpu.CompilerParams(
+            collective_id=2, has_side_effects=True, vmem_limit_bytes=58 * 2**20
+        ),
+        name="front",
+    )(tokens, w_bd, w_x, gain)
 
 
 def body(
@@ -432,7 +1002,9 @@
     gate_gain, w_out,
 ):
     heads_n = lax.axis_size("heads")
+    dp_n = lax.axis_size("dp")
     head_index = lax.axis_index("heads")
+    dp_index = lax.axis_index("dp")
     count, columns = tokens.shape
     width = columns * heads_n
     blocks = starts.shape[0]
@@ -441,16 +1013,11 @@
     heads = w_dt.shape[1]
     bc = w_bc.shape[1]
     total_inner = inner * heads_n
-    dt_pad = jnp.pad(w_dt, ((0, 0), (0, chunk - heads)))
-    packed = jnp.concatenate([w_x, w_z, w_bc, dt_pad, w_out], axis=1)
-    rows_all = lax.all_gather(packed, "dp", axis=0, tiled=True)
-    rows_x, rows_z = rows_all[:, :inner], rows_all[:, inner : 2 * inner]
-    rows_bd, rows_out = rows_all[:, 2 * inner : 2 * inner + bc + chunk], rows_all[:, 2 * inner + bc + chunk :]
-    whole = lax.all_gather(tokens, "heads", axis=1, tiled=True).astype(F32)
-    inverse = lax.rsqrt(jnp.mean(whole * whole, axis=-1, keepdims=True) + EPS)
-    normed = (whole * inverse * norm_gain).astype(BF)
-    px, pz, pbd = nn(normed, rows_x), nn(normed, rows_z), nn(normed, rows_bd)
+    w_bd = jnp.concatenate([w_bc, jnp.pad(w_dt, ((0, 0), (0, chunk - heads)))], axis=1)
+    px, pbd, normed, normed_t, q_wide, rows_x, rows_bd = front(dp_n, 4, tokens, w_bd, w_x, norm_gain[None, :])
+    rows_z, rows_out = (lax.all_gather(w, "dp", axis=0, tiled=True) for w in (w_z, w_out))
     y, sin = scan_forward(px, pbd, conv_x, conv_bc, dt_bias, a_log, skip, starts, fill)
+    pz = nn(normed, rows_z)
     g_full = lax.all_gather(cotangent, "heads", axis=1, tiled=True)
     ggn = nn(g_full, rows_out)
     gated = y * jax.nn.silu(pz)
@@ -461,43 +1028,41 @@
     rows = jnp.pad(jnp.transpose(both.reshape(2, blocks, chunk), (1, 0, 2)), ((0, 0), (0, 6), (0, 0)))
     gate_inverse = lax.rsqrt(both[0] / total_inner + EPS)[:, None]
     gated_normed = (gated * gate_inverse * gate_gain).astype(BF)
-    partial_out = nt(gated_normed, rows_out)
-    out_share = lax.psum_scatter(partial_out, "heads", scatter_dimension=1, tiled=True)
-    block_out = (tokens.astype(F32) + out_share).astype(BF)
     lpx, lpz, lpbd, acc_x, acc_bc, acc_s = scan_backward(
         ggn, y, pz, px, pbd, sin, rows, gate_gain, conv_x, conv_bc, dt_bias, a_log, skip, starts, fill,
         total_inner,
     )
-    partial_in = nt(lpx, rows_x) + nt(lpz, rows_z) + nt(lpbd, rows_bd)
-    in_share = lax.psum_scatter(partial_in, "heads", scatter_dimension=1, tiled=True)
+    block_out, in_share, row_sums, grad_w_x, grad_w_z, grad_w_out, grad_w_bc, small = tail(
+        dp_n, 4, normed_t, normed, g_full.T, gated_normed, lpx, lpz, lpbd, rows_x, rows_z, rows_bd, rows_out,
+        tokens, acc_x, acc_bc, acc_s,
+    )
     own = tokens.astype(F32)
     own_gain = lax.dynamic_slice_in_dim(norm_gain, head_index * columns, columns, 0)
-    gain_part = jnp.sum(in_share * own * inverse, axis=0)
-    norm_dots = lax.psum(jnp.sum(in_share * own_gain * own, axis=-1), "heads")
+    inverse = q_wide[:, 0:1]
     grad_tokens = (
         cotangent.astype(F32)
         + inverse * own_gain * in_share
-        - own * inverse**3 * (norm_dots / width)[:, None]
-    )
-    grads = jnp.concatenate(
-        [tn(normed, lpx), tn(normed, lpz), tn(normed, lpbd), tn(g_full, gated_normed)], axis=1
-    )
-    grads = lax.psum_scatter(grads, "dp", scatter_dimension=0, tiled=True)
-    grad_w_x, grad_w_z = grads[:, :inner], grads[:, inner : 2 * inner]
-    grad_bd = grads[:, 2 * inner : 2 * inner + bc + chunk]
-    grad_w_bc = lax.psum(grad_bd[:, :bc], "heads")
-    grad_w_dt = grad_bd[:, bc : bc + heads]
-    grad_w_out = grads[:, 2 * inner + bc + chunk :]
+        - own * (inverse * inverse) * (row_sums.reshape(-1) / width)[:, None]
+    )
+    return (block_out, grad_tokens) + outputs(
+        small, dp_index, head_index, own_gain, conv_x, bc, heads, inner, width // dp_n, chunk,
+        grad_w_x, grad_w_z, grad_w_bc, grad_w_out,
+    )
+
+
+def outputs(small, dp_index, head_index, own_gain, conv_x, bc, heads, inner, block, chunk, g_x, g_z, g_bc, g_out):
     taps = conv_x.shape[0]
-    small = jnp.concatenate([acc_x.reshape(-1), jnp.sum(acc_s, axis=1), gain_part])
-    small = lax.psum(small, "dp")
-    grad_conv_bc = lax.psum(acc_bc[:taps], ("dp", "heads"))
-    acc_x = small[: acc_x.size].reshape(acc_x.shape)
-    acc_s = small[acc_x.size : acc_x.size + 2 * heads]
+    width = small.shape[1]
+    columns = own_gain.shape[0]
+    grad_w_dt = lax.dynamic_slice_in_dim(small[8 : 8 + heads], dp_index * block, block, 1).T
+    gain_sum = lax.dynamic_slice_in_dim(small[0], head_index * columns, columns, 0)
+    per = width // inner
+    scans = small[2 : 2 + -(-(taps + 2) // per)].reshape(-1, inner)
+    at = 2 + -(-(taps + 2) // per)
+    lanes = jnp.sum(small[at:8].reshape(-1, chunk)[: 2 * heads], axis=1)
     return (
-        block_out, grad_tokens, small[acc_x.size + 2 * heads :], grad_w_x, grad_w_z, grad_w_dt, grad_w_bc,
-        acc_x[:taps], grad_conv_bc, acc_s[:heads], acc_s[heads:],
-        jnp.sum(acc_x[taps + 1].reshape(heads, HD), axis=1), acc_x[taps], grad_w_out,
+        gain_sum / own_gain, g_x, g_z, grad_w_dt, g_bc, scans[:taps], small[1].reshape(taps, bc), lanes[:heads],
+        lanes[heads:], jnp.sum(scans[taps + 1].reshape(heads, HD), axis=1), scans[taps], g_out,
     )
 
 

time: 579 us -> 315 us (0.54)
  waiting for transfers between devices: 293 us -> 44.5 us
  Pallas kernels: 62.5 us -> 187 us
  blocking collectives: 93.3 us -> 10.7 us
  matrix products: 76.6 us -> 18.6 us
    reduce_scatter x3 -> x0, waiting for transfers between devices: 190 us -> none  [the longest x1 124 us: body(): grads = lax.psum_scatter(grads, 'dp', scatter_dimension=0, tiled=True)]
    pallas_call x0 -> x2, Pallas kernels: none -> 125 us  [the longest x1 73.9 us: tail(): pl.pallas_call(functools.partial(tail_kernel, dp_n, units), out_shape=[sd...]
    all_gather x2, waiting for transfers between devices: 101 us -> 7.68 us  [body(): lax.all_gather(w, 'dp', axis=0, tiled=True)]
    psum x3 -> x0, blocking collectives: 83 us -> none  [the longest x1 39.4 us: body(): grad_conv_bc = lax.psum(acc_bc[:taps], ('dp', 'heads'))]
    dot_general x8 -> x0, matrix products: 47 us -> none  [the longest x4 35 us: nt(): lax.dot_general(a, b, (((1,), (1,)), ((), ())), preferred_element_type=F32)]
    all_gather x1, waiting for transfers between devices: 0.01 us -> 35.4 us  [body(): g_full = lax.all_gather(cotangent, 'heads', axis=1, tiled=True)]
    dot_general x4 -> x2, matrix products: 29.5 us -> 18.6 us  [nn(): lax.dot_general(a, b, (((1,), (0,)), ((), ())), preferred_element_type=F32)]
    unnamed x70 -> x60, local copies, waits for them, and re-layouts: 11.3 us -> 14.4 us
  transfers between devices with their start and end apart: 7 -> 3, of which waited for: 5 -> 2; matrix products, arithmetic and copies ran while one was open for 13% -> 4% of each run, Pallas kernels for 3% -> 23%
where the time goes in v2:
time: 315 us; the launch traced here: 309 us
  Pallas kernels  187 us (59%)
  waiting for transfers between devices  44.5 us (14%)
  local copies, waits for them, and re-layouts  21.7 us (7%)
  matrix products  18.6 us (6%)
  between operations  14.5 us (5%)
  other arithmetic  12.2 us (4%)
  blocking collectives  10.7 us (3%)
    pallas_call x1, Pallas kernels, tail(): pl.pallas_call(functools.partial(tail_kernel, dp_n, units), out_shape=[sd...  73.9 us
    pallas_call x1, Pallas kernels, front(): pl.pallas_call(functools.partial(front_kernel, dp_n, units), out_shape=ou...  50.8 us
    pallas_call x1, Pallas kernels, scan_backward(): pl.pallas_call(kernel, grid_spec=pltpu.PrefetchScalarGridSpec(num_scalar_...  42.2 us
    all_gather x1, waiting for transfers between devices, body(): g_full = lax.all_gather(cotangent, 'heads', axis=1, tiled=True)  35.4 us
    pallas_call x1, Pallas kernels, scan_forward(): pl.pallas_call(functools.partial(scan_fwd_kernel, heads), grid_spec=pltpu...  19.8 us
    dot_general x2, matrix products, nn(): lax.dot_general(a, b, (((1,), (0,)), ((), ())), preferred_element_type=F32)  18.6 us
    unnamed x60, local copies, waits for them, and re-layouts  14.4 us
    psum x1, blocking collectives, body(): both = lax.psum(both, 'heads')  10.7 us
  transfers between devices with their start and end apart: 3, of which 2 were waited for; matrix products, arithmetic and copies ran while one was open for 4% of the time, Pallas kernels for 23%

profile of v2, /device:TPU:0, one launch (start us, length us, event | category | flops | bytes accessed | tf_op | source)
XLA Modules:
  0.0 308.9 jit_solution(12767341416293772965)
XLA Ops:
  7.2 0.0 copy-start.3
  7.2 0.0 copy-start.8
  7.2 0.0 copy-start.25
  7.2 0.0 copy-start.11
  7.2 0.0 copy-start.9
  7.2 0.0 copy-start.16
  7.3 0.0 all-gather.6.cloned.1.call-start
  7.3 0.7 all-gather.6.cloned.1.call-update
  8.0 0.0 all-gather.8.cloned.1.call-start
  8.0 0.7 all-gather.8.cloned.1.call-update
  8.7 0.0 all-gather.4.cloned.1.call-start
  8.8 2.3 copy.44
  11.1 0.0 all-gather.4.cloned.1.call-update
  11.1 0.7 broadcast_in_dim.13
  11.8 0.1 broadcast_in_dim_reshape.4.skip.refs_16_
  11.9 0.8 copy.45
  12.7 1.5 fusion.1.w_bd
  14.2 50.8 %front.1 = (f32[2048,512]{1,0:T(8,128)}, f32[2048,384]{1,0:T(8,128)}, bf16[2048,1024]{1,0:T(8,128)(2,1)}, bf16[1024,2048]{1,0:T(8,128)(2,1)}, f32[2048,128]{1,0:...) custom-call(bf16[2048,256]{1,0:T(8,128)(2,1)} %tokens.3, bf16[128,384]{1,0:T(8,128)(2,1)} %fusion.1.w_bd, ...), custom_call_target="tpu_custom_call" | custom-call | tf_op jit(solution)/shard_map/front/pallas_call | solution.py:981
  65.0 0.0 copy-done.25
  65.0 0.1 broadcast_in_dim.12.rate.refs_15_
  65.1 0.1 broadcast_in_dim.11.bias.refs_14_
  65.2 0.0 copy-done.3
  65.2 1.9 copy-done
  67.1 19.8 %scan_forward.1 = (f32[2048,512]{1,0:T(8,128)}, bf16[16,128,512]{2,1,0:T(8,128)(2,1)S(1)}) custom-call(s32[16]{0:T(128)S(1)} %copy-done.15, s32[16]{0:T(128)S(1)} %copy-done.16, f32[2048,512]{1,0:T(8,128)} %get-tuple-element.37.px.refs_5_.refs_6_, f32[2048,384]{1,0:T(8,128)S(1)} %copy-done, f32[4,512]{1,0:T(4,128)S(1)} %copy-done.9, ...), custom_call_target="tpu_custom_call" | custom-call | tf_op jit(solution)/shard_map/scan_forward/pallas_call | solution.py:177
  86.9 1.3 copy-done.1
  88.2 0.6 slice_reduce_fusion
  88.8 0.0 all-gather.6.cloned.1.call-done.rows_z_in
  88.9 0.0 copy-start.14
  88.9 6.8 %fusion.8.refs_4_ = f32[2048,512]{1,0:T(8,128)} fusion(bf16[2048,1024]{1,0:T(8,128)(2,1)} %get-tuple-element.40.normed_in, bf16[1024,512]{1,0:T(8,128)(2,1)} %all-gather.6.cloned.1.call-done.rows_z_in), kind=kOutput, calls=%fused_computation.25 | convolution fusion | flops 2147483648 | bytes 9437184 | tf_op jit(solution)/shard_map/dot_general | solution.py:19
  95.7 7.7 %all-gather.8.cloned.1.call-done.rows_out_in = bf16[1024,512]{1,0:T(8,128)(2,1)} async-done(((bf16[128,512]{1,0:T(8,128)(2,1)}), bf16[1024,512]{1,0:T(8,128)(2,1)}) %all-gather.8.cloned.1.call-update) | async-done | bytes 1048592 | tf_op jit(solution)/shard_map/all_gather | solution.py:1018
  103.3 35.4 %all-gather.4.cloned.1.call-done = bf16[2048,1024]{0,1:T(8,128)(2,1)} async-done(((bf16[2048,256]{0,1:T(8,128)(2,1)}), bf16[2048,1024]{0,1:T(8,128)(2,1)}) %all-gather.4.cloned.1.call-update) | async-done | bytes 4194320 | tf_op jit(solution)/shard_map/all_gather | solution.py:1021
  138.7 11.8 %multiply_reduce_fusion.1 = (f32[2048]{0:T(1024)S(1)}, f32[2048]{0:T(1024)S(1)}, f32[2048,512]{1,0:T(8,128)}, f32[2048,512]{1,0:T(8,128)}) fusion(f32[512]{0:T(512)S(1)} %copy-done.14, f32[2048,512]{1,0:T(8,128)} %get-tuple-element.39.refs_3_, f32[2048,512]{1,0:T(8,128)} %fusion.8.refs_4_, bf16[2048,1024]{0,1:T(8,128)(2,1)} %all-gather.4.cloned.1.call-done, ...), kind=kOutput, calls=%fused_computation.2 | convolution fusion | flops 2157965312 | bytes 22038528 | tf_op jit(solution)/shard_map/dot_general | solution.py:19
  150.6 10.7 %psum.7 = f32[2,2048]{1,0:T(2,128)S(1)} all-reduce(f32[2,2048]{1,0:T(2,128)S(1)} %pad_maximum_fusion), channel_id=1, replica_groups=mesh['dp'=8,'heads'=4] {'heads'}, use_global_device_ids=true, to_apply=%region_2.3 | all-reduce | flops 4096 | bytes 32768 | tf_op jit(solution)/shard_map/psum | solution.py:1027
  161.3 3.9 %multiply_convert_fusion.gn_in = bf16[2048,512]{1,0:T(8,128)(2,1)} fusion(f32[2048,512]{1,0:T(8,128)} %get-tuple-element.66, f32[2048]{0:T(1024)S(1)} %bitcast.26, f32[512]{0:T(512)S(1)} %copy-done.14), kind=kLoop, calls=%fused_computation | loop fusion | flops 3145728 | bytes 6301696 | tf_op jit(solution)/shard_map/convert_element_type | solution.py:1030
  165.2 0.0 copy-done.5
  165.2 0.0 copy-done.6
  165.3 0.0 copy-done.7
  165.3 42.2 %scan_backward.1 = (bf16[2048,512]{1,0:T(8,128)(2,1)S(1)}, bf16[2048,512]{1,0:T(8,128)(2,1)}, bf16[2048,384]{1,0:T(8,128)(2,1)S(1)}, f32[8,512]{1,0:T(8,128)S(1)...) custom-call(s32[16]{0:T(128)S(1)} %copy-done.15, s32[16]{0:T(128)S(1)} %copy-done.16, ...), custom_call_target="tpu_custom_call" | custom-call | tf_op jit(solution)/shard_map/scan_backward/pallas_call | solution.py:393
  207.4 1.4 copy-done.2
  208.8 1.2 copy-done.4
  210.0 0.6 copy-done.10
  210.6 0.6 copy-done.12
  211.2 0.6 copy-done.13
  211.8 73.9 %tail.1 = (bf16[2048,256]{1,0:T(8,128)(2,1)}, f32[2048,256]{1,0:T(8,128)}, f32[2,1024]{1,0:T(2,128)}, f32[128,512]{1,0:T(8,128)}, f32[128,512]{1,0:T(8,128)}, /*...) custom-call(bf16[1024,2048]{1,0:T(8,128)(2,1)} %bitcast.23, ...), custom_call_target="tpu_custom_call" | custom-call | tf_op jit(solution)/shard_map/tail/pallas_call | solution.py:781
  285.7 0.9 slice_reduce_fusion.1
  286.6 0.8 slice.56
  287.3 0.8 fusion.5
  288.2 0.8 slice.48
  288.9 0.7 multiply_bitcast_fusion
  289.6 0.6 reshape_squeeze.6
  290.2 1.3 fusion.4
  291.6 0.6 fusion.6
  292.2 0.1 reshape_squeeze.7
  292.2 0.6 reduce_sum.39
  292.9 0.1 reduce_sum.38
  293.0 0.6 fusion.7
  293.6 0.6 slice.50
  294.2 0.6 dynamic-slice_bitcast_fusion
  294.8 3.4 %multiply_subtract_fusion = f32[2048,256]{1,0:T(8,128)} fusion(bf16[2048,256]{1,0:T(8,128)(2,1)S(1)} %copy-done.17, f32[2048,256]{1,0:T(8,128)} %get-tuple-element.53, bf16[2048,256]{1,0:T(8,128)(2,1)} %param.24, f32[2048]{0:T(1024)S(1)} %bitcast.25, f32[2048]{0:T(1024)S(1)} %get-tuple-element.63, f32[256]{0:T(256)S(1)} %get-tuple-element.65, ...), kind=kLoop, calls=%fused_computation.4 | loop fusion | flops 4194304 | bytes 6317056 | tf_op jit(solution)/shard_map/sub | solution.py:1043
  298.2 1.0 copy.61
  299.2 0.7 copy.62
  299.9 0.7 copy.63
  300.6 0.7 copy.64
  301.3 0.7 copy.65
  (41 shorter events, 0.1 us)
Async XLA Ops:
  7.2 58.0 %copy-start.3 = (bf16[128,1536]{1,0:T(8,128)(2,1)S(1)}, bf16[128,1536]{1,0:T(8,128)(2,1)}, u32[]{:S(2)}) copy-start(bf16[128,1536]{1,0:T(8,128)(2,1)} %constant.45.clone.spread.refs_18_) | copy-start | bytes 1179652
  7.2 58.0 %copy-start.8 = (bf16[128,128]{1,0:T(8,128)(2,1)S(1)}, bf16[128,128]{1,0:T(8,128)(2,1)}, u32[]{:S(2)}) copy-start(bf16[128,128]{1,0:T(8,128)(2,1)} %constant.44.clone.upper.refs_17_) | copy-start | bytes 98308
  7.2 57.8 %copy-start.25 = (f32[8]{0:T(128)S(1)}, f32[8]{0:T(128)}, u32[]{:S(2)}) copy-start(f32[8]{0:T(128)} %param.35) | copy-start | bytes 100
  7.2 58.0 %copy-start.11 = (f32[4,256]{1,0:T(4,128)S(1)}, f32[4,256]{1,0:T(4,128)}, u32[]{:S(2)}) copy-start(f32[4,256]{1,0:T(4,128)} %refs_13_.1) | copy-start | bytes 12292
  7.2 57.9 %copy-start.9 = (f32[4,512]{1,0:T(4,128)S(1)}, f32[4,512]{1,0:T(4,128)}, u32[]{:S(2)}) copy-start(f32[4,512]{1,0:T(4,128)} %refs_12_.1) | copy-start | bytes 24580
  7.2 57.9 %copy-start.16 = (s32[16]{0:T(128)S(1)}, s32[16]{0:T(128)}, u32[]{:S(2)}) copy-start(s32[16]{0:T(128)} %refs_1_.1) | copy-start | bytes 196
  7.2 57.9 %copy-start.15 = (s32[16]{0:T(128)S(1)}, s32[16]{0:T(128)}, u32[]{:S(2)}) copy-start(s32[16]{0:T(128)} %refs_0_.1) | copy-start | bytes 196
  7.3 57.8 %copy-start.24 = (f32[8]{0:T(128)S(1)}, f32[8]{0:T(128)}, u32[]{:S(2)}) copy-start(f32[8]{0:T(128)} %param.34) | copy-start | bytes 100
  7.3 81.6 %all-gather.6.cloned.1.call-start = ((), (), s32[]{:S(2)}) async-start(), calls=%async_computation.1 | async-start | bytes 1179648 | tf_op jit(solution)/shard_map/all_gather | solution.py:1018
  8.0 95.3 %all-gather.8.cloned.1.call-start = ((), (), s32[]{:S(2)}) async-start(), calls=%async_computation.2 | async-start | bytes 1179648 | tf_op jit(solution)/shard_map/all_gather | solution.py:1018
  8.7 130.0 %all-gather.4.cloned.1.call-start = ((), (), s32[]{:S(2)}) async-start(), calls=%async_computation | async-start | bytes 5242880 | tf_op jit(solution)/shard_map/all_gather | solution.py:1021
  65.2 1.9 copy-start
  67.1 21.1 %copy-start.19 = (f32[2048,128]{1,0:T(8,128)S(1)}, f32[2048,128]{1,0:T(8,128)}, u32[]{:S(2)}) copy-start(f32[2048,128]{1,0:T(8,128)} %get-tuple-element.52) | copy-start | bytes 3145732
  86.9 1.3 copy-start.1
  88.9 49.9 %copy-start.14 = (f32[512]{0:T(512)S(1)}, f32[512]{0:T(512)}, u32[]{:S(2)}) copy-start(f32[512]{0:T(512)} %param.37) | copy-start | bytes 6148
  150.6 14.7 %copy-start.5 = (bf16[3,512,128]{2,1,0:T(8,128)(2,1)S(1)}, bf16[3,512,128]{2,1,0:T(8,128)(2,1)}, u32[]{:S(2)}) copy-start(bf16[3,512,128]{2,1,0:T(8,128)(2,1)} %constant.46.clone.refs_19_) | copy-start | bytes 1179652
  150.6 14.7 %copy-start.6 = (bf16[1024,128]{1,0:T(8,128)(2,1)S(1)}, bf16[1024,128]{1,0:T(8,128)(2,1)}, u32[]{:S(2)}) copy-start(bf16[1024,128]{1,0:T(8,128)(2,1)} %constant.47.clone.refs_21_) | copy-start | bytes 786436
  150.6 14.7 %copy-start.7 = (bf16[128,512]{1,0:T(8,128)(2,1)S(1)}, bf16[128,512]{1,0:T(8,128)(2,1)}, u32[]{:S(2)}) copy-start(bf16[128,512]{1,0:T(8,128)(2,1)} %constant.48.clone.refs_20_) | copy-start | bytes 393220
  207.4 1.4 copy-start.2
  208.8 1.2 copy-start.4
  210.0 0.6 copy-start.10
  210.6 0.6 copy-start.12
  211.2 0.6 copy-start.13
  211.8 83.0 %copy-start.17 = (bf16[2048,256]{1,0:T(8,128)(2,1)S(1)}, bf16[2048,256]{1,0:T(8,128)(2,1)}, u32[]{:S(2)}) copy-start(bf16[2048,256]{1,0:T(8,128)(2,1)} %tokens.3) | copy-start | bytes 3145732
  285.7 12.5 %copy-start.18 = (bf16[2048,256]{1,0:T(8,128)(2,1)S(1)}, bf16[2048,256]{1,0:T(8,128)(2,1)}, u32[]{:S(2)}) copy-start(bf16[2048,256]{1,0:T(8,128)(2,1)} %get-tuple-element.90) | copy-start | bytes 3145732
  294.8 4.4 %copy-start.22 = (f32[128,512]{1,0:T(8,128)S(1)}, f32[128,512]{1,0:T(8,128)}, u32[]{:S(2)}) copy-start(f32[128,512]{1,0:T(8,128)} %get-tuple-element.93) | copy-start | bytes 786436
  294.8 5.1 %copy-start.21 = (f32[128,512]{1,0:T(8,128)S(1)}, f32[128,512]{1,0:T(8,128)}, u32[]{:S(2)}) copy-start(f32[128,512]{1,0:T(8,128)} %get-tuple-element.94) | copy-start | bytes 786436
  294.8 5.8 %copy-start.23 = (f32[128,256]{1,0:T(8,128)S(1)}, f32[128,256]{1,0:T(8,128)}, u32[]{:S(2)}) copy-start(f32[128,256]{1,0:T(8,128)} %get-tuple-element.96) | copy-start | bytes 393220
  294.8 6.4 %copy-start.20 = (f32[128,512]{1,0:T(8,128)S(1)}, f32[128,512]{1,0:T(8,128)}, u32[]{:S(2)}) copy-start(f32[128,512]{1,0:T(8,128)} %get-tuple-element.103) | copy-start | bytes 786436
Sparse Core Ops, SparseCore 0:
  10.2 51.5 all-gather.5
  64.0 39.3 all-gather.7
  105.5 33.2 all-gather.3

commit v3 on v2

--- a/solution.py
+++ b/solution.py
@@ -80,7 +80,7 @@
 def dt_rows(pdt, bias, rate, fill, heads, upper):
     chunk = pdt.shape[0]
     pre = jnp.transpose(pdt)[:heads] + bias
-    live = (iota2(heads, chunk, 1) < fill).astype(F32)
+    live = (iota2(heads, chunk, 1).astype(F32) < fill).astype(F32)
     dt = softplus(pre) * live
     hi, mid, low = split3(dt * rate)
     stacked = jnp.concatenate([hi, mid, low], axis=0).astype(BF)
@@ -109,14 +109,18 @@
 
 
 def scan_fwd_kernel(
-    heads, starts, fill, px, pbd, convx, convbc, bias, rate, skip, upper, spread,
-    y_out, sin_out, state, extx, extb,
+    heads, dp_n, meta, px, pbd, convx, convbc, bias, rate, skip, upper, spread, cot, w_z, w_out,
+    y_out, sin_out, parts, rows_z, rows_out, state, extx, extb,
+    s_loc, s_sib, r_sib, s_x, r_x, s_f, r_f, s_w, r_w,
 ):
     c = pl.program_id(0)
     chunk, inner = px.shape
     bc = convbc.shape[1]
     ns = bc // 2
-    keep = starts[c] == 0
+    keep = meta[0, 0:1, 0:1] > 0.5
+    finish = gather_beside_scan(
+        dp_n, cot, w_z, w_out, parts, rows_z, rows_out, s_loc, s_sib, r_sib, s_x, r_x, s_f, r_f, s_w, r_w
+    )
 
     @pl.when(c == 0)
     def _():
@@ -130,11 +134,11 @@
     extx[8 : chunk + 8, :] = px[...]
     extb[8 : chunk + 8, :] = pbd[:, :bc]
 
-    n_live = fill[c]
+    n_live = meta[0, 1:2, 0:1]
     u = conv_from(extx, convx[...], chunk, 8)
-    x = u * sigmoid(u) * (iota2(chunk, inner, 0) < n_live).astype(F32)
+    x = u * sigmoid(u) * (iota2(chunk, inner, 0).astype(F32) < n_live).astype(F32)
     ub = conv_from(extb, convbc[...], chunk, 8)
-    act = (ub * sigmoid(ub) * (iota2(chunk, bc, 0) < n_live).astype(F32)).astype(BF)
+    act = (ub * sigmoid(ub) * (iota2(chunk, bc, 0).astype(F32) < n_live).astype(F32)).astype(BF)
     b, cc = act[:, :ns], act[:, ns:]
 
     _, _, dt, run = dt_rows(pbd[:, bc:], bias[...], rate[...], n_live, heads, upper[...])
@@ -159,11 +163,100 @@
     sin_out[0] = enter_b
     y_out[...] = jnp.concatenate(diag, axis=1) + ein_w * nn(cc, enter_b) + skip[...] * x
     state[...] = ein_w[chunk - 1 : chunk, :] * enter + tn(b, (xd * eout_w).astype(BF))
-
-
-def scan_forward(px, pbd, conv_x, conv_bc, dt_bias, a_log, skip, starts, fill):
+    pl.when(c == pl.num_programs(0) - 1)(finish)
+
+
+def gather_beside_scan(
+    dp_n, cot, w_z, w_out, parts, rows_z, rows_out, s_loc, s_sib, r_sib, s_x, r_x, s_f, r_f, s_w, r_w
+):
+    c = pl.program_id(0)
+    last = pl.num_programs(0) - 1
+    who = peers(dp_n)
+    count = cot.shape[0]
+    pieces = s_x.shape[0]
+    span = count // pieces
+    block, inner = w_z.shape
+    here = pl.ds(pl.multiple_of(who["dp"] * block, block), block)
+    local = [
+        pltpu.make_async_copy(cot, parts.at[who["mine"]], s_loc.at[0]),
+        pltpu.make_async_copy(w_z, rows_z.at[here], s_loc.at[1]),
+        pltpu.make_async_copy(w_out, rows_out.at[here], s_loc.at[2]),
+    ]
+
+    def to_x(j):
+        at = pl.ds(j * span, span)
+        return push(cot.at[at], parts.at[who["mine"], at], s_x.at[j], r_x.at[j], who["xn"])
+
+    def to_sib():
+        return push(cot, parts.at[who["mine"]], s_sib.at[0], r_sib.at[0], who["sib"])
+
+    def forward(j):
+        there = parts.at[who["other"], pl.ds(j * span, span)]
+        return push(there, there, s_f.at[j], r_f.at[j], who["sib"])
+
+    cuts = [
+        shares(ref, rows, dp_n, pl.ds(h * (inner // 2), inner // 2), s_w.at[2 * i + h], r_w.at[2 * i + h], who)
+        for i, (ref, rows) in enumerate(((w_z, rows_z), (w_out, rows_out)))
+        for h in (0, 1)
+    ]
+
+    @pl.when(c == 0)
+    def _():
+        for copy in local:
+            copy.start()
+        meet(who)
+        for j in range(pieces):
+            to_x(j).start()
+        for own, along, onward in cuts:
+            loop_line(who["lines"], lambda k: along(k).start())
+            own().start()
+        to_sib().start()
+
+    def pass_cot(j):
+        to_x(j).wait()
+        forward(j).start()
+
+    def pass_rows(p):
+        own, along, onward = cuts[p]
+
+        def one(k):
+            along(k).wait()
+            onward(k).start()
+
+        loop_line(who["lines"], one)
+
+    events = {}
+    for p, at in enumerate((5, 10, 14)):
+        events.setdefault(at, []).append((pass_rows, p))
+    for j, at in enumerate((3, 6, 8, 11, 13)):
+        if j < pieces:
+            events.setdefault(at, []).append((pass_cot, j))
+    late = [(pass_rows, 3)] + [(pass_cot, j) for j in range(5, pieces)]
+    for at, steps in events.items():
+
+        @pl.when(c == at)
+        def _(steps=steps):
+            for fn, k in steps:
+                fn(k)
+
+    def finish():
+        for fn, k in late:
+            fn(k)
+        for copy in local:
+            copy.wait()
+        to_sib().wait()
+        for j in range(pieces):
+            forward(j).wait()
+        for own, along, onward in cuts:
+            own().wait()
+            loop_line(who["lines"], lambda k: onward(k).wait())
+
+    return finish
+
+
+def scan_forward(dp_n, px, pbd, conv_x, conv_bc, dt_bias, a_log, skip, meta, cot, w_z, w_out):
     tokens, inner = px.shape
-    blocks = starts.shape[0]
+    blocks = meta.shape[0]
     chunk = tokens // blocks
     heads = inner // HD
     bc = conv_bc.shape[1]
@@ -171,36 +264,118 @@
     bias = jnp.broadcast_to(dt_bias[:, None], (heads, chunk))
     rate = jnp.broadcast_to(-jnp.exp(a_log)[:, None], (heads, chunk))
     skip_w = jnp.repeat(skip, HD)[None, :]
-    fixed = lambda c, *_: (0, 0)
-    whole = lambda a: pl.BlockSpec(a.shape, fixed)
-    rows = lambda w: pl.BlockSpec((chunk, w), lambda c, *_: (c, 0))
+    whole = lambda a: pl.BlockSpec(a.shape, lambda c: (0, 0))
+    rows = lambda w: pl.BlockSpec((chunk, w), lambda c: (c, 0))
+    hbm = pl.BlockSpec(memory_space=pl.ANY)
+    dma = pltpu.SemaphoreType.DMA
+    sds = jax.ShapeDtypeStruct
+    pieces = 8
+    ways = dp_n - 1
     return pl.pallas_call(
-        functools.partial(scan_fwd_kernel, heads),
-        grid_spec=pltpu.PrefetchScalarGridSpec(
-            num_scalar_prefetch=2,
-            grid=(blocks,),
-            in_specs=[rows(inner), rows(pbd.shape[1])]
-            + [whole(a) for a in (conv_x, conv_bc, bias, rate, skip_w, upper, spread)],
-            out_specs=[rows(inner), pl.BlockSpec((1, bc // 2, inner), lambda c, *_: (c, 0, 0))],
-            scratch_shapes=[
-                pltpu.VMEM((bc // 2, inner), F32),
-                pltpu.VMEM((chunk + 8, inner), F32),
-                pltpu.VMEM((chunk + 8, bc), F32),
-            ],
+        functools.partial(scan_fwd_kernel, heads, dp_n),
+        grid=(blocks,),
+        in_specs=[pl.BlockSpec((1, 8, chunk), lambda c: (c, 0, 0)), rows(inner), rows(pbd.shape[1])]
+        + [whole(a) for a in (conv_x, conv_bc, bias, rate, skip_w, upper, spread)]
+        + [hbm] * 3,
+        out_specs=[rows(inner), pl.BlockSpec((1, bc // 2, inner), lambda c: (c, 0, 0))] + [hbm] * 3,
+        scratch_shapes=[
+            pltpu.VMEM((bc // 2, inner), F32),
+            pltpu.VMEM((chunk + 8, inner), F32),
+            pltpu.VMEM((chunk + 8, bc), F32),
+            dma((3,)), dma((1,)), dma((1,)), dma((pieces,)), dma((pieces,)), dma((pieces,)), dma((pieces,)),
+            dma((4, ways)), dma((4, ways)),
+        ],
+        out_shape=[
+            sds((tokens, inner), F32), sds((blocks, bc // 2, inner), BF),
+            sds((4,) + cot.shape, BF), sds((w_z.shape[0] * dp_n, inner), BF), sds((w_z.shape[0] * dp_n, inner), BF),
+        ],
+        compiler_params=pltpu.CompilerParams(
+            collective_id=3, has_side_effects=True, vmem_limit_bytes=48 * 2**20
         ),
+        name="scan_forward",
+    )(meta, px, pbd, conv_x, conv_bc, bias, rate, skip_w, upper, spread, cot, w_z, w_out)
+
+
+def gate_kernel(
+    dp_n, normed, rows_z, rows_out, parts, y, gain, pz, ggn, grad_t, sums, h_send, h_recv, s_h, r_h,
+):
+    i = pl.program_id(0)
+    who = peers(dp_n)
+    names = ("sib", "xn", "dg")
+    barrier = pltpu.get_barrier_semaphore()
+    span, quarter = parts.shape[1:]
+    chunk = h_send.shape[2]
+
+    @pl.when(i == 0)
+    def _():
+        for name in names:
+            pl.semaphore_signal(barrier, inc=1, device_id=who[name], device_id_type=MESH)
+
+    z = nn(normed[...], rows_z[...])
+    pz[...] = z
+    g = nn(parts[0], rows_out[0:quarter, :])
+    for k in range(1, 4):
+        g = g + nn(parts[k], rows_out[k * quarter : (k + 1) * quarter, :])
+    ggn[...] = g
+    for k in range(4):
+        grad_t[k * quarter : (k + 1) * quarter, :] = jnp.transpose(parts[k])
+    gated = y[...] * (z * sigmoid(z))
+    ones = jnp.ones((8, gated.shape[1]), BF)
+    for k, value in enumerate((gated * gated, gated * gain[...] * g)):
+        row = nt(ones, value.astype(BF))
+        for j in range(span // chunk):
+            h_send[k, pl.ds(i * (span // chunk) + j, 1), :] = row[0:1, j * chunk : (j + 1) * chunk]
+
+    @pl.when(i == pl.num_programs(0) - 1)
+    def _():
+        pl.semaphore_wait(barrier, 3)
+        copies = [push(h_send, h_recv.at[k], s_h.at[k], r_h.at[k], who[name]) for k, name in enumerate(names)]
+        for copy in copies:
+            copy.start()
+        for copy in copies:
+            copy.wait()
+        sums[...] = h_send[...] + h_recv[0] + h_recv[1] + h_recv[2]
+
+
+def gate(dp_n, blocks, normed, rows_z, rows_out, parts, y, gain):
+    count, width = normed.shape
+    inner = y.shape[1]
+    chunk = count // blocks
+    steps = 8
+    span = count // steps
+    quarter = width // 4
+    sds = jax.ShapeDtypeStruct
+    rows = lambda w: pl.BlockSpec((span, w), lambda i: (i, 0))
+    whole = lambda a: pl.BlockSpec(a.shape, lambda i: (0, 0))
+    return pl.pallas_call(
+        functools.partial(gate_kernel, dp_n),
+        grid=(steps,),
+        in_specs=[
+            rows(width), whole(rows_z), whole(rows_out),
+            pl.BlockSpec((4, span, quarter), lambda i: (0, i, 0)), rows(inner), whole(gain),
+        ],
+        out_specs=[
+            rows(inner), rows(inner), pl.BlockSpec((width, span), lambda i: (0, i)),
+            pl.BlockSpec((2, blocks, chunk), lambda i: (0, 0, 0)),
+        ],
         out_shape=[
-            jax.ShapeDtypeStruct((tokens, inner), F32),
-            jax.ShapeDtypeStruct((blocks, bc // 2, inner), BF),
+            sds((count, inner), F32), sds((count, inner), F32), sds((width, count), BF), sds((2, blocks, chunk), F32),
         ],
-        compiler_params=pltpu.CompilerParams(vmem_limit_bytes=48 * 2**20),
-        name="scan_forward",
-    )(starts, fill, px, pbd, conv_x, conv_bc, bias, rate, skip_w, upper, spread)
+        scratch_shapes=[
+            pltpu.VMEM((2, blocks, chunk), F32), pltpu.VMEM((3, 2, blocks, chunk), F32),
+            pltpu.SemaphoreType.DMA((3,)), pltpu.SemaphoreType.DMA((3,)),
+        ],
+        compiler_params=pltpu.CompilerParams(
+            collective_id=4, has_side_effects=True, vmem_limit_bytes=48 * 2**20
+        ),
+        name="gate",
+    )(normed, rows_z, rows_out, parts, y, gain)
 
 
 def scan_bwd_kernel(
     heads, total_inner, starts, fill, ggn, y, pz, px, px_halo, pbd, pbd_halo, sin, rows, gain, convx, convbc,
     bias, rate, skip, upper, spread, gather, ones_h,
-    lpx, lpz, lpbd, acc_x, acc_bc, acc_s, dstate, extx, extb, dux, dub,
+    lpx, lpz, lpbd, gn, acc_x, acc_bc, acc_s, dstate, extx, extb, dux, dub,
 ):
     i = pl.program_id(0)
     blocks = pl.num_programs(0)
@@ -220,7 +395,9 @@
             ref[...] = jnp.zeros_like(ref)
 
     moved = jnp.transpose(
-        jnp.concatenate([rows[0], jnp.zeros((chunk - rows.shape[1], chunk), F32)], axis=0)
+        jnp.concatenate(
+            [rows[0, pl.ds(c, 1), :], rows[1, pl.ds(c, 1), :], jnp.zeros((chunk - 2, chunk), F32)], axis=0
+        )
     )
     inv = lax.rsqrt(moved[:, 0:1] / total_inner + EPS)
     coef = inv * inv * inv * (moved[:, 1:2] / total_inner)
@@ -233,6 +410,7 @@
     d_gated = inv * (g * gain[...]) - gated * coef
     lpz[...] = (d_gated * yv * (sz * (1.0 + z * (1.0 - sz)))).astype(BF)
     dy = d_gated * silu_z
+    gn[...] = (gated * inv * gain[...]).astype(BF)
     acc_x[taps_n : taps_n + 1, :] += jnp.sum(g * gated * inv, axis=0, keepdims=True)
 
     extx[0:8, :] = jnp.where(keep, px_halo[...], 0.0)
@@ -398,11 +576,11 @@
             in_specs=[
                 back(inner), back(inner), back(inner), back(inner), halo(inner), back(width), halo(width),
                 pl.BlockSpec((1, bc // 2, inner), lambda i, *_: (blocks - 1 - i, 0, 0)),
-                pl.BlockSpec((1, 8, chunk), lambda i, *_: (blocks - 1 - i, 0, 0)),
+                pl.BlockSpec(rows.shape, lambda i, *_: (0, 0, 0)),
             ]
             + [whole(a) for a in consts],
             out_specs=[
-                back(inner), back(inner), back(width),
+                back(inner), back(inner), back(width), back(inner),
                 pl.BlockSpec((8, inner), lambda i, *_: (0, 0)),
                 pl.BlockSpec((8, bc), lambda i, *_: (0, 0)),
                 pl.BlockSpec((2 * heads, chunk), lambda i, *_: (0, 0)),
@@ -419,6 +597,7 @@
             jax.ShapeDtypeStruct((tokens, inner), BF),
             jax.ShapeDtypeStruct((tokens, inner), BF),
             jax.ShapeDtypeStruct((tokens, width), BF),
+            jax.ShapeDtypeStruct((tokens, inner), BF),
             jax.ShapeDtypeStruct((8, inner), F32),
             jax.ShapeDtypeStruct((8, bc), F32),
             jax.ShapeDtypeStruct((2 * heads, chunk), F32),
@@ -466,11 +645,11 @@
 def tail_kernel(
     dp_n, units,
     grad_t_in, gn_in, rows_out_in, normed_t_in, lpz_in, rows_z_in, lpx_in, rows_x_in, lpbd_in, rows_bd_in, normed_in,
-    tokens, acc_x, acc_bc, acc_s,
-    block_out, in_share, row_sums, g_x, g_z, g_out, g_bc, small_out,
+    tokens, acc_x, acc_bc, acc_s, cot, q_wide, gain,
+    block_out, grad_tokens, g_x, g_z, g_out, g_bc, small_out,
     sib_send, sib_recv, x_send, x_recv, part, held,
     y_send, y_recv, z_send, z_recv, g_own, yb_send, yb_recv, zb_send, zb_recv, gb_own, bh_send, bh_recv,
-    bx_send, bx_recv, bs_recv, h_send, h_recv, sy_send, sy_recv, sz_send, sz_recv, dy_send, dy_recv, dz_send, dz_recv,
+    bx_send, bx_recv, bs_recv, h_send, h_recv, sy_send, sy_recv, sz_send, sz_recv, dy_send, dy_recv, dz_send, dz_recv, row_sums,
     grad_t, gn, rows_out, normed_t, lpz, rows_z, lpx, rows_x, lpbd, rows_bd, normed,
     s_in, s_sib, r_sib, s_x, r_x, s_y, r_y, s_z, r_z, s_m, r_m, s_sl, r_sl,
 ):
@@ -542,7 +721,20 @@
             at = slice(u * span, (u + 1) * span)
             block_out[at, :] = (tokens[at, :].astype(F32) + total).astype(BF)
         else:
-            in_share[(u - units) * span : (u - units + 1) * span, :] = total
+            first = (u - units) * span
+            lanes = q_wide.shape[1]
+            cols = pl.ds(pl.multiple_of(who["mine"] * quarter, quarter), quarter)
+            for j in range(span // lanes):
+                at = slice(first + j * lanes, first + (j + 1) * lanes)
+                row, lane = (first + j * lanes) // width, (first + j * lanes) % width
+                dots = jnp.transpose(jnp.broadcast_to(row_sums[row : row + 1, lane : lane + lanes], (lanes, lanes)))
+                q = q_wide[at, :]
+                coef = q * q * (dots / width)
+                grad_tokens[at, :] = (
+                    cot[at, :].astype(F32)
+                    + q[:, 0:1] * gain[:, cols] * total[j * lanes : (j + 1) * lanes]
+                    - tokens[at, :].astype(F32) * coef[:, 0:1]
+                )
 
     def rows_of(line, pair):
         return pl.ds(pl.multiple_of((2 * line + pair) * block, block), block)
@@ -708,7 +900,7 @@
         for k in range(3):
             copy_h(k).wait()
         over_heads = h_send[...] + h_recv[0] + h_recv[1] + h_recv[2]
-        row_sums[...] = over_heads[2 : 2 + token_rows, :]
+        row_sums[0:token_rows, :] = over_heads[2 : 2 + token_rows, :]
         sy_send[...] = jnp.zeros_like(sy_send)
         sy_send[0:2, :] = over_heads[0:2, :]
         per = width // inner
@@ -761,7 +953,7 @@
     seq((small_d,), (head_c, 6), (grad_c, 4), (bc_f,), (head_c, 7), (grad_c, 5))
 
 
-def tail(dp_n, units, normed_t, normed, grad_t, gn, lpx, lpz, lpbd, rows_x, rows_z, rows_bd, rows_out, tokens, acc_x, acc_bc, acc_s):
+def tail(dp_n, units, normed_t, normed, grad_t, gn, lpx, lpz, lpbd, rows_x, rows_z, rows_bd, rows_out, tokens, acc_x, acc_bc, acc_s, cot, q_wide, gain):
     count, width = normed.shape
     inner = lpx.shape[1]
     bc = acc_bc.shape[1]
@@ -775,18 +967,19 @@
     dma = pltpu.SemaphoreType.DMA
     operands = (
         grad_t, gn, rows_out, normed_t, lpz, rows_z, lpx, rows_x, lpbd, rows_bd, normed, tokens, acc_x, acc_bc, acc_s,
+        cot, q_wide, gain,
     )
     sds = jax.ShapeDtypeStruct
     spec = pl.BlockSpec(memory_space=pltpu.VMEM)
     return pl.pallas_call(
         functools.partial(tail_kernel, dp_n, units),
         out_shape=[
-            sds((count, quarter), BF), sds((count, quarter), F32), sds((count // width, width), F32),
+            sds((count, quarter), BF), sds((count, quarter), F32),
             sds((block, inner), F32), sds((block, inner), F32), sds((block, inner), F32), sds((block, bc), F32),
             sds((24, width), F32),
         ],
-        in_specs=[pl.BlockSpec(memory_space=pl.ANY)] * 11 + [spec] * 4,
-        out_specs=[spec] * 8,
+        in_specs=[pl.BlockSpec(memory_space=pl.ANY)] * 11 + [spec] * 7,
+        out_specs=[spec] * 7,
         scratch_shapes=[
             vm((2 * units, 2, span, quarter), BF), vm((2 * units, 2, span, quarter), BF),
             vm((2 * units, span, quarter), BF), vm((2 * units, span, quarter), BF),
@@ -802,6 +995,7 @@
             vm((8, width), F32), vm((3, 8, width), F32),
             vm((8, width), F32), vm((8, width), F32), vm((8, width), F32), vm((more, 8, width), F32),
             vm((16, width), BF), vm((16, width), BF), vm((16, width), BF), vm((more, 16, width), BF),
+            vm((8, width), F32),
         ]
         + [vm(a.shape, a.dtype) for a in operands[:11]]
         + [
@@ -1015,35 +1209,22 @@
     total_inner = inner * heads_n
     w_bd = jnp.concatenate([w_bc, jnp.pad(w_dt, ((0, 0), (0, chunk - heads)))], axis=1)
     px, pbd, normed, normed_t, q_wide, rows_x, rows_bd = front(dp_n, 4, tokens, w_bd, w_x, norm_gain[None, :])
-    rows_z, rows_out = (lax.all_gather(w, "dp", axis=0, tiled=True) for w in (w_z, w_out))
-    y, sin = scan_forward(px, pbd, conv_x, conv_bc, dt_bias, a_log, skip, starts, fill)
-    pz = nn(normed, rows_z)
-    g_full = lax.all_gather(cotangent, "heads", axis=1, tiled=True)
-    ggn = nn(g_full, rows_out)
-    gated = y * jax.nn.silu(pz)
-    both = jnp.stack(
-        [jnp.sum(gated * gated, axis=-1), jnp.sum(gated * gate_gain * ggn, axis=-1)], axis=0
-    )
-    both = lax.psum(both, "heads")
-    rows = jnp.pad(jnp.transpose(both.reshape(2, blocks, chunk), (1, 0, 2)), ((0, 0), (0, 6), (0, 0)))
-    gate_inverse = lax.rsqrt(both[0] / total_inner + EPS)[:, None]
-    gated_normed = (gated * gate_inverse * gate_gain).astype(BF)
-    lpx, lpz, lpbd, acc_x, acc_bc, acc_s = scan_backward(
-        ggn, y, pz, px, pbd, sin, rows, gate_gain, conv_x, conv_bc, dt_bias, a_log, skip, starts, fill,
+    keep = jnp.where(starts == 0, 1.0, 0.0).astype(F32)
+    meta = jnp.stack([keep, fill.astype(F32)] + [keep] * 6, axis=1)
+    meta = jnp.broadcast_to(meta[:, :, None], (blocks, 8, chunk))
+    y, sin, parts, rows_z, rows_out = scan_forward(
+        dp_n, px, pbd, conv_x, conv_bc, dt_bias, a_log, skip, meta, cotangent, w_z, w_out
+    )
+    pz, ggn, grad_t, sums = gate(dp_n, blocks, normed, rows_z, rows_out, parts, y, gate_gain[None, :])
+    lpx, lpz, lpbd, gn, acc_x, acc_bc, acc_s = scan_backward(
+        ggn, y, pz, px, pbd, sin, sums, gate_gain, conv_x, conv_bc, dt_bias, a_log, skip, starts, fill,
         total_inner,
     )
-    block_out, in_share, row_sums, grad_w_x, grad_w_z, grad_w_out, grad_w_bc, small = tail(
-        dp_n, 4, normed_t, normed, g_full.T, gated_normed, lpx, lpz, lpbd, rows_x, rows_z, rows_bd, rows_out,
-        tokens, acc_x, acc_bc, acc_s,
-    )
-    own = tokens.astype(F32)
+    block_out, grad_tokens, grad_w_x, grad_w_z, grad_w_out, grad_w_bc, small = tail(
+        dp_n, 4, normed_t, normed, grad_t, gn, lpx, lpz, lpbd, rows_x, rows_z, rows_bd, rows_out,
+        tokens, acc_x, acc_bc, acc_s, cotangent, q_wide, norm_gain[None, :],
+    )
     own_gain = lax.dynamic_slice_in_dim(norm_gain, head_index * columns, columns, 0)
-    inverse = q_wide[:, 0:1]
-    grad_tokens = (
-        cotangent.astype(F32)
-        + inverse * own_gain * in_share
-        - own * (inverse * inverse) * (row_sums.reshape(-1) / width)[:, None]
-    )
     return (block_out, grad_tokens) + outputs(
         small, dp_index, head_index, own_gain, conv_x, bc, heads, inner, width // dp_n, chunk,
         grad_w_x, grad_w_z, grad_w_bc, grad_w_out,

time: 315 us -> 249 us (0.79); the launches traced: 309 us -> 248 us
  waiting for transfers between devices: 44.5 us -> 0 us
  Pallas kernels: 187 us -> 212 us
  matrix products: 18.6 us -> 0 us
  between operations: 14.5 us -> 0.92 us
  blocking collectives: 10.7 us -> 0 us
  local copies, waits for them, and re-layouts: 21.7 us -> 28.8 us
  other arithmetic: 12.2 us -> 5.55 us
    all_gather x3 -> x0, waiting for transfers between devices: 43.1 us -> none  [the longest x1 35.4 us: body(): g_full = lax.all_gather(cotangent, 'heads', axis=1, tiled=True)]
    pallas_call x1 -> x2, Pallas kernels: 19.8 us -> 49.4 us  [the longest x1 32.9 us: scan_forward(): pl.pallas_call(functools.partial(scan_fwd_kernel, heads, dp_n), grid=(blo...]
    dot_general x2 -> x0, matrix products: 18.6 us -> none  [nn(): lax.dot_general(a, b, (((1,), (0,)), ((), ())), preferred_element_type=F32)]
    psum x1 -> x0, blocking collectives: 10.7 us -> none  [body(): both = lax.psum(both, 'heads')]
    unnamed x60 -> x65, local copies, waits for them, and re-layouts: 14.4 us -> 20.7 us
    pallas_call x1, Pallas kernels: 50.8 us -> 46.5 us  [front(): pl.pallas_call(functools.partial(front_kernel, dp_n, units), out_shape=ou...]
    convert_element_type x1 -> x0, other arithmetic: 3.94 us -> none  [body(): gated_normed = (gated * gate_inverse * gate_gain).astype(BF)]
    sub x1 -> x0, other arithmetic: 3.39 us -> none  [body(): cotangent.astype(F32) + inverse * own_gain * in_share]
  transfers between devices with their start and end apart: 3 -> 0, of which waited for: 2 -> 0; matrix products, arithmetic and copies ran while one was open for 4% -> 0% of each run, Pallas kernels for 23% -> 0%
where the time goes in v3:
time: 249 us; the launch traced here: 248 us
  Pallas kernels  212 us (85%)
  local copies, waits for them, and re-layouts  28.8 us (12%)
  other arithmetic  5.55 us (2%)
    pallas_call x1, Pallas kernels, tail(): pl.pallas_call(functools.partial(tail_kernel, dp_n, units), out_shape=[sd...  73.5 us
    pallas_call x1, Pallas kernels, front(): pl.pallas_call(functools.partial(front_kernel, dp_n, units), out_shape=ou...  46.5 us
    pallas_call x1, Pallas kernels, scan_backward(): pl.pallas_call(kernel, grid_spec=pltpu.PrefetchScalarGridSpec(num_scalar_...  42.9 us
    pallas_call x1, Pallas kernels, scan_forward(): pl.pallas_call(functools.partial(scan_fwd_kernel, heads, dp_n), grid=(blo...  32.9 us
    unnamed x65, local copies, waits for them, and re-layouts  20.7 us
    pallas_call x1, Pallas kernels, gate(): pl.pallas_call(functools.partial(gate_kernel, dp_n), grid=(steps,), in_sp...  16.5 us

profile of v3, /device:TPU:0, one launch (start us, length us, event | category | flops | bytes accessed | tf_op | source)
XLA Modules:
  0.0 247.5 jit_solution(7307794342598301445)
XLA Ops:
  0.6 0.8 copy.37
  1.4 1.5 fusion.1.w_bd
  2.9 46.5 %front.1 = (f32[2048,512]{1,0:T(8,128)}, f32[2048,384]{1,0:T(8,128)}, bf16[2048,1024]{1,0:T(8,128)(2,1)}, bf16[1024,2048]{1,0:T(8,128)(2,1)}, f32[2048,128]{1,0:...) custom-call(bf16[2048,256]{1,0:T(8,128)(2,1)} %tokens.3, bf16[128,384]{1,0:T(8,128)(2,1)} %fusion.1.w_bd, ...), custom_call_target="tpu_custom_call" | custom-call | tf_op jit(solution)/shard_map/front/pallas_call | solution.py:1175
  49.4 0.7 fusion.2
  50.1 0.7 convert_bitcast_fusion
  50.7 0.1 copy.38
  50.8 0.1 broadcast_in_dim.23.meta
  50.9 0.7 broadcast_in_dim.24.bias.refs_14_
  51.6 0.7 exponential_negate_fusion
  52.3 0.1 broadcast_in_dim.25.rate.refs_15_
  52.4 0.7 broadcast_in_dim.26
  53.1 0.1 broadcast_in_dim_reshape.4.skip.refs_16_
  53.2 1.2 copy-done
  54.4 1.0 copy-done.5
  55.4 0.9 copy-done.10
  56.3 0.9 copy-done.11
  57.2 0.8 copy-done.13
  58.0 0.7 copy-done.15
  58.7 0.7 copy-done.17
  59.3 32.9 %scan_forward.1 = (f32[2048,512]{1,0:T(8,128)}, bf16[16,128,512]{2,1,0:T(8,128)(2,1)S(1)}, bf16[4,2048,256]{2,1,0:T(8,128)(2,1)}, bf16[1024,512]{1,0:T(8,128)(2,1)S(1)}, bf16[1024,512]{1,0:T(8,128)(2,1)S(1)}) custom-call(f32[16,8,128]{2,1,0:T(8,128)S(1)} %broadcast_in_dim.23.meta, f32[2048,512]{1,0:T(8,128)} %get-tuple-element.45.px.refs_5_.refs_6_, ...), custom_call_target="tpu_custom_call" | custom-call | tf_op jit(solution)/shard_map/scan_forward/pallas_call | solution.py:274
  92.3 0.0 copy-start.4
  92.3 1.3 copy-done.4
  93.6 0.0 copy-start.8
  93.6 0.0 copy-start.9
  93.6 0.0 copy-start.12
  93.6 0.0 copy-start.14
  93.6 0.0 copy-start.16
  93.7 0.0 copy-start.18
  93.7 0.0 copy-start.23
  93.7 0.0 copy-start.24
  93.7 16.5 %gate.1 = (f32[2048,512]{1,0:T(8,128)}, f32[2048,512]{1,0:T(8,128)}, bf16[1024,2048]{1,0:T(8,128)(2,1)}, f32[2,16,128]{2,1,0:T(8,128)S(1)}) custom-call(bf16[2048,1024]{1,0:T(8,128)(2,1)} %get-tuple-element.44.normed.normed_in, bf16[1024,512]{1,0:T(8,128)(2,1)S(1)} %get-tuple-element.47.rows_z.rows_z_in, ...), custom_call_target="tpu_custom_call" | custom-call | tf_op jit(solution)/shard_map/gate/pallas_call | solution.py:350
  110.2 0.0 copy-done.1
  110.2 0.0 copy-done.2
  110.2 0.0 copy-done.6
  110.2 0.0 copy-done.8
  110.2 0.0 copy-done.9
  110.2 0.0 copy-done.12
  110.2 0.0 copy-done.14
  110.3 42.9 %scan_backward.1 = (bf16[2048,512]{1,0:T(8,128)(2,1)S(1)}, bf16[2048,512]{1,0:T(8,128)(2,1)}, bf16[2048,384]{1,0:T(8,128)(2,1)S(1)}, bf16[2048,512]{1,0:T(8,128)...) custom-call(s32[16]{0:T(128)S(1)} %copy-done.23, s32[16]{0:T(128)S(1)} %copy-done.24, ...), custom_call_target="tpu_custom_call" | custom-call | tf_op jit(solution)/shard_map/scan_backward/pallas_call | solution.py:571
  153.2 1.3 copy-done.3
  154.5 1.2 copy-done.7
  155.7 0.6 copy-done.19
  156.3 0.6 copy-done.20
  156.9 0.6 copy-done.21
  157.5 73.5 %tail.1 = (bf16[2048,256]{1,0:T(8,128)(2,1)}, f32[2048,256]{1,0:T(8,128)}, f32[128,512]{1,0:T(8,128)}, f32[128,512]{1,0:T(8,128)}, f32[128,512]{1,0:T(8,128)}, /*index=5*/f32[128,256]{1,0:T(8,128)}, f32[24,1024]{1,0:T(8,128)}) custom-call(bf16[1024,2048]{1,0:T(8,128)(2,1)} %get-tuple-element.51.grad_t_in, bf16[2048,512]{1,0:T(8,128)(2,1)} %get-tuple-element.56.gn_in, ...), custom_call_target="tpu_custom_call" | custom-call | tf_op jit(solution)/shard_map/tail/pallas_call | solution.py:974
  231.0 0.9 slice_reduce_fusion
  231.9 1.3 dynamic-slice_divide_fusion
  233.2 0.8 slice.40
  234.0 0.6 dynamic-slice_bitcast_fusion
  234.6 0.8 fusion.3
  235.4 0.6 slice.42
  236.0 0.6 reshape_squeeze.6
  236.7 0.1 reduce_sum.18
  236.8 0.6 fusion.5
  237.4 0.8 slice.48
  238.1 0.6 fusion.4
  238.7 0.1 reshape_squeeze.7
  238.8 0.6 reduce_sum.19
  239.4 2.3 copy.45
  241.7 3.0 %copy.46 = f32[2048,256]{1,0:T(8,128)} copy(f32[2048,256]{1,0:T(8,128)} %get-tuple-element.97) | data formatting | bytes 4194304
  244.7 0.7 copy.47
  245.4 0.7 copy.48
  246.2 0.7 copy.49
  246.8 0.7 copy.50
  (33 shorter events, 0.1 us)
Async XLA Ops:
  53.2 1.2 copy-start
  54.4 1.0 copy-start.5
  55.4 0.9 copy-start.10
  56.3 0.9 copy-start.11
  57.2 0.8 copy-start.13
  58.0 0.7 copy-start.15
  58.7 0.7 copy-start.17
  59.3 34.2 %copy-start.22 = (f32[512]{0:T(512)S(1)}, f32[512]{0:T(512)}, u32[]{:S(2)}) copy-start(f32[512]{0:T(512)} %param.37) | copy-start | bytes 6148
  92.3 1.3 copy-start.4
  93.6 16.6 %copy-start.1 = (bf16[1024,512]{1,0:T(8,128)(2,1)}, bf16[1024,512]{1,0:T(8,128)(2,1)S(1)}, u32[]{:S(2)}) copy-start(bf16[1024,512]{1,0:T(8,128)(2,1)S(1)} %get-tuple-element.47.rows_z.rows_z_in) | copy-start | bytes 3145732
  93.6 16.6 %copy-start.2 = (bf16[1024,512]{1,0:T(8,128)(2,1)}, bf16[1024,512]{1,0:T(8,128)(2,1)S(1)}, u32[]{:S(2)}) copy-start(bf16[1024,512]{1,0:T(8,128)(2,1)S(1)} %get-tuple-element.48.rows_out.rows_out_in) | copy-start | bytes 3145732
  93.6 16.6 %copy-start.6 = (bf16[128,1536]{1,0:T(8,128)(2,1)S(1)}, bf16[128,1536]{1,0:T(8,128)(2,1)}, u32[]{:S(2)}) copy-start(bf16[128,1536]{1,0:T(8,128)(2,1)} %constant.36.clone.spread.refs_18_) | copy-start | bytes 1179652
  93.6 16.6 %copy-start.8 = (bf16[3,512,128]{2,1,0:T(8,128)(2,1)S(1)}, bf16[3,512,128]{2,1,0:T(8,128)(2,1)}, u32[]{:S(2)}) copy-start(bf16[3,512,128]{2,1,0:T(8,128)(2,1)} %constant.37.clone.refs_19_) | copy-start | bytes 1179652
  93.6 16.6 %copy-start.9 = (bf16[1024,128]{1,0:T(8,128)(2,1)S(1)}, bf16[1024,128]{1,0:T(8,128)(2,1)}, u32[]{:S(2)}) copy-start(bf16[1024,128]{1,0:T(8,128)(2,1)} %constant.38.clone.refs_21_) | copy-start | bytes 786436
  93.6 16.6 %copy-start.12 = (bf16[128,512]{1,0:T(8,128)(2,1)S(1)}, bf16[128,512]{1,0:T(8,128)(2,1)}, u32[]{:S(2)}) copy-start(bf16[128,512]{1,0:T(8,128)(2,1)} %constant.39.clone.refs_20_) | copy-start | bytes 393220
  93.6 16.6 %copy-start.14 = (bf16[128,128]{1,0:T(8,128)(2,1)S(1)}, bf16[128,128]{1,0:T(8,128)(2,1)}, u32[]{:S(2)}) copy-start(bf16[128,128]{1,0:T(8,128)(2,1)} %constant.35.clone.upper.refs_17_) | copy-start | bytes 98308
  93.6 16.6 %copy-start.16 = (f32[4,512]{1,0:T(4,128)S(1)}, f32[4,512]{1,0:T(4,128)}, u32[]{:S(2)}) copy-start(f32[4,512]{1,0:T(4,128)} %refs_12_.1) | copy-start | bytes 24580
  93.7 16.6 %copy-start.18 = (f32[4,256]{1,0:T(4,128)S(1)}, f32[4,256]{1,0:T(4,128)}, u32[]{:S(2)}) copy-start(f32[4,256]{1,0:T(4,128)} %refs_13_.1) | copy-start | bytes 12292
  93.7 16.6 %copy-start.23 = (s32[16]{0:T(128)S(1)}, s32[16]{0:T(128)}, u32[]{:S(2)}) copy-start(s32[16]{0:T(128)} %refs_0_.1) | copy-start | bytes 196
  93.7 16.6 %copy-start.24 = (s32[16]{0:T(128)S(1)}, s32[16]{0:T(128)}, u32[]{:S(2)}) copy-start(s32[16]{0:T(128)} %refs_1_.1) | copy-start | bytes 196
  153.2 1.3 copy-start.3
  154.5 1.2 copy-start.7
  155.7 0.6 copy-start.19
  156.3 0.6 copy-start.20
  156.9 0.6 copy-start.21
  231.0 13.8 %copy-start.27 = (f32[128,512]{1,0:T(8,128)S(1)}, f32[128,512]{1,0:T(8,128)}, u32[]{:S(2)}) copy-start(f32[128,512]{1,0:T(8,128)} %get-tuple-element.99) | copy-start | bytes 786436
  231.0 14.5 %copy-start.26 = (f32[128,512]{1,0:T(8,128)S(1)}, f32[128,512]{1,0:T(8,128)}, u32[]{:S(2)}) copy-start(f32[128,512]{1,0:T(8,128)} %get-tuple-element.100) | copy-start | bytes 786436
  231.0 15.2 %copy-start.28 = (f32[128,256]{1,0:T(8,128)S(1)}, f32[128,256]{1,0:T(8,128)}, u32[]{:S(2)}) copy-start(f32[128,256]{1,0:T(8,128)} %get-tuple-element.102) | copy-start | bytes 393220
  231.0 15.8 %copy-start.25 = (f32[128,512]{1,0:T(8,128)S(1)}, f32[128,512]{1,0:T(8,128)}, u32[]{:S(2)}) copy-start(f32[128,512]{1,0:T(8,128)} %get-tuple-element.109) | copy-start | bytes 786436

commit v4 on v3

--- a/solution.py
+++ b/solution.py
@@ -1,7 +1,6 @@
 import functools
 import jax
 import jax.numpy as jnp
-import numpy as np
 from jax import lax
 from jax.experimental import pallas as pl
 from jax.experimental.pallas import tpu as pltpu
@@ -51,22 +50,27 @@
     return lax.broadcasted_iota(jnp.int32, (rows, cols), axis)
 
 
-def scan_constants(chunk, heads):
+def zero_one(cond):
+    return jnp.where(cond, 1.0, 0.0).astype(BF)
+
+
+def set_upper(upper):
+    upper[...] = zero_one(iota2(*upper.shape, 0) <= iota2(*upper.shape, 1))
+
+
+def set_spread(spread, heads):
+    rows, lanes = iota2(*spread.shape, 0), iota2(*spread.shape, 1)
     inner = heads * HD
-    t = np.arange(chunk)
-    upper = (t[:, None] <= t[None, :]).astype(np.float32)
-    head_of = np.arange(inner) // HD
-    spread = np.zeros((chunk, 3 * inner), np.float32)
+    base = heads * (1 + 2 * (lanes // inner)) + (lanes % inner) // HD
+    spread[...] = zero_one(jnp.logical_or(rows == base, rows == base + heads))
+
+
+def set_gather(gather, ones_h, heads):
     for q in range(3):
-        for part in range(2):
-            base = heads * (1 + 2 * q + part)
-            for h in range(heads):
-                spread[base + h, q * inner : (q + 1) * inner] = head_of == h
-    gather = np.zeros((3, inner, chunk), np.float32)
-    for q in range(3):
-        for h in range(heads):
-            gather[q, :, q * heads + h] = head_of == h
-    return jnp.asarray(upper, BF), jnp.asarray(spread, BF), jnp.asarray(gather, BF)
+        rows, lanes = iota2(*gather.shape[1:], 0), iota2(*gather.shape[1:], 1)
+        gather[q] = zero_one(lanes == q * heads + rows // HD)
+    rows, lanes = iota2(*ones_h.shape, 0), iota2(*ones_h.shape, 1)
+    ones_h[...] = zero_one(lanes == heads + rows // ones_h.shape[1])
 
 
 def conv_from(ext, taps, rows, halo):
@@ -108,40 +112,51 @@
     return jnp.concatenate([jnp.where(low_lanes, v, zero), jnp.where(low_lanes, zero, v)], axis=0)
 
 
-def scan_fwd_kernel(
-    heads, dp_n, meta, px, pbd, convx, convbc, bias, rate, skip, upper, spread, cot, w_z, w_out,
-    y_out, sin_out, parts, rows_z, rows_out, state, extx, extb,
-    s_loc, s_sib, r_sib, s_x, r_x, s_f, r_f, s_w, r_w,
-):
-    c = pl.program_id(0)
+def read_vec(vec, heads, chunk, inner, bc, taps):
+    return dict(
+        convx=vec[0:taps, :inner], skip=vec[4:5, :inner], gain=vec[5:6, :inner],
+        bias=vec[8 : 8 + heads, :chunk], rate=vec[8 : 8 + heads, chunk : 2 * chunk], convbc=vec[16 : 16 + taps, :bc],
+    )
+
+
+def read_block(vec, c, chunk):
+    row = vec[pl.ds(24 + c, 1), :]
+    return row[:, 0:1] > 0.5, row[:, chunk : chunk + 1], row[:, 2 * chunk : 2 * chunk + 1] > 0.5
+
+
+def pack_vec(conv_x, skip, gate_gain, norm_gain, dt_bias, a_log, conv_bc, starts, fill, chunk):
+    width = norm_gain.shape[0]
+    wide = lambda a: jnp.pad(a, ((0, 0), (0, width - a.shape[1])))
+    down = lambda a, rows: jnp.pad(a, ((0, rows - a.shape[0]), (0, 0)))
+    cols = lambda *vs: jnp.concatenate([jnp.broadcast_to(v[:, None], (v.shape[0], chunk)) for v in vs], axis=1)
+    keep = jnp.where(starts == 0, 1.0, 0.0).astype(F32)
+    keep_next = jnp.concatenate([keep[1:], jnp.zeros((1,), F32)])
+    rows = [
+        wide(conv_x), wide(jnp.repeat(skip, HD)[None]), wide(gate_gain[None]), norm_gain[None],
+        jnp.zeros((1, width), F32), down(wide(cols(dt_bias, -jnp.exp(a_log))), 8), down(wide(conv_bc), 8),
+        wide(cols(keep, fill.astype(F32), keep_next)),
+    ]
+    return jnp.concatenate(rows, axis=0)
+
+
+def scan_step(heads, par, block, px, pbd, upper, spread, state, extx, extb):
     chunk, inner = px.shape
-    bc = convbc.shape[1]
+    bc = par["convbc"].shape[1]
     ns = bc // 2
-    keep = meta[0, 0:1, 0:1] > 0.5
-    finish = gather_beside_scan(
-        dp_n, cot, w_z, w_out, parts, rows_z, rows_out, s_loc, s_sib, r_sib, s_x, r_x, s_f, r_f, s_w, r_w
-    )
-
-    @pl.when(c == 0)
-    def _():
-        state[...] = jnp.zeros_like(state)
-        extx[...] = jnp.zeros_like(extx)
-        extb[...] = jnp.zeros_like(extb)
-
+    keep, n_live, _ = block
     state[...] = jnp.where(keep, state[...], 0.0)
     extx[0:8, :] = jnp.where(keep, extx[chunk : chunk + 8, :], 0.0)
     extb[0:8, :] = jnp.where(keep, extb[chunk : chunk + 8, :], 0.0)
     extx[8 : chunk + 8, :] = px[...]
     extb[8 : chunk + 8, :] = pbd[:, :bc]
 
-    n_live = meta[0, 1:2, 0:1]
-    u = conv_from(extx, convx[...], chunk, 8)
+    u = conv_from(extx, par["convx"], chunk, 8)
     x = u * sigmoid(u) * (iota2(chunk, inner, 0).astype(F32) < n_live).astype(F32)
-    ub = conv_from(extb, convbc[...], chunk, 8)
+    ub = conv_from(extb, par["convbc"], chunk, 8)
     act = (ub * sigmoid(ub) * (iota2(chunk, bc, 0).astype(F32) < n_live).astype(F32)).astype(BF)
     b, cc = act[:, :ns], act[:, ns:]
 
-    _, _, dt, run = dt_rows(pbd[:, bc:], bias[...], rate[...], n_live, heads, upper[...])
+    _, _, dt, run = dt_rows(pbd[:, bc:], par["bias"], par["rate"], n_live, heads, upper[...])
     cols, wide = spread_all(run, dt, heads, chunk, spread[...])
     dt_w, ein_w, eout_w = wide[:, :inner], wide[:, inner : 2 * inner], wide[:, 2 * inner :]
 
@@ -160,144 +175,13 @@
         diag.append(nn(jnp.concatenate(mix, axis=1), pair))
     enter = state[...]
     enter_b = enter.astype(BF)
-    sin_out[0] = enter_b
-    y_out[...] = jnp.concatenate(diag, axis=1) + ein_w * nn(cc, enter_b) + skip[...] * x
+    y = jnp.concatenate(diag, axis=1) + ein_w * nn(cc, enter_b) + par["skip"] * x
     state[...] = ein_w[chunk - 1 : chunk, :] * enter + tn(b, (xd * eout_w).astype(BF))
-    pl.when(c == pl.num_programs(0) - 1)(finish)
-
-
-def gather_beside_scan(
-    dp_n, cot, w_z, w_out, parts, rows_z, rows_out, s_loc, s_sib, r_sib, s_x, r_x, s_f, r_f, s_w, r_w
-):
-    c = pl.program_id(0)
-    last = pl.num_programs(0) - 1
-    who = peers(dp_n)
-    count = cot.shape[0]
-    pieces = s_x.shape[0]
-    span = count // pieces
-    block, inner = w_z.shape
-    here = pl.ds(pl.multiple_of(who["dp"] * block, block), block)
-    local = [
-        pltpu.make_async_copy(cot, parts.at[who["mine"]], s_loc.at[0]),
-        pltpu.make_async_copy(w_z, rows_z.at[here], s_loc.at[1]),
-        pltpu.make_async_copy(w_out, rows_out.at[here], s_loc.at[2]),
-    ]
-
-    def to_x(j):
-        at = pl.ds(j * span, span)
-        return push(cot.at[at], parts.at[who["mine"], at], s_x.at[j], r_x.at[j], who["xn"])
-
-    def to_sib():
-        return push(cot, parts.at[who["mine"]], s_sib.at[0], r_sib.at[0], who["sib"])
-
-    def forward(j):
-        there = parts.at[who["other"], pl.ds(j * span, span)]
-        return push(there, there, s_f.at[j], r_f.at[j], who["sib"])
-
-    cuts = [
-        shares(ref, rows, dp_n, pl.ds(h * (inner // 2), inner // 2), s_w.at[2 * i + h], r_w.at[2 * i + h], who)
-        for i, (ref, rows) in enumerate(((w_z, rows_z), (w_out, rows_out)))
-        for h in (0, 1)
-    ]
-
-    @pl.when(c == 0)
-    def _():
-        for copy in local:
-            copy.start()
-        meet(who)
-        for j in range(pieces):
-            to_x(j).start()
-        for own, along, onward in cuts:
-            loop_line(who["lines"], lambda k: along(k).start())
-            own().start()
-        to_sib().start()
-
-    def pass_cot(j):
-        to_x(j).wait()
-        forward(j).start()
-
-    def pass_rows(p):
-        own, along, onward = cuts[p]
-
-        def one(k):
-            along(k).wait()
-            onward(k).start()
-
-        loop_line(who["lines"], one)
-
-    events = {}
-    for p, at in enumerate((5, 10, 14)):
-        events.setdefault(at, []).append((pass_rows, p))
-    for j, at in enumerate((3, 6, 8, 11, 13)):
-        if j < pieces:
-            events.setdefault(at, []).append((pass_cot, j))
-    late = [(pass_rows, 3)] + [(pass_cot, j) for j in range(5, pieces)]
-    for at, steps in events.items():
-
-        @pl.when(c == at)
-        def _(steps=steps):
-            for fn, k in steps:
-                fn(k)
-
-    def finish():
-        for fn, k in late:
-            fn(k)
-        for copy in local:
-            copy.wait()
-        to_sib().wait()
-        for j in range(pieces):
-            forward(j).wait()
-        for own, along, onward in cuts:
-            own().wait()
-            loop_line(who["lines"], lambda k: onward(k).wait())
-
-    return finish
-
-
-def scan_forward(dp_n, px, pbd, conv_x, conv_bc, dt_bias, a_log, skip, meta, cot, w_z, w_out):
-    tokens, inner = px.shape
-    blocks = meta.shape[0]
-    chunk = tokens // blocks
-    heads = inner // HD
-    bc = conv_bc.shape[1]
-    upper, spread, _ = scan_constants(chunk, heads)
-    bias = jnp.broadcast_to(dt_bias[:, None], (heads, chunk))
-    rate = jnp.broadcast_to(-jnp.exp(a_log)[:, None], (heads, chunk))
-    skip_w = jnp.repeat(skip, HD)[None, :]
-    whole = lambda a: pl.BlockSpec(a.shape, lambda c: (0, 0))
-    rows = lambda w: pl.BlockSpec((chunk, w), lambda c: (c, 0))
-    hbm = pl.BlockSpec(memory_space=pl.ANY)
-    dma = pltpu.SemaphoreType.DMA
-    sds = jax.ShapeDtypeStruct
-    pieces = 8
-    ways = dp_n - 1
-    return pl.pallas_call(
-        functools.partial(scan_fwd_kernel, heads, dp_n),
-        grid=(blocks,),
-        in_specs=[pl.BlockSpec((1, 8, chunk), lambda c: (c, 0, 0)), rows(inner), rows(pbd.shape[1])]
-        + [whole(a) for a in (conv_x, conv_bc, bias, rate, skip_w, upper, spread)]
-        + [hbm] * 3,
-        out_specs=[rows(inner), pl.BlockSpec((1, bc // 2, inner), lambda c: (c, 0, 0))] + [hbm] * 3,
-        scratch_shapes=[
-            pltpu.VMEM((bc // 2, inner), F32),
-            pltpu.VMEM((chunk + 8, inner), F32),
-            pltpu.VMEM((chunk + 8, bc), F32),
-            dma((3,)), dma((1,)), dma((1,)), dma((pieces,)), dma((pieces,)), dma((pieces,)), dma((pieces,)),
-            dma((4, ways)), dma((4, ways)),
-        ],
-        out_shape=[
-            sds((tokens, inner), F32), sds((blocks, bc // 2, inner), BF),
-            sds((4,) + cot.shape, BF), sds((w_z.shape[0] * dp_n, inner), BF), sds((w_z.shape[0] * dp_n, inner), BF),
-        ],
-        compiler_params=pltpu.CompilerParams(
-            collective_id=3, has_side_effects=True, vmem_limit_bytes=48 * 2**20
-        ),
-        name="scan_forward",
-    )(meta, px, pbd, conv_x, conv_bc, bias, rate, skip_w, upper, spread, cot, w_z, w_out)
+    return y, enter_b
 
 
 def gate_kernel(
-    dp_n, normed, rows_z, rows_out, parts, y, gain, pz, ggn, grad_t, sums, h_send, h_recv, s_h, r_h,
+    dp_n, normed, rows_z, rows_out, parts, y, vec, pz, ggn, grad_t, sums, h_send, h_recv, s_h, r_h,
 ):
     i = pl.program_id(0)
     who = peers(dp_n)
@@ -321,7 +205,7 @@
         grad_t[k * quarter : (k + 1) * quarter, :] = jnp.transpose(parts[k])
     gated = y[...] * (z * sigmoid(z))
     ones = jnp.ones((8, gated.shape[1]), BF)
-    for k, value in enumerate((gated * gated, gated * gain[...] * g)):
+    for k, value in enumerate((gated * gated, gated * vec[5:6, : gated.shape[1]] * g)):
         row = nt(ones, value.astype(BF))
         for j in range(span // chunk):
             h_send[k, pl.ds(i * (span // chunk) + j, 1), :] = row[0:1, j * chunk : (j + 1) * chunk]
@@ -337,7 +221,7 @@
         sums[...] = h_send[...] + h_recv[0] + h_recv[1] + h_recv[2]
 
 
-def gate(dp_n, blocks, normed, rows_z, rows_out, parts, y, gain):
+def gate(dp_n, blocks, normed, rows_z, rows_out, parts, y, vec):
     count, width = normed.shape
     inner = y.shape[1]
     chunk = count // blocks
@@ -352,7 +236,7 @@
         grid=(steps,),
         in_specs=[
             rows(width), whole(rows_z), whole(rows_out),
-            pl.BlockSpec((4, span, quarter), lambda i: (0, i, 0)), rows(inner), whole(gain),
+            pl.BlockSpec((4, span, quarter), lambda i: (0, i, 0)), rows(inner), whole(vec),
         ],
         out_specs=[
             rows(inner), rows(inner), pl.BlockSpec((width, span), lambda i: (0, i)),
@@ -369,30 +253,29 @@
             collective_id=4, has_side_effects=True, vmem_limit_bytes=48 * 2**20
         ),
         name="gate",
-    )(normed, rows_z, rows_out, parts, y, gain)
+    )(normed, rows_z, rows_out, parts, y, vec)
 
 
 def scan_bwd_kernel(
-    heads, total_inner, starts, fill, ggn, y, pz, px, px_halo, pbd, pbd_halo, sin, rows, gain, convx, convbc,
-    bias, rate, skip, upper, spread, gather, ones_h,
-    lpx, lpz, lpbd, gn, acc_x, acc_bc, acc_s, dstate, extx, extb, dux, dub,
+    heads, total_inner, taps_n, bc, ggn, y, pz, px, px_halo, pbd, pbd_halo, sin, rows, vec,
+    lpx, lpz, lpbd, gn, acc, dstate, extx, extb, dux, dub, acc_x, acc_bc, acc_s, upper, spread, gather, ones_h,
 ):
     i = pl.program_id(0)
     blocks = pl.num_programs(0)
     c = blocks - 1 - i
     chunk, inner = px.shape
-    bc = convbc.shape[1]
     ns = bc // 2
-    taps_n = convx.shape[0]
-    keep = starts[c] == 0
-    nxt = jnp.minimum(c + 1, blocks - 1)
-    keep_next = jnp.logical_and(starts[nxt] == 0, i > 0)
-    n_live = fill[c]
+    par = read_vec(vec, heads, chunk, inner, bc, taps_n)
+    keep, n_live, keep_next = read_block(vec, c, chunk)
+    taps, taps_b, bias, rate, skip, gain = (par[k] for k in ("convx", "convbc", "bias", "rate", "skip", "gain"))
 
     @pl.when(i == 0)
     def _():
         for ref in (dstate, dux, dub, acc_x, acc_bc, acc_s):
             ref[...] = jnp.zeros_like(ref)
+        set_upper(upper)
+        set_spread(spread, heads)
+        set_gather(gather, ones_h, heads)
 
     moved = jnp.transpose(
         jnp.concatenate(
@@ -407,20 +290,18 @@
     yv = y[...]
     gated = yv * silu_z
     g = ggn[...]
-    d_gated = inv * (g * gain[...]) - gated * coef
+    d_gated = inv * (g * gain) - gated * coef
     lpz[...] = (d_gated * yv * (sz * (1.0 + z * (1.0 - sz)))).astype(BF)
     dy = d_gated * silu_z
-    gn[...] = (gated * inv * gain[...]).astype(BF)
+    gn[...] = (gated * inv * gain).astype(BF)
     acc_x[taps_n : taps_n + 1, :] += jnp.sum(g * gated * inv, axis=0, keepdims=True)
 
     extx[0:8, :] = jnp.where(keep, px_halo[...], 0.0)
     extb[0:8, :] = jnp.where(keep, pbd_halo[:, :bc], 0.0)
     extx[8 : chunk + 8, :] = px[...]
     extb[8 : chunk + 8, :] = pbd[:, :bc]
-    taps = convx[...]
-    taps_b = convbc[...]
-    live_x = (iota2(chunk, inner, 0) < n_live).astype(F32)
-    live_b = (iota2(chunk, bc, 0) < n_live).astype(F32)
+    live_x = (iota2(chunk, inner, 0).astype(F32) < n_live).astype(F32)
+    live_b = (iota2(chunk, bc, 0).astype(F32) < n_live).astype(F32)
     u = conv_from(extx, taps, chunk, 8)
     su = sigmoid(u)
     x = u * su * live_x
@@ -431,7 +312,7 @@
     db_du = sb * (1.0 + ub * (1.0 - sb)) * live_b
     b, cc = act[:, :ns], act[:, ns:]
 
-    pre, live, dt, run = dt_rows(pbd[:, bc:], bias[...], rate[...], n_live, heads, upper[...])
+    pre, live, dt, run = dt_rows(pbd[:, bc:], bias, rate, n_live, heads, upper[...])
     cols, wide = spread_all(run, dt, heads, chunk, spread[...])
     dt_w, ein_w, eout_w = wide[:, :inner], wide[:, inner : 2 * inner], wide[:, 2 * inner :]
     xd = x * dt_w
@@ -495,15 +376,18 @@
     kept = jnp.sum(enter_b.astype(F32) * d_state, axis=0, keepdims=True) * decay
     kept_hi, kept_lo = split2(kept)
     kept_two = jnp.concatenate([kept_hi, kept_lo, jnp.zeros((6, inner), F32)], axis=0).astype(BF)
-    kept_cols = nt(gather[3][:, :inner], kept_two)
-    d_last = whole_q2 + kept_cols[:heads, 0:1] + kept_cols[:heads, 1:2]
+    kept_rows = nn(kept_two, gather[0])
+    kept_cols = jnp.transpose(
+        jnp.concatenate([kept_rows[0:1] + kept_rows[1:2], jnp.zeros((chunk - 1, chunk), F32)], axis=0)
+    )
+    d_last = whole_q2 + kept_cols[:heads, 0:1]
     hi, mid, low = split3(d_run)
     back = nt(jnp.concatenate([hi, mid, low], axis=0).astype(BF), upper[...])
     d_a = back[:heads] + back[heads : 2 * heads] + back[2 * heads :] + d_last
-    d_dt = dt_direct + d_a * rate[...]
+    d_dt = dt_direct + d_a * rate
     d_pre = d_dt * live * sigmoid(pre)
     acc_s[0:heads, :] += d_pre
-    acc_s[heads : 2 * heads, :] += d_a * dt * rate[...]
+    acc_s[heads : 2 * heads, :] += d_a * dt * rate
 
     def conv_back(d_u, du_ref, ext_ref, tap_values, acc):
         du_ref[chunk : chunk + 8, :] = jnp.where(keep_next, du_ref[0:8, :], 0.0)
@@ -518,93 +402,62 @@
             )
         return out
 
-    d_x = d_xd * dt_w + skip[...] * dy
+    d_x = d_xd * dt_w + skip * dy
     lpx[...] = conv_back(d_x * dx_du, dux, extx, taps, acc_x).astype(BF)
     d_act = jnp.concatenate([d_b, d_cb], axis=1)
     lpbd[:, :bc] = conv_back(d_act * db_du, dub, extb, taps_b, acc_bc).astype(BF)
     pad = jnp.concatenate([d_pre, jnp.zeros((chunk - heads, chunk), F32)], axis=0)
     lpbd[:, bc:] = jnp.transpose(pad).astype(BF)
 
-
-def scan_backward(
-    ggn, y, pz, px, pbd, sin, rows, gain, conv_x, conv_bc, dt_bias, a_log, skip, starts, fill, total_inner
-):
+    @pl.when(i == blocks - 1)
+    def _():
+        acc[...] = jnp.zeros_like(acc)
+        for k in range(taps_n):
+            acc[1:2, k * bc : (k + 1) * bc] = acc_bc[k : k + 1, :]
+        per = acc.shape[1] // inner
+        for k in range(taps_n + 1):
+            acc[2 + k // per : 3 + k // per, (k % per) * inner : (k % per + 1) * inner] = acc_x[k : k + 1, :]
+        per_head = jnp.sum(
+            jnp.transpose(jnp.concatenate([acc_s[...], jnp.zeros((chunk - 2 * heads, chunk), F32)], axis=0)),
+            axis=0, keepdims=True,
+        )
+        three = jnp.concatenate(split3(acc_x[taps_n + 1 : taps_n + 2, :]) + (jnp.zeros((5, inner), F32),), axis=0)
+        skips = jnp.sum(nn(three.astype(BF), gather[2]), axis=0, keepdims=True)
+        acc[5:6, 0:chunk] = per_head + skips
+
+
+def scan_backward(ggn, y, pz, px, pbd, sin, rows, vec, heads, taps, bc, total_inner):
     tokens, inner = px.shape
-    blocks = starts.shape[0]
+    blocks = sin.shape[0]
     chunk = tokens // blocks
-    heads = inner // HD
-    bc = conv_bc.shape[1]
-    upper, spread, gather = scan_constants(chunk, heads)
-    selector = np.zeros((1, inner, chunk), np.float32)
-    lanes = np.zeros((chunk, inner), np.float32)
-    for h in range(heads):
-        lanes[h, h * HD : (h + 1) * HD] = 1.0
-    ones_h = np.zeros((heads * chunk, chunk), np.float32)
-    for h in range(heads):
-        ones_h[h * chunk : (h + 1) * chunk, heads + h] = 1.0
-    ones_h = jnp.asarray(ones_h, BF)
-    lanes = jnp.asarray(lanes, BF)
-    bias = jnp.broadcast_to(dt_bias[:, None], (heads, chunk))
-    rate = jnp.broadcast_to(-jnp.exp(a_log)[:, None], (heads, chunk))
-    skip_w = jnp.repeat(skip, HD)[None, :]
-    whole = lambda a: pl.BlockSpec(a.shape, lambda i, *_: (0,) * a.ndim)
-    back = lambda w: pl.BlockSpec((chunk, w), lambda i, *_: (blocks - 1 - i, 0))
-    halo = lambda w: pl.BlockSpec(
-        (8, w), lambda i, *_: (jnp.maximum((blocks - 1 - i) * (chunk // 8) - 1, 0), 0)
-    )
+    whole = lambda a: pl.BlockSpec(a.shape, lambda i: (0,) * a.ndim)
+    back = lambda w: pl.BlockSpec((chunk, w), lambda i: (blocks - 1 - i, 0))
+    halo = lambda w: pl.BlockSpec((8, w), lambda i: (jnp.maximum((blocks - 1 - i) * (chunk // 8) - 1, 0), 0))
     width = pbd.shape[1]
-    consts = (gain[None, :], conv_x, conv_bc, bias, rate, skip_w, upper, spread, gather, lanes, ones_h)
-
-    def kernel(*refs):
-        n_in = 2 + 9
-        ins, cons, rest = refs[:n_in], refs[n_in : n_in + 11], refs[n_in + 11 :]
-        gain_r, cx, cb, bias_r, rate_r, skip_r, up, sp, ga, la, on = cons
-
-        class Gather:
-            def __getitem__(self, k):
-                return la[...] if k == 3 else ga[k]
-
-        scan_bwd_kernel(
-            heads, total_inner, *ins, gain_r, cx, cb, bias_r, rate_r, skip_r, up, sp, Gather(), on, *rest
-        )
-
+    vm, sds = pltpu.VMEM, jax.ShapeDtypeStruct
     return pl.pallas_call(
-        kernel,
-        grid_spec=pltpu.PrefetchScalarGridSpec(
-            num_scalar_prefetch=2,
-            grid=(blocks,),
-            in_specs=[
-                back(inner), back(inner), back(inner), back(inner), halo(inner), back(width), halo(width),
-                pl.BlockSpec((1, bc // 2, inner), lambda i, *_: (blocks - 1 - i, 0, 0)),
-                pl.BlockSpec(rows.shape, lambda i, *_: (0, 0, 0)),
-            ]
-            + [whole(a) for a in consts],
-            out_specs=[
-                back(inner), back(inner), back(width), back(inner),
-                pl.BlockSpec((8, inner), lambda i, *_: (0, 0)),
-                pl.BlockSpec((8, bc), lambda i, *_: (0, 0)),
-                pl.BlockSpec((2 * heads, chunk), lambda i, *_: (0, 0)),
-            ],
-            scratch_shapes=[
-                pltpu.VMEM((bc // 2, inner), F32),
-                pltpu.VMEM((chunk + 8, inner), F32),
-                pltpu.VMEM((chunk + 8, bc), F32),
-                pltpu.VMEM((chunk + 8, inner), F32),
-                pltpu.VMEM((chunk + 8, bc), F32),
-            ],
-        ),
+        functools.partial(scan_bwd_kernel, heads, total_inner, taps, bc),
+        grid=(blocks,),
+        in_specs=[
+            back(inner), back(inner), back(inner), back(inner), halo(inner), back(width), halo(width),
+            pl.BlockSpec((1, bc // 2, inner), lambda i: (blocks - 1 - i, 0, 0)), whole(rows), whole(vec),
+        ],
+        out_specs=[
+            back(inner), back(inner), back(width), back(inner), pl.BlockSpec((8, vec.shape[1]), lambda i: (0, 0)),
+        ],
+        scratch_shapes=[
+            vm((bc // 2, inner), F32), vm((chunk + 8, inner), F32), vm((chunk + 8, bc), F32),
+            vm((chunk + 8, inner), F32), vm((chunk + 8, bc), F32),
+            vm((8, inner), F32), vm((8, bc), F32), vm((2 * heads, chunk), F32),
+            vm((chunk, chunk), BF), vm((chunk, 3 * inner), BF), vm((3, inner, chunk), BF), vm((heads * chunk, chunk), BF),
+        ],
         out_shape=[
-            jax.ShapeDtypeStruct((tokens, inner), BF),
-            jax.ShapeDtypeStruct((tokens, inner), BF),
-            jax.ShapeDtypeStruct((tokens, width), BF),
-            jax.ShapeDtypeStruct((tokens, inner), BF),
-            jax.ShapeDtypeStruct((8, inner), F32),
-            jax.ShapeDtypeStruct((8, bc), F32),
-            jax.ShapeDtypeStruct((2 * heads, chunk), F32),
+            sds((tokens, inner), BF), sds((tokens, inner), BF), sds((tokens, width), BF), sds((tokens, inner), BF),
+            sds((8, vec.shape[1]), F32),
         ],
         compiler_params=pltpu.CompilerParams(vmem_limit_bytes=48 * 2**20),
         name="scan_backward",
-    )(starts, fill, ggn, y, pz, px, px, pbd, pbd, sin, rows, *consts)
+    )(ggn, y, pz, px, px, pbd, pbd, sin, rows, vec)
 def peers(dp_n):
     dp, hm = lax.axis_index("dp"), lax.axis_index("heads")
     across, core = hm // 2, hm % 2
@@ -645,7 +498,7 @@
 def tail_kernel(
     dp_n, units,
     grad_t_in, gn_in, rows_out_in, normed_t_in, lpz_in, rows_z_in, lpx_in, rows_x_in, lpbd_in, rows_bd_in, normed_in,
-    tokens, acc_x, acc_bc, acc_s, cot, q_wide, gain,
+    tokens, acc, cot, q_wide, vec,
     block_out, grad_tokens, g_x, g_z, g_out, g_bc, small_out,
     sib_send, sib_recv, x_send, x_recv, part, held,
     y_send, y_recv, z_send, z_recv, g_own, yb_send, yb_recv, zb_send, zb_recv, gb_own, bh_send, bh_recv,
@@ -668,13 +521,11 @@
     count = normed.shape[0]
     width = normed.shape[1]
     inner = lpx.shape[1]
-    bc = acc_bc.shape[1]
+    bc = 2 * bh_send.shape[1]
     quarter = width // 4
     span = count // units
     block = width // dp_n
     lines = who["lines"]
-    heads = acc_s.shape[0] // 2
-    taps_rows = acc_x.shape[0]
 
     def copy_sib(u):
         return push(sib_send.at[u], sib_recv.at[u], s_sib.at[u], r_sib.at[u], who["sib"])
@@ -732,7 +583,7 @@
                 coef = q * q * (dots / width)
                 grad_tokens[at, :] = (
                     cot[at, :].astype(F32)
-                    + q[:, 0:1] * gain[:, cols] * total[j * lanes : (j + 1) * lanes]
+                    + q[:, 0:1] * vec[6:7, cols] * total[j * lanes : (j + 1) * lanes]
                     - tokens[at, :].astype(F32) * coef[:, 0:1]
                 )
 
@@ -855,7 +706,6 @@
         g_bc[:, half:] = jnp.where(first, theirs, mine)
 
     three = (("sib", 4), ("xn", 5), ("dg", 6))
-    taps = width // bc
     token_rows = count // width
 
     def copy_h(k):
@@ -863,8 +713,7 @@
         return push(h_send, h_recv.at[k], s_m.at[sem], r_m.at[sem], who[name])
 
     def small_a():
-        for k in range(taps):
-            h_send[1:2, k * bc : (k + 1) * bc] = acc_bc[k : k + 1, :]
+        h_send[1:2, :] = acc[1:2, :]
         for k in range(3):
             copy_h(k).start()
 
@@ -901,16 +750,8 @@
             copy_h(k).wait()
         over_heads = h_send[...] + h_recv[0] + h_recv[1] + h_recv[2]
         row_sums[0:token_rows, :] = over_heads[2 : 2 + token_rows, :]
-        sy_send[...] = jnp.zeros_like(sy_send)
         sy_send[0:2, :] = over_heads[0:2, :]
-        per = width // inner
-        for k in range(taps + 2):
-            sy_send[2 + k // per : 3 + k // per, (k % per) * inner : (k % per + 1) * inner] = acc_x[k : k + 1, :]
-        lanes = acc_s.shape[1]
-        at = 2 + -(-(taps + 2) // per)
-        fit = width // lanes
-        for k in range(2 * heads):
-            sy_send[at + k // fit : at + k // fit + 1, (k % fit) * lanes : (k % fit + 1) * lanes] = acc_s[k : k + 1, :]
+        sy_send[2:8, :] = acc[2:8, :]
         copy_sy().start()
 
     def small_c():
@@ -953,10 +794,9 @@
     seq((small_d,), (head_c, 6), (grad_c, 4), (bc_f,), (head_c, 7), (grad_c, 5))
 
 
-def tail(dp_n, units, normed_t, normed, grad_t, gn, lpx, lpz, lpbd, rows_x, rows_z, rows_bd, rows_out, tokens, acc_x, acc_bc, acc_s, cot, q_wide, gain):
+def tail(dp_n, units, normed_t, normed, grad_t, gn, lpx, lpz, lpbd, rows_x, rows_z, rows_bd, rows_out, tokens, acc, cot, q_wide, vec, bc):
     count, width = normed.shape
     inner = lpx.shape[1]
-    bc = acc_bc.shape[1]
     quarter = width // 4
     span = count // units
     block = width // dp_n
@@ -966,8 +806,7 @@
     vm = pltpu.VMEM
     dma = pltpu.SemaphoreType.DMA
     operands = (
-        grad_t, gn, rows_out, normed_t, lpz, rows_z, lpx, rows_x, lpbd, rows_bd, normed, tokens, acc_x, acc_bc, acc_s,
-        cot, q_wide, gain,
+        grad_t, gn, rows_out, normed_t, lpz, rows_z, lpx, rows_x, lpbd, rows_bd, normed, tokens, acc, cot, q_wide, vec,
     )
     sds = jax.ShapeDtypeStruct
     spec = pl.BlockSpec(memory_space=pltpu.VMEM)
@@ -978,7 +817,7 @@
             sds((block, inner), F32), sds((block, inner), F32), sds((block, inner), F32), sds((block, bc), F32),
             sds((24, width), F32),
         ],
-        in_specs=[pl.BlockSpec(memory_space=pl.ANY)] * 11 + [spec] * 7,
+        in_specs=[pl.BlockSpec(memory_space=pl.ANY)] * 11 + [spec] * 5,
         out_specs=[spec] * 7,
         scratch_shapes=[
             vm((2 * units, 2, span, quarter), BF), vm((2 * units, 2, span, quarter), BF),
@@ -1037,30 +876,37 @@
 
 
 def front_kernel(
-    dp_n, units,
-    tokens, w_bd, w_x, gain,
-    px_out, pbd_out, normed_out, normed_t_out, q_out, rows_x, rows_bd,
-    tok, wx, wbd, px, pbd, normed, normed_t, q,
-    s_loc, s_sib, r_sib, s_x, r_x, s_f, r_f, s_b, r_b, s_w, r_w, s_out,
+    dp_n, heads, units, taps, bc,
+    tokens, cot, w_x, w_bd, w_z, w_out, vec,
+    px_out, pbd_out, normed_out, normed_t_out, q_out, y_out, sin_out, parts, rows_x, rows_bd, rows_z, rows_out,
+    tok, wx, wbd, px, pbd, normed, normed_t, q, y, sin, state, extx, extb, upper, spread,
+    s_loc, s_sib, r_sib, s_x, r_x, s_f, r_f, s_cx, r_cx, s_cf, r_cf, s_w, r_w, s_out, s_y,
 ):
     who = peers(dp_n)
     count, quarter = tokens.shape
     width = 4 * quarter
     span = count // units
     lines = who["lines"]
-    block = w_x.shape[0]
+    block, inner = w_x.shape
+    blocks = sin.shape[0]
+    chunk = count // blocks
+    per = blocks // units
+    pieces = s_cx.shape[0]
+    cot_span = count // pieces
     here = pl.ds(pl.multiple_of(who["dp"] * block, block), block)
     local = [
-        pltpu.make_async_copy(tokens, tok.at[who["mine"]], s_loc.at[0]),
-        pltpu.make_async_copy(w_bd, wbd.at[here], s_loc.at[1]),
-        pltpu.make_async_copy(w_x, wx.at[here], s_loc.at[2]),
+        pltpu.make_async_copy(src, dst, s_loc.at[k])
+        for k, (src, dst) in enumerate((
+            (tokens, tok.at[who["mine"]]), (w_x, wx.at[here]), (w_bd, wbd.at[here]),
+            (w_z, rows_z.at[here]), (w_out, rows_out.at[here]), (cot, parts.at[who["mine"]]),
+        ))
     ]
-    for copy in local:
+    for copy in local[:3]:
         copy.start()
     meet(who)
 
-    def rows(s):
-        return pl.ds(s * span, span)
+    def rows(s, n=span):
+        return pl.ds(pl.multiple_of(s * n, n), n)
 
     def to_x(s):
         return push(tokens.at[rows(s)], tok.at[who["mine"], rows(s)], s_x.at[s], r_x.at[s], who["xn"])
@@ -1069,126 +915,238 @@
         return push(tokens, tok.at[who["mine"]], s_sib.at[0], r_sib.at[0], who["sib"])
 
     def forward(s):
-        here = tok.at[who["other"], rows(s)]
-        return push(here, here, s_f.at[s], r_f.at[s], who["sib"])
-
-    every = slice(None)
-    bd_own, bd_along, bd_onward = shares(w_bd, wbd, dp_n, every, s_b, r_b, who)
-    x_own, x_along, x_onward = shares(w_x, wx, dp_n, every, s_w, r_w, who)
+        at = tok.at[who["other"], rows(s)]
+        return push(at, at, s_f.at[s], r_f.at[s], who["sib"])
+
+    def cot_x(j):
+        at = rows(j, cot_span)
+        return push(cot.at[at], parts.at[who["mine"], at], s_cx.at[j], r_cx.at[j], who["xn"])
+
+    def cot_sib():
+        return push(cot, parts.at[who["mine"]], s_sib.at[1], r_sib.at[1], who["sib"])
+
+    def cot_forward(j):
+        at = parts.at[who["other"], rows(j, cot_span)]
+        return push(at, at, s_cf.at[j], r_cf.at[j], who["sib"])
+
+    half = inner // 2
+    cuts = [
+        shares(ref, to, dp_n, cols, s_w.at[n], r_w.at[n], who)
+        for n, (ref, to, cols) in enumerate((
+            (w_x, wx, pl.ds(0, half)), (w_x, wx, pl.ds(half, half)), (w_bd, wbd, slice(None)),
+            (w_z, rows_z, pl.ds(0, half)), (w_z, rows_z, pl.ds(half, half)),
+            (w_out, rows_out, pl.ds(0, half)), (w_out, rows_out, pl.ds(half, half)),
+        ))
+    ]
+
+    def offer(n):
+        own, along, onward = cuts[n]
+        loop_line(lines, lambda k: along(k).start())
+        own().start()
+
+    def pass_rows(n):
+        own, along, onward = cuts[n]
+
+        def one(k):
+            along(k).wait()
+            onward(k).start()
+
+        loop_line(lines, one)
+
+    def have(n):
+        own, along, onward = cuts[n]
+        own().wait()
+        loop_line(lines, lambda k: onward(k).wait())
+
+    def pass_cot(j):
+        cot_x(j).wait()
+        cot_forward(j).start()
+
     to_x(0).start()
-    loop_line(lines, lambda k: bd_along(k).start())
-    bd_own().start()
+    offer(0)
     for s in range(1, units):
         to_x(s).start()
     to_sib().start()
-    loop_line(lines, lambda k: x_along(k).start())
-    x_own().start()
-
-    def pass_on(along, onward, k):
-        along(k).wait()
-        onward(k).start()
+    for n in (1, 2):
+        offer(n)
+    for j in range(pieces):
+        cot_x(j).start()
+    for n in (3, 4, 5, 6):
+        offer(n)
+    set_upper(upper)
+    set_spread(spread, heads)
+    state[...] = jnp.zeros_like(state)
+    extx[...] = jnp.zeros_like(extx)
+    extb[...] = jnp.zeros_like(extb)
+    par = read_vec(vec, heads, chunk, inner, bc, taps)
+    gain = vec[6:7, :width]
+
+    def out_copies(s):
+        at = rows(s)
+        every = slice(None)
+        return [
+            pltpu.make_async_copy(ref.at[to], out.at[to], s_out.at[n, s])
+            for n, (ref, out, to) in enumerate((
+                (normed, normed_out, (at,)), (normed_t, normed_t_out, (every, at)), (q, q_out, (at,)),
+                (px, px_out, (at,)), (pbd, pbd_out, (at,)),
+            ))
+        ]
 
     def norm(s):
-        at = slice(s * span, (s + 1) * span)
-        parts = [tok[h, at, :].astype(F32) for h in range(4)]
-        total = sum(jnp.sum(p * p, axis=1, keepdims=True) for p in parts)
+        at = rows(s)
+        values = [tok[h, at, :].astype(F32) for h in range(4)]
+        total = sum(jnp.sum(p * p, axis=1, keepdims=True) for p in values)
         inv = lax.rsqrt(total / width + EPS)
         q[at, :] = jnp.broadcast_to(inv, (span, q.shape[1]))
         for h in range(4):
             cols = slice(h * quarter, (h + 1) * quarter)
-            value = (parts[h] * inv * gain[:, cols]).astype(BF)
+            value = (values[h] * inv * gain[:, cols]).astype(BF)
             normed[at, cols] = value
             normed_t[cols, at] = jnp.transpose(value)
-
-    def outward(ref, out, i, at):
-        return pltpu.make_async_copy(ref.at[at], out.at[at], s_out.at[i])
-
-    def send_norm(s):
-        at = (slice(s * span, (s + 1) * span),)
-        copies = [
-            outward(normed, normed_out, 3 * s, at),
-            outward(normed_t, normed_t_out, 3 * s + 1, (slice(None),) + at),
-            outward(q, q_out, 3 * s + 2, at),
-        ]
-        return copies
+        for copy in out_copies(s)[:3]:
+            copy.start()
 
     def project(s):
-        at = slice(s * span, (s + 1) * span)
+        at = rows(s)
         pbd[at, :] = nn(normed[at, :], wbd[...])
         px[at, :] = nn(normed[at, :], wx[...])
-
-    def send_proj(s):
-        at = (slice(s * span, (s + 1) * span),)
-        base = 3 * units + 2 * s
-        return [outward(px, px_out, base, at), outward(pbd, pbd_out, base + 1, at)]
-
-    outs = []
-
-    def go(copies):
-        for copy in copies:
+        for copy in out_copies(s)[3:]:
             copy.start()
-        outs.extend(copies)
 
     local[0].wait()
     to_x(0).wait()
     forward(0).start()
-    loop_line(lines, lambda k: pass_on(bd_along, bd_onward, k))
+    pass_rows(0)
     to_sib().wait()
-    for s in range(units):
+    forward(0).wait()
+    norm(0)
+    to_x(1).wait()
+    forward(1).start()
+    pass_rows(1)
+    forward(1).wait()
+    norm(1)
+    pass_rows(2)
+    to_x(2).wait()
+    forward(2).start()
+    for copy in local[3:]:
+        copy.start()
+    cot_sib().start()
+    forward(2).wait()
+    norm(2)
+    for copy in local[1:3]:
+        copy.wait()
+    for n in (0, 1, 2):
+        have(n)
+    keep_rows = [
+        pltpu.make_async_copy(wx, rows_x, s_loc.at[6]), pltpu.make_async_copy(wbd, rows_bd, s_loc.at[7]),
+    ]
+    for copy in keep_rows:
+        copy.start()
+
+    def last_tokens(s):
+        to_x(s).wait()
+        forward(s).start()
+
+    def last_norm(s):
         forward(s).wait()
         norm(s)
-        go(send_norm(s))
-        if s + 1 < units:
-            to_x(s + 1).wait()
-            forward(s + 1).start()
-        if s == 1:
-            bd_own().wait()
-            loop_line(lines, lambda k: bd_onward(k).wait())
-            local[1].wait()
-            copy = pltpu.make_async_copy(wbd, rows_bd, s_out.at[5 * units])
-            go([copy])
-        if s == units - 2:
-            loop_line(lines, lambda k: pass_on(x_along, x_onward, k))
-    x_own().wait()
-    loop_line(lines, lambda k: x_onward(k).wait())
-    local[2].wait()
-    go([pltpu.make_async_copy(wx, rows_x, s_out.at[5 * units + 1])])
+
+    events = {1: [(last_tokens, units - 1)], 2: [(last_norm, units - 1)]}
+    late = []
+    plan = [(pass_rows, 3, 4), (pass_rows, 4, 8), (pass_rows, 5, 12)]
+    plan += [(pass_cot, j, 5 + 2 * j) for j in range(pieces)] + [(pass_rows, 6, blocks)]
+    for fn, k, at in plan:
+        if at < blocks:
+            events.setdefault(at, []).append((fn, k))
+        else:
+            late.append((fn, k))
+
+    def y_copies(c):
+        at = rows(c, chunk)
+        return (
+            pltpu.make_async_copy(y.at[at], y_out.at[at], s_y.at[0, c]),
+            pltpu.make_async_copy(sin.at[c], sin_out.at[c], s_y.at[1, c]),
+        )
+
+    def step(c, carry):
+        for at, fns in events.items():
+
+            @pl.when(c == at)
+            def _(fns=fns):
+                for fn, k in fns:
+                    fn(k)
+
+        @pl.when(c % per == 0)
+        def _():
+            project(c // per)
+
+        at = rows(c, chunk)
+        y_c, enter = scan_step(
+            heads, par, read_block(vec, c, chunk), px.at[at], pbd.at[at], upper, spread, state, extx, extb
+        )
+        y[at, :] = y_c
+        sin[c] = enter
+        for copy in y_copies(c):
+            copy.start()
+        return carry
+
+    lax.fori_loop(0, blocks, step, 0)
+    for fn, k in late:
+        fn(k)
+
+    def end_y(c, carry):
+        for copy in y_copies(c):
+            copy.wait()
+        return carry
+
+    lax.fori_loop(0, blocks, end_y, 0)
     for s in range(units):
-        project(s)
-        go(send_proj(s))
-    for copy in outs:
+        for copy in out_copies(s):
+            copy.wait()
+    for copy in local[3:] + keep_rows:
         copy.wait()
-
-
-def front(dp_n, units, tokens, w_bd, w_x, gain):
+    cot_sib().wait()
+    for j in range(pieces):
+        cot_forward(j).wait()
+    for n in (3, 4, 5, 6):
+        have(n)
+
+
+def front(dp_n, heads, taps, bc, blocks, tokens, cot, w_x, w_bd, w_z, w_out, vec):
     count, quarter = tokens.shape
     width = 4 * quarter
     inner, wide = w_x.shape[1], w_bd.shape[1]
+    chunk = count // blocks
+    units, pieces = 4, 8
     vm, dma, sds = pltpu.VMEM, pltpu.SemaphoreType.DMA, jax.ShapeDtypeStruct
     hbm = pl.BlockSpec(memory_space=pl.ANY)
-    lines = dp_n // 2
-    ways = 2 * lines - 1
+    ways = dp_n - 1
     outs = [
         sds((count, inner), F32), sds((count, wide), F32), sds((count, width), BF), sds((width, count), BF),
-        sds((count, 128), F32), sds((width, inner), BF), sds((width, wide), BF),
+        sds((count, 128), F32), sds((count, inner), F32), sds((blocks, bc // 2, inner), BF),
+        sds((4, count, quarter), BF), sds((width, inner), BF), sds((width, wide), BF), sds((width, inner), BF),
+        sds((width, inner), BF),
     ]
     return pl.pallas_call(
-        functools.partial(front_kernel, dp_n, units),
+        functools.partial(front_kernel, dp_n, heads, units, taps, bc),
         out_shape=outs,
-        in_specs=[hbm] * 3 + [pl.BlockSpec(memory_space=pltpu.VMEM)],
-        out_specs=[hbm] * 7,
+        in_specs=[hbm] * 6 + [pl.BlockSpec(memory_space=pltpu.VMEM)],
+        out_specs=[hbm] * len(outs),
         scratch_shapes=[
             vm((4, count, quarter), BF), vm((width, inner), BF), vm((width, wide), BF),
             vm((count, inner), F32), vm((count, wide), F32), vm((count, width), BF), vm((width, count), BF),
-            vm((count, 128), F32),
-            dma((3,)), dma((1,)), dma((1,)), dma((units,)), dma((units,)), dma((units,)), dma((units,)),
-            dma((ways,)), dma((ways,)), dma((ways,)), dma((ways,)), dma((5 * units + 2,)),
+            vm((count, 128), F32), vm((count, inner), F32), vm((blocks, bc // 2, inner), BF),
+            vm((bc // 2, inner), F32), vm((chunk + 8, inner), F32), vm((chunk + 8, bc), F32),
+            vm((chunk, chunk), BF), vm((chunk, 3 * inner), BF),
+            dma((8,)), dma((2,)), dma((2,)), dma((units,)), dma((units,)), dma((units,)), dma((units,)),
+            dma((pieces,)), dma((pieces,)), dma((pieces,)), dma((pieces,)),
+            dma((7, ways)), dma((7, ways)), dma((5, units)), dma((2, blocks)),
         ],
         compiler_params=pltpu.CompilerParams(
             collective_id=2, has_side_effects=True, vmem_limit_bytes=58 * 2**20
         ),
         name="front",
-    )(tokens, w_bd, w_x, gain)
+    )(tokens, cot, w_x, w_bd, w_z, w_out, vec)
 
 
 def body(
@@ -1205,45 +1163,28 @@
     chunk = count // blocks
     inner = w_x.shape[1]
     heads = w_dt.shape[1]
-    bc = w_bc.shape[1]
-    total_inner = inner * heads_n
+    taps, bc = conv_bc.shape
     w_bd = jnp.concatenate([w_bc, jnp.pad(w_dt, ((0, 0), (0, chunk - heads)))], axis=1)
-    px, pbd, normed, normed_t, q_wide, rows_x, rows_bd = front(dp_n, 4, tokens, w_bd, w_x, norm_gain[None, :])
-    keep = jnp.where(starts == 0, 1.0, 0.0).astype(F32)
-    meta = jnp.stack([keep, fill.astype(F32)] + [keep] * 6, axis=1)
-    meta = jnp.broadcast_to(meta[:, :, None], (blocks, 8, chunk))
-    y, sin, parts, rows_z, rows_out = scan_forward(
-        dp_n, px, pbd, conv_x, conv_bc, dt_bias, a_log, skip, meta, cotangent, w_z, w_out
+    vec = pack_vec(conv_x, skip, gate_gain, norm_gain, dt_bias, a_log, conv_bc, starts, fill, chunk)
+    px, pbd, normed, normed_t, q_wide, y, sin, parts, rows_x, rows_bd, rows_z, rows_out = front(
+        dp_n, heads, taps, bc, blocks, tokens, cotangent, w_x, w_bd, w_z, w_out, vec
     )
-    pz, ggn, grad_t, sums = gate(dp_n, blocks, normed, rows_z, rows_out, parts, y, gate_gain[None, :])
-    lpx, lpz, lpbd, gn, acc_x, acc_bc, acc_s = scan_backward(
-        ggn, y, pz, px, pbd, sin, sums, gate_gain, conv_x, conv_bc, dt_bias, a_log, skip, starts, fill,
-        total_inner,
+    pz, ggn, grad_t, sums = gate(dp_n, blocks, normed, rows_z, rows_out, parts, y, vec)
+    lpx, lpz, lpbd, gn, acc = scan_backward(
+        ggn, y, pz, px, pbd, sin, sums, vec, heads, taps, bc, inner * heads_n
     )
     block_out, grad_tokens, grad_w_x, grad_w_z, grad_w_out, grad_w_bc, small = tail(
         dp_n, 4, normed_t, normed, grad_t, gn, lpx, lpz, lpbd, rows_x, rows_z, rows_bd, rows_out,
-        tokens, acc_x, acc_bc, acc_s, cotangent, q_wide, norm_gain[None, :],
+        tokens, acc, cotangent, q_wide, vec, bc,
     )
+    block = width // dp_n
     own_gain = lax.dynamic_slice_in_dim(norm_gain, head_index * columns, columns, 0)
-    return (block_out, grad_tokens) + outputs(
-        small, dp_index, head_index, own_gain, conv_x, bc, heads, inner, width // dp_n, chunk,
-        grad_w_x, grad_w_z, grad_w_bc, grad_w_out,
-    )
-
-
-def outputs(small, dp_index, head_index, own_gain, conv_x, bc, heads, inner, block, chunk, g_x, g_z, g_bc, g_out):
-    taps = conv_x.shape[0]
-    width = small.shape[1]
-    columns = own_gain.shape[0]
+    gain_sum = lax.dynamic_slice_in_dim(small[0], head_index * columns, columns, 0)
     grad_w_dt = lax.dynamic_slice_in_dim(small[8 : 8 + heads], dp_index * block, block, 1).T
-    gain_sum = lax.dynamic_slice_in_dim(small[0], head_index * columns, columns, 0)
-    per = width // inner
-    scans = small[2 : 2 + -(-(taps + 2) // per)].reshape(-1, inner)
-    at = 2 + -(-(taps + 2) // per)
-    lanes = jnp.sum(small[at:8].reshape(-1, chunk)[: 2 * heads], axis=1)
     return (
-        gain_sum / own_gain, g_x, g_z, grad_w_dt, g_bc, scans[:taps], small[1].reshape(taps, bc), lanes[:heads],
-        lanes[heads:], jnp.sum(scans[taps + 1].reshape(heads, HD), axis=1), scans[taps], g_out,
+        block_out, grad_tokens, gain_sum / own_gain, grad_w_x, grad_w_z, grad_w_dt, grad_w_bc,
+        small[2:4].reshape(taps, inner), small[1].reshape(taps, bc), small[5, :heads], small[5, heads : 2 * heads],
+        small[5, 2 * heads : 3 * heads], small[4, :inner], grad_w_out,
     )
 
 

time: 249 us -> 247 us (level)
  Pallas kernels: 212 us -> 209 us
    pallas_call x3 -> x2, Pallas kernels: 122 us -> 115 us  [the longest x1 74.3 us: front(): pl.pallas_call(functools.partial(front_kernel, dp_n, heads, units, taps,...]
    unnamed x65 -> x29, local copies, waits for them, and re-layouts: 20.7 us -> 16.7 us
    concatenate x0 -> x1, local copies, waits for them, and re-layouts: none -> 3.2 us  [pack_vec(): return jnp.concatenate(rows, axis=0)]
    slice x8 -> x5, local copies, waits for them, and re-layouts: 5.03 us -> 3.76 us  [the longest x1 1.3 us: body(): small[4, :inner]]
where the time goes in v4:
time: 247 us; the launch traced here: 246 us
  Pallas kernels  209 us (85%)
  local copies, waits for them, and re-layouts  30.7 us (12%)
  other arithmetic  4.89 us (2%)
    pallas_call x1, Pallas kernels, tail(): pl.pallas_call(functools.partial(tail_kernel, dp_n, units), out_shape=[sd...  75.8 us
    pallas_call x1, Pallas kernels, front(): pl.pallas_call(functools.partial(front_kernel, dp_n, heads, units, taps,...  74.3 us
    pallas_call x1, Pallas kernels, scan_backward(): pl.pallas_call(functools.partial(scan_bwd_kernel, heads, total_inner, tap...  40.7 us
    pallas_call x1, Pallas kernels, gate(): pl.pallas_call(functools.partial(gate_kernel, dp_n), grid=(steps,), in_sp...  18.6 us
    unnamed x29, local copies, waits for them, and re-layouts  16.7 us

profile of v4, /device:TPU:0, one launch (start us, length us, event | category | flops | bytes accessed | tf_op | source)
XLA Modules:
  0.0 245.7 jit_solution(15324551959651128196)
XLA Ops:
  0.6 0.8 copy.30
  1.4 1.5 fusion.1.w_bd
  2.9 0.7 pad.32
  3.6 0.7 broadcast_in_dim.26
  4.4 0.1 broadcast_in_dim_reshape.3
  4.4 0.7 pad.34
  5.1 0.7 exponential_negate_fusion
  5.8 0.1 broadcast_in_dim.55
  5.9 0.7 broadcast_in_dim.54
  6.6 0.7 pad.51
  7.3 0.7 compare_select_fusion
  8.0 0.1 slice.27
  8.0 0.1 pad_maximum_fusion
  8.1 0.1 broadcast_in_dim.60
  8.2 0.7 convert_element_type.18
  8.8 0.1 broadcast_in_dim.59
  8.9 0.1 broadcast_in_dim.58
  9.0 3.2 %concatenate.19.vec = f32[40,1024]{1,0:T(8,128)} concatenate(f32[4,1024]{1,0:T(4,128)S(1)} %pad.32, f32[1,1024]{1,0:T(1,128)S(1)} %pad.33, f32[1,1024]{1,0:T(1,128)S(1)} %pad.34, f32[1,1024]{1,0:T(1,128)} %bitcast.12, f32[1,1024]{1,0:T(1,128)S(1)} %broadcast_in_dim.53, f32[8,1024]{1,0:T(8,128)S(1)} %select_maximum_fusion.2, f32[8,1024]{1,0:T(8,128)S(1)} %pad.51, ...), dimensions={0} | concatenate | bytes 327680 | tf_op jit(solution)/shard_map/concatenate | solution.py:139
  12.2 74.3 %front.1 = (f32[2048,512]{1,0:T(8,128)}, f32[2048,384]{1,0:T(8,128)}, bf16[2048,1024]{1,0:T(8,128)(2,1)}, bf16[1024,2048]{1,0:T(8,128)(2,1)}, f32[2048,128]{1,0:...) custom-call(bf16[2048,256]{1,0:T(8,128)(2,1)} %tokens.3, ...), custom_call_target="tpu_custom_call" | custom-call | tf_op jit(solution)/shard_map/front/pallas_call | solution.py:1130
  86.5 0.0 copy-start
  86.5 1.2 copy-done
  87.7 0.0 copy-start.1
  87.7 1.2 copy-done.1
  89.0 0.0 copy-start.2
  89.0 0.9 copy-done.2
  89.9 18.6 %gate.1 = (f32[2048,512]{1,0:T(8,128)}, f32[2048,512]{1,0:T(8,128)}, bf16[1024,2048]{1,0:T(8,128)(2,1)}, f32[2,16,128]{2,1,0:T(8,128)S(1)}) custom-call(bf16[2048,1024]{1,0:T(8,128)(2,1)} %get-tuple-element.42.normed.normed_in, bf16[1024,512]{1,0:T(8,128)(2,1)S(1)} %copy-done, bf16[1024,512]{1,0:T(8,128)(2,1)S(1)} %copy-done.1, ...), custom_call_target="tpu_custom_call" | custom-call | tf_op jit(solution)/shard_map/gate/pallas_call | solution.py:234
  108.5 40.7 %scan_backward.1 = (bf16[2048,512]{1,0:T(8,128)(2,1)S(1)}, bf16[2048,512]{1,0:T(8,128)(2,1)S(1)}, bf16[2048,384]{1,0:T(8,128)(2,1)S(1)}, bf16[2048,512]{1,0:T(8,128)(2,1)}, f32[8,1024]{1,0:T(8,128)S(1)}) custom-call(f32[2048,512]{1,0:T(8,128)} %get-tuple-element.48.ggn, f32[2048,512]{1,0:T(8,128)} %get-tuple-element.46.y, f32[2048,512]{1,0:T(8,128)} %get-tuple-element.49.pz, ...), custom_call_target="tpu_custom_call" | custom-call | tf_op jit(solution)/shard_map/scan_backward/pallas_call | solution.py:438
  149.2 0.0 copy-start.3
  149.2 1.3 copy-done.3
  150.5 0.0 copy-start.4
  150.5 1.3 copy-done.4
  151.8 0.0 copy-start.5
  151.8 1.2 copy-done.5
  153.0 0.0 copy-start.6
  153.0 0.6 copy-done.6
  153.6 75.8 %tail.1 = (bf16[2048,256]{1,0:T(8,128)(2,1)}, f32[2048,256]{1,0:T(8,128)}, f32[128,512]{1,0:T(8,128)}, f32[128,512]{1,0:T(8,128)}, f32[128,512]{1,0:T(8,128)}, /*index=5*/f32[128,256]{1,0:T(8,128)}, f32[24,1024]{1,0:T(8,128)}) custom-call(bf16[1024,2048]{1,0:T(8,128)(2,1)} %get-tuple-element.47.grad_t_in, bf16[2048,512]{1,0:T(8,128)(2,1)} %get-tuple-element.54.gn_in, ...), custom_call_target="tpu_custom_call" | custom-call | tf_op jit(solution)/shard_map/tail/pallas_call | solution.py:813
  229.4 0.0 copy-start.9
  229.4 0.0 copy-start.8
  229.4 0.0 copy-start.10
  229.4 0.0 copy-start.7
  229.4 0.9 slice_reduce_fusion
  230.3 1.3 dynamic-slice_divide_fusion
  231.6 0.8 slice.29
  232.4 0.6 dynamic-slice_bitcast_fusion
  233.0 0.8 slice.30
  233.8 0.6 reshape.37
  234.4 0.6 reshape_squeeze.3
  235.0 1.4 slice_bitcast_fusion
  236.4 1.3 slice.35
  237.7 2.3 copy.37
  239.9 3.0 %copy.38 = f32[2048,256]{1,0:T(8,128)} copy(f32[2048,256]{1,0:T(8,128)} %get-tuple-element.90) | data formatting | bytes 4194304
  243.0 0.0 copy-done.9
  243.0 0.7 copy.39
  243.7 0.0 copy-done.8
  243.7 0.7 copy.40
  244.4 0.0 copy-done.10
  244.4 0.7 copy.41
  245.0 0.0 copy-done.7
  245.0 0.7 copy.42
  (5 shorter events, 0.0 us)
Async XLA Ops:
  86.5 1.2 copy-start
  87.7 1.2 copy-start.1
  89.0 0.9 copy-start.2
  149.2 1.3 copy-start.3
  150.5 1.3 copy-start.4
  151.8 1.2 copy-start.5
  153.0 0.6 copy-start.6
  229.4 13.6 %copy-start.9 = (f32[128,512]{1,0:T(8,128)S(1)}, f32[128,512]{1,0:T(8,128)}, u32[]{:S(2)}) copy-start(f32[128,512]{1,0:T(8,128)} %get-tuple-element.92) | copy-start | bytes 786436
  229.4 14.3 %copy-start.8 = (f32[128,512]{1,0:T(8,128)S(1)}, f32[128,512]{1,0:T(8,128)}, u32[]{:S(2)}) copy-start(f32[128,512]{1,0:T(8,128)} %get-tuple-element.93) | copy-start | bytes 786436
  229.4 15.0 %copy-start.10 = (f32[128,256]{1,0:T(8,128)S(1)}, f32[128,256]{1,0:T(8,128)}, u32[]{:S(2)}) copy-start(f32[128,256]{1,0:T(8,128)} %get-tuple-element.95) | copy-start | bytes 393220
  229.4 15.6 %copy-start.7 = (f32[128,512]{1,0:T(8,128)S(1)}, f32[128,512]{1,0:T(8,128)}, u32[]{:S(2)}) copy-start(f32[128,512]{1,0:T(8,128)} %get-tuple-element.102) | copy-start | bytes 786436

commit v5 on v4

--- a/solution.py
+++ b/solution.py
@@ -124,19 +124,27 @@
     return row[:, 0:1] > 0.5, row[:, chunk : chunk + 1], row[:, 2 * chunk : 2 * chunk + 1] > 0.5
 
 
-def pack_vec(conv_x, skip, gate_gain, norm_gain, dt_bias, a_log, conv_bc, starts, fill, chunk):
-    width = norm_gain.shape[0]
-    wide = lambda a: jnp.pad(a, ((0, 0), (0, width - a.shape[1])))
-    down = lambda a, rows: jnp.pad(a, ((0, rows - a.shape[0]), (0, 0)))
-    cols = lambda *vs: jnp.concatenate([jnp.broadcast_to(v[:, None], (v.shape[0], chunk)) for v in vs], axis=1)
-    keep = jnp.where(starts == 0, 1.0, 0.0).astype(F32)
-    keep_next = jnp.concatenate([keep[1:], jnp.zeros((1,), F32)])
-    rows = [
-        wide(conv_x), wide(jnp.repeat(skip, HD)[None]), wide(gate_gain[None]), norm_gain[None],
-        jnp.zeros((1, width), F32), down(wide(cols(dt_bias, -jnp.exp(a_log))), 8), down(wide(conv_bc), 8),
-        wide(cols(keep, fill.astype(F32), keep_next)),
-    ]
-    return jnp.concatenate(rows, axis=0)
+def pack_vec(vec, conv_x, conv_bc, norm_gain, gate_gain, dt_bias, a_log, skip, starts, fill, chunk):
+    taps, inner = conv_x.shape
+    vec[...] = jnp.zeros_like(vec)
+    vec[0:taps, :inner] = conv_x[...]
+    vec[16 : 16 + taps, : conv_bc.shape[1]] = conv_bc[...]
+    vec[5:6, :inner] = gate_gain[...]
+    vec[6:7, :] = norm_gain[...]
+    head = iota2(1, inner, 1) // HD
+    skips = jnp.zeros((1, inner), F32)
+    for h in range(dt_bias.shape[0]):
+        skips = jnp.where(head == h, skip[h], skips)
+        vec[8 + h : 9 + h, 0:chunk] = jnp.full((1, chunk), dt_bias[h], F32)
+        vec[8 + h : 9 + h, chunk : 2 * chunk] = -jnp.exp(jnp.full((1, chunk), a_log[h], F32))
+    vec[4:5, :inner] = skips
+    blocks = starts.shape[0]
+    for c in range(blocks):
+        row = slice(24 + c, 25 + c)
+        vec[row, 0:chunk] = jnp.full((1, chunk), 1 - starts[c], jnp.int32).astype(F32)
+        vec[row, chunk : 2 * chunk] = jnp.full((1, chunk), fill[c], jnp.int32).astype(F32)
+        if c + 1 < blocks:
+            vec[row, 2 * chunk : 3 * chunk] = jnp.full((1, chunk), 1 - starts[c + 1], jnp.int32).astype(F32)
 
 
 def scan_step(heads, par, block, px, pbd, upper, spread, state, extx, extb):
@@ -850,19 +858,20 @@
 def shares(ref_in, block_of, dp_n, width, send, recv, who):
     rows = ref_in.shape[0]
     lines = who["lines"]
+    source = ref_in.at[:, width] if ref_in.shape[1] != width.size else ref_in
 
     def at(dp):
         return block_of.at[pl.ds(pl.multiple_of(dp * rows, rows), rows), width]
 
     def own():
-        return push(ref_in.at[:, width], at(who["dp"]), send.at[0], recv.at[0], who["yn"])
+        return push(source, at(who["dp"]), send.at[0], recv.at[0], who["yn"])
 
     def along(k):
-        return push(ref_in.at[:, width], at(who["dp"]), send.at[k], recv.at[k], who["line"](k))
+        return push(source, at(who["dp"]), send.at[k], recv.at[k], who["line"](k))
 
     def onward(k):
-        source = at(2 * ((who["line_index"] - k + lines) % lines) + who["pair"])
-        return push(source, source, send.at[lines - 1 + k], recv.at[lines - 1 + k], who["yn"])
+        there = at(2 * ((who["line_index"] - k + lines) % lines) + who["pair"])
+        return push(there, there, send.at[lines - 1 + k], recv.at[lines - 1 + k], who["yn"])
 
     return own, along, onward
 
@@ -877,9 +886,9 @@
 
 def front_kernel(
     dp_n, heads, units, taps, bc,
-    tokens, cot, w_x, w_bd, w_z, w_out, vec,
-    px_out, pbd_out, normed_out, normed_t_out, q_out, y_out, sin_out, parts, rows_x, rows_bd, rows_z, rows_out,
-    tok, wx, wbd, px, pbd, normed, normed_t, q, y, sin, state, extx, extb, upper, spread,
+    tokens, cot, w_x, w_bc, w_z, w_out, w_dt, conv_x, conv_bc, norm_gain, gate_gain, dt_bias, a_log, skip, starts, fill,
+    vec, px_out, pbd_out, normed_out, normed_t_out, q_out, y_out, sin_out, parts, rows_x, rows_bd, rows_z, rows_out,
+    own_dt, tok, wx, wbd, px, pbd, normed, normed_t, q, y, sin, own_w, own_cot, state, extx, extb, upper, spread,
     s_loc, s_sib, r_sib, s_x, r_x, s_f, r_f, s_cx, r_cx, s_cf, r_cf, s_w, r_w, s_out, s_y,
 ):
     who = peers(dp_n)
@@ -894,15 +903,26 @@
     pieces = s_cx.shape[0]
     cot_span = count // pieces
     here = pl.ds(pl.multiple_of(who["dp"] * block, block), block)
+    own_half = pl.ds(pl.multiple_of(who["core"] * (bc // 2), bc // 2), bc // 2)
+    dt_cols = pl.ds(bc, chunk)
     local = [
         pltpu.make_async_copy(src, dst, s_loc.at[k])
         for k, (src, dst) in enumerate((
-            (tokens, tok.at[who["mine"]]), (w_x, wx.at[here]), (w_bd, wbd.at[here]),
-            (w_z, rows_z.at[here]), (w_out, rows_out.at[here]), (cot, parts.at[who["mine"]]),
+            (tokens, tok.at[who["mine"]]), (w_x, wx.at[here]), (w_bc.at[:, own_half], wbd.at[here, own_half]),
+            (w_z, own_w.at[0]), (w_out, own_w.at[1]), (cot, own_cot),
         ))
     ]
-    for copy in local[:3]:
+    for copy in local:
         copy.start()
+    own_dt[...] = jnp.zeros_like(own_dt)
+    own_dt[:, :heads] = w_dt[...]
+    wbd[here, dt_cols] = own_dt[...]
+    onto = [
+        pltpu.make_async_copy(src, dst, s_loc.at[8 + k])
+        for k, (src, dst) in enumerate((
+            (own_w.at[0], rows_z.at[here]), (own_w.at[1], rows_out.at[here]), (own_cot, parts.at[who["mine"]]),
+        ))
+    ]
     meet(who)
 
     def rows(s, n=span):
@@ -933,19 +953,22 @@
     cuts = [
         shares(ref, to, dp_n, cols, s_w.at[n], r_w.at[n], who)
         for n, (ref, to, cols) in enumerate((
-            (w_x, wx, pl.ds(0, half)), (w_x, wx, pl.ds(half, half)), (w_bd, wbd, slice(None)),
+            (w_x, wx, pl.ds(0, half)), (w_x, wx, pl.ds(half, half)), (w_bc, wbd, own_half), (own_dt, wbd, dt_cols),
             (w_z, rows_z, pl.ds(0, half)), (w_z, rows_z, pl.ds(half, half)),
             (w_out, rows_out, pl.ds(0, half)), (w_out, rows_out, pl.ds(half, half)),
         ))
     ]
 
     def offer(n):
-        own, along, onward = cuts[n]
-        loop_line(lines, lambda k: along(k).start())
-        own().start()
+        loop_line(lines, lambda k: cuts[n][1](k).start())
+
+    def other_half():
+        cols = wbd.at[:, own_half]
+        return push(cols, cols, s_sib.at[2], r_sib.at[2], who["sib"])
 
     def pass_rows(n):
         own, along, onward = cuts[n]
+        own().start()
 
         def one(k):
             along(k).wait()
@@ -967,12 +990,13 @@
     for s in range(1, units):
         to_x(s).start()
     to_sib().start()
-    for n in (1, 2):
+    for n in (1, 2, 3):
         offer(n)
     for j in range(pieces):
         cot_x(j).start()
-    for n in (3, 4, 5, 6):
+    for n in (4, 5, 6, 7):
         offer(n)
+    pack_vec(vec, conv_x, conv_bc, norm_gain, gate_gain, dt_bias, a_log, skip, starts, fill, chunk)
     set_upper(upper)
     set_spread(spread, heads)
     state[...] = jnp.zeros_like(state)
@@ -1026,17 +1050,23 @@
     forward(1).wait()
     norm(1)
     pass_rows(2)
+    pass_rows(3)
+    have(2)
+    local[2].wait()
+    other_half().start()
     to_x(2).wait()
     forward(2).start()
     for copy in local[3:]:
+        copy.wait()
+    for copy in onto:
         copy.start()
     cot_sib().start()
     forward(2).wait()
     norm(2)
-    for copy in local[1:3]:
-        copy.wait()
-    for n in (0, 1, 2):
+    local[1].wait()
+    for n in (0, 1, 3):
         have(n)
+    other_half().wait()
     keep_rows = [
         pltpu.make_async_copy(wx, rows_x, s_loc.at[6]), pltpu.make_async_copy(wbd, rows_bd, s_loc.at[7]),
     ]
@@ -1053,8 +1083,8 @@
 
     events = {1: [(last_tokens, units - 1)], 2: [(last_norm, units - 1)]}
     late = []
-    plan = [(pass_rows, 3, 4), (pass_rows, 4, 8), (pass_rows, 5, 12)]
-    plan += [(pass_cot, j, 5 + 2 * j) for j in range(pieces)] + [(pass_rows, 6, blocks)]
+    plan = [(pass_rows, 4, 3), (pass_rows, 5, 7), (pass_rows, 6, 11)]
+    plan += [(pass_cot, j, 5 + 2 * j) for j in range(pieces)] + [(pass_rows, 7, 15)]
     for fn, k, at in plan:
         if at < blocks:
             events.setdefault(at, []).append((fn, k))
@@ -1103,25 +1133,29 @@
     for s in range(units):
         for copy in out_copies(s):
             copy.wait()
-    for copy in local[3:] + keep_rows:
+    for copy in onto + keep_rows:
         copy.wait()
     cot_sib().wait()
     for j in range(pieces):
         cot_forward(j).wait()
-    for n in (3, 4, 5, 6):
+    for n in (4, 5, 6, 7):
         have(n)
 
 
-def front(dp_n, heads, taps, bc, blocks, tokens, cot, w_x, w_bd, w_z, w_out, vec):
+def front(dp_n, tokens, cot, w_x, w_bc, w_z, w_out, w_dt, conv_x, conv_bc, norm_gain, gate_gain, *scalars):
     count, quarter = tokens.shape
     width = 4 * quarter
-    inner, wide = w_x.shape[1], w_bd.shape[1]
+    inner, heads = w_x.shape[1], w_dt.shape[1]
+    taps, bc = conv_bc.shape
+    blocks = scalars[-1].shape[0]
     chunk = count // blocks
+    wide = bc + chunk
     units, pieces = 4, 8
     vm, dma, sds = pltpu.VMEM, pltpu.SemaphoreType.DMA, jax.ShapeDtypeStruct
-    hbm = pl.BlockSpec(memory_space=pl.ANY)
+    hbm, vmem = pl.BlockSpec(memory_space=pl.ANY), pl.BlockSpec(memory_space=pltpu.VMEM)
     ways = dp_n - 1
     outs = [
+        sds((24 + blocks, width), F32),
         sds((count, inner), F32), sds((count, wide), F32), sds((count, width), BF), sds((width, count), BF),
         sds((count, 128), F32), sds((count, inner), F32), sds((blocks, bc // 2, inner), BF),
         sds((4, count, quarter), BF), sds((width, inner), BF), sds((width, wide), BF), sds((width, inner), BF),
@@ -1130,23 +1164,27 @@
     return pl.pallas_call(
         functools.partial(front_kernel, dp_n, heads, units, taps, bc),
         out_shape=outs,
-        in_specs=[hbm] * 6 + [pl.BlockSpec(memory_space=pltpu.VMEM)],
-        out_specs=[hbm] * len(outs),
+        in_specs=[hbm] * 6 + [vmem] * 5 + [pl.BlockSpec(memory_space=pltpu.SMEM)] * 5,
+        out_specs=[vmem] + [hbm] * (len(outs) - 1),
         scratch_shapes=[
+            vm((w_x.shape[0], chunk), BF),
             vm((4, count, quarter), BF), vm((width, inner), BF), vm((width, wide), BF),
             vm((count, inner), F32), vm((count, wide), F32), vm((count, width), BF), vm((width, count), BF),
             vm((count, 128), F32), vm((count, inner), F32), vm((blocks, bc // 2, inner), BF),
+            vm((2,) + w_z.shape, BF), vm(cot.shape, BF),
             vm((bc // 2, inner), F32), vm((chunk + 8, inner), F32), vm((chunk + 8, bc), F32),
             vm((chunk, chunk), BF), vm((chunk, 3 * inner), BF),
-            dma((8,)), dma((2,)), dma((2,)), dma((units,)), dma((units,)), dma((units,)), dma((units,)),
+            dma((11,)), dma((3,)), dma((3,)), dma((units,)), dma((units,)), dma((units,)), dma((units,)),
             dma((pieces,)), dma((pieces,)), dma((pieces,)), dma((pieces,)),
-            dma((7, ways)), dma((7, ways)), dma((5, units)), dma((2, blocks)),
+            dma((8, ways)), dma((8, ways)), dma((5, units)), dma((2, blocks)),
         ],
         compiler_params=pltpu.CompilerParams(
             collective_id=2, has_side_effects=True, vmem_limit_bytes=58 * 2**20
         ),
         name="front",
-    )(tokens, cot, w_x, w_bd, w_z, w_out, vec)
+    )(
+        tokens, cot, w_x, w_bc, w_z, w_out, w_dt, conv_x, conv_bc, norm_gain[None, :], gate_gain[None, :], *scalars
+    )
 
 
 def body(
@@ -1164,10 +1202,9 @@
     inner = w_x.shape[1]
     heads = w_dt.shape[1]
     taps, bc = conv_bc.shape
-    w_bd = jnp.concatenate([w_bc, jnp.pad(w_dt, ((0, 0), (0, chunk - heads)))], axis=1)
-    vec = pack_vec(conv_x, skip, gate_gain, norm_gain, dt_bias, a_log, conv_bc, starts, fill, chunk)
-    px, pbd, normed, normed_t, q_wide, y, sin, parts, rows_x, rows_bd, rows_z, rows_out = front(
-        dp_n, heads, taps, bc, blocks, tokens, cotangent, w_x, w_bd, w_z, w_out, vec
+    vec, px, pbd, normed, normed_t, q_wide, y, sin, parts, rows_x, rows_bd, rows_z, rows_out = front(
+        dp_n, tokens, cotangent, w_x, w_bc, w_z, w_out, w_dt, conv_x, conv_bc, norm_gain, gate_gain, dt_bias, a_log,
+        skip, starts, fill,
     )
     pz, ggn, grad_t, sums = gate(dp_n, blocks, normed, rows_z, rows_out, parts, y, vec)
     lpx, lpz, lpbd, gn, acc = scan_backward(

time: 247 us -> 225 us (0.911)
  Pallas kernels: 209 us -> 198 us
  local copies, waits for them, and re-layouts: 30.7 us -> 24.1 us
  other arithmetic: 4.89 us -> 1.33 us
    pallas_call x1, Pallas kernels: 74.3 us -> 68.8 us  [front(): pl.pallas_call(functools.partial(front_kernel, dp_n, heads, units, taps,...]
    pallas_call x1, Pallas kernels: 75.8 us -> 71 us  [tail(): pl.pallas_call(functools.partial(tail_kernel, dp_n, units), out_shape=[sd...]
    concatenate x1 -> x0, local copies, waits for them, and re-layouts: 3.2 us -> none  [pack_vec(): return jnp.concatenate(rows, axis=0)]
where the time goes in v5:
time: 225 us; the launch traced here: 224 us
  Pallas kernels  198 us (88%)
  local copies, waits for them, and re-layouts  24.1 us (11%)
    pallas_call x1, Pallas kernels, tail(): pl.pallas_call(functools.partial(tail_kernel, dp_n, units), out_shape=[sd...  71 us
    pallas_call x1, Pallas kernels, front(): pl.pallas_call(functools.partial(front_kernel, dp_n, heads, units, taps,...  68.8 us
    pallas_call x1, Pallas kernels, scan_backward(): pl.pallas_call(functools.partial(scan_bwd_kernel, heads, total_inner, tap...  40.7 us
    pallas_call x1, Pallas kernels, gate(): pl.pallas_call(functools.partial(gate_kernel, dp_n), grid=(steps,), in_sp...  17.4 us
    unnamed x29, local copies, waits for them, and re-layouts  17.3 us

profile of v5, /device:TPU:0, one launch (start us, length us, event | category | flops | bytes accessed | tf_op | source)
XLA Modules:
  0.0 224.2 jit_solution(15116016272849236854)
XLA Ops:
  0.6 1.4 copy.30.w_dt
  2.0 68.8 %front.1 = (f32[40,1024]{1,0:T(8,128)}, f32[2048,512]{1,0:T(8,128)}, f32[2048,384]{1,0:T(8,128)}, bf16[2048,1024]{1,0:T(8,128)(2,1)}, bf16[1024,2048]{1,0:T(8,12...) custom-call(bf16[2048,256]{1,0:T(8,128)(2,1)} %tokens.3, ...), custom_call_target="tpu_custom_call" | custom-call | tf_op jit(solution)/shard_map/front/pallas_call | solution.py:1164
  70.9 0.0 copy-start
  70.9 1.2 copy-done
  72.1 0.0 copy-start.1
  72.1 1.2 copy-done.1
  73.3 0.0 copy-start.5
  73.3 0.9 copy-done.5
  74.2 17.4 %gate.1 = (f32[2048,512]{1,0:T(8,128)}, f32[2048,512]{1,0:T(8,128)}, bf16[1024,2048]{1,0:T(8,128)(2,1)}, f32[2,16,128]{2,1,0:T(8,128)S(1)}) custom-call(bf16[2048,1024]{1,0:T(8,128)(2,1)} %get-tuple-element.43.normed.normed_in, bf16[1024,512]{1,0:T(8,128)(2,1)S(1)} %copy-done, bf16[1024,512]{1,0:T(8,128)(2,1)S(1)} %copy-done.1, ...), custom_call_target="tpu_custom_call" | custom-call | tf_op jit(solution)/shard_map/gate/pallas_call | solution.py:242
  91.7 40.7 %scan_backward.1 = (bf16[2048,512]{1,0:T(8,128)(2,1)S(1)}, bf16[2048,512]{1,0:T(8,128)(2,1)S(1)}, bf16[2048,384]{1,0:T(8,128)(2,1)S(1)}, bf16[2048,512]{1,0:T(8,128)(2,1)}, f32[8,1024]{1,0:T(8,128)S(1)}) custom-call(f32[2048,512]{1,0:T(8,128)} %get-tuple-element.50.ggn, f32[2048,512]{1,0:T(8,128)} %get-tuple-element.47.y, f32[2048,512]{1,0:T(8,128)} %get-tuple-element.51.pz, ...), custom_call_target="tpu_custom_call" | custom-call | tf_op jit(solution)/shard_map/scan_backward/pallas_call | solution.py:446
  132.4 0.0 copy-start.2
  132.4 1.3 copy-done.2
  133.7 0.0 copy-start.3
  133.7 1.3 copy-done.3
  135.0 0.0 copy-start.4
  135.0 1.2 copy-done.4
  136.2 0.0 copy-start.6
  136.2 0.6 copy-done.6
  136.8 71.0 %tail.1 = (bf16[2048,256]{1,0:T(8,128)(2,1)}, f32[2048,256]{1,0:T(8,128)}, f32[128,512]{1,0:T(8,128)}, f32[128,512]{1,0:T(8,128)}, f32[128,512]{1,0:T(8,128)}, /*index=5*/f32[128,256]{1,0:T(8,128)}, f32[24,1024]{1,0:T(8,128)}) custom-call(bf16[1024,2048]{1,0:T(8,128)(2,1)} %get-tuple-element.49.grad_t_in, bf16[2048,512]{1,0:T(8,128)(2,1)} %get-tuple-element.56.gn_in, ...), custom_call_target="tpu_custom_call" | custom-call | tf_op jit(solution)/shard_map/tail/pallas_call | solution.py:821
  207.8 0.0 copy-start.9
  207.8 0.0 copy-start.8
  207.8 0.0 copy-start.10
  207.9 0.0 copy-start.7
  207.9 0.9 slice_reduce_fusion
  208.8 1.3 dynamic-slice_divide_fusion
  210.1 0.8 slice.25
  210.8 0.6 dynamic-slice_bitcast_fusion
  211.4 0.8 slice.26
  212.2 0.6 reshape.32
  212.8 0.6 reshape_squeeze.3
  213.4 1.4 slice_bitcast_fusion
  214.8 1.3 slice.31
  216.1 2.3 %copy.37 = bf16[2048,256]{1,0:T(8,128)(2,1)} copy(bf16[2048,256]{1,0:T(8,128)(2,1)} %get-tuple-element.91) | data formatting | bytes 2097152
  218.4 3.0 %copy.38 = f32[2048,256]{1,0:T(8,128)} copy(f32[2048,256]{1,0:T(8,128)} %get-tuple-element.92) | data formatting | bytes 4194304
  221.4 0.0 copy-done.9
  221.4 0.7 copy.39
  222.1 0.0 copy-done.8
  222.1 0.7 copy.40
  222.8 0.0 copy-done.10
  222.8 0.7 copy.41
  223.5 0.0 copy-done.7
  223.5 0.7 copy.42
  (1 shorter events, 0.0 us)
Async XLA Ops:
  70.9 1.2 copy-start
  72.1 1.2 copy-start.1
  73.3 0.9 copy-start.5
  132.4 1.3 copy-start.2
  133.7 1.3 copy-start.3
  135.0 1.2 copy-start.4
  136.2 0.6 copy-start.6
  207.8 13.6 %copy-start.9 = (f32[128,512]{1,0:T(8,128)S(1)}, f32[128,512]{1,0:T(8,128)}, u32[]{:S(2)}) copy-start(f32[128,512]{1,0:T(8,128)} %get-tuple-element.94) | copy-start | bytes 786436
  207.8 14.3 %copy-start.8 = (f32[128,512]{1,0:T(8,128)S(1)}, f32[128,512]{1,0:T(8,128)}, u32[]{:S(2)}) copy-start(f32[128,512]{1,0:T(8,128)} %get-tuple-element.95) | copy-start | bytes 786436
  207.8 15.0 %copy-start.10 = (f32[128,256]{1,0:T(8,128)S(1)}, f32[128,256]{1,0:T(8,128)}, u32[]{:S(2)}) copy-start(f32[128,256]{1,0:T(8,128)} %get-tuple-element.97) | copy-start | bytes 393220
  207.9 15.6 %copy-start.7 = (f32[128,512]{1,0:T(8,128)S(1)}, f32[128,512]{1,0:T(8,128)}, u32[]{:S(2)}) copy-start(f32[128,512]{1,0:T(8,128)} %get-tuple-element.104) | copy-start | bytes 786436

commit v6 on v5

--- a/solution.py
+++ b/solution.py
@@ -188,15 +188,24 @@
     return y, enter_b
 
 
+def pair_rows(dp_n, block, pair, values):
+    return jnp.concatenate(
+        [values[pl.ds(pl.multiple_of((2 * l + pair) * block, block), block), :] for l in range(dp_n // 2)], axis=0
+    )
+
+
 def gate_kernel(
-    dp_n, normed, rows_z, rows_out, parts, y, vec, pz, ggn, grad_t, sums, h_send, h_recv, s_h, r_h,
+    dp_n, normed, rows_z, rows_out, parts, y, vec, pz, ggn, sums, gn, y_send, g_own,
+    h_send, h_recv, gated_all, grad_t, s_h, r_h,
 ):
     i = pl.program_id(0)
     who = peers(dp_n)
     names = ("sib", "xn", "dg")
     barrier = pltpu.get_barrier_semaphore()
     span, quarter = parts.shape[1:]
-    chunk = h_send.shape[2]
+    blocks, chunk = h_send.shape[1:]
+    inner = y.shape[1]
+    here = pl.ds(pl.multiple_of(i * span, span), span)
 
     @pl.when(i == 0)
     def _():
@@ -210,10 +219,11 @@
         g = g + nn(parts[k], rows_out[k * quarter : (k + 1) * quarter, :])
     ggn[...] = g
     for k in range(4):
-        grad_t[k * quarter : (k + 1) * quarter, :] = jnp.transpose(parts[k])
+        grad_t[k * quarter : (k + 1) * quarter, here] = jnp.transpose(parts[k])
     gated = y[...] * (z * sigmoid(z))
-    ones = jnp.ones((8, gated.shape[1]), BF)
-    for k, value in enumerate((gated * gated, gated * vec[5:6, : gated.shape[1]] * g)):
+    gated_all[here, :] = gated
+    ones = jnp.ones((8, inner), BF)
+    for k, value in enumerate((gated * gated, gated * vec[5:6, :inner] * g)):
         row = nt(ones, value.astype(BF))
         for j in range(span // chunk):
             h_send[k, pl.ds(i * (span // chunk) + j, 1), :] = row[0:1, j * chunk : (j + 1) * chunk]
@@ -227,6 +237,19 @@
         for copy in copies:
             copy.wait()
         sums[...] = h_send[...] + h_recv[0] + h_recv[1] + h_recv[2]
+        gain = vec[5:6, :inner]
+        squares = jnp.transpose(
+            jnp.concatenate([sums[0], jnp.zeros((chunk - blocks, chunk), F32)], axis=0)
+        )
+        inv = lax.rsqrt(squares / (4 * inner) + EPS)
+        for b in range(blocks):
+            at = slice(b * chunk, (b + 1) * chunk)
+            gn[at, :] = (gated_all[at, :] * inv[:, b : b + 1] * gain).astype(BF)
+        block = grad_t.shape[0] // dp_n
+        for v in range(2):
+            cols = slice(v * (inner // 2), (v + 1) * (inner // 2))
+            y_send[v] = nn(pair_rows(dp_n, block, 1 - who["pair"], grad_t), gn[:, cols]).astype(BF)
+            g_own[v] = nn(pair_rows(dp_n, block, who["pair"], grad_t), gn[:, cols])
 
 
 def gate(dp_n, blocks, normed, rows_z, rows_out, parts, y, vec):
@@ -238,36 +261,138 @@
     quarter = width // 4
     sds = jax.ShapeDtypeStruct
     rows = lambda w: pl.BlockSpec((span, w), lambda i: (i, 0))
-    whole = lambda a: pl.BlockSpec(a.shape, lambda i: (0, 0))
+    whole = lambda shape: pl.BlockSpec(shape, lambda i: (0,) * len(shape))
+    halves = (2, width // 2, inner // 2)
     return pl.pallas_call(
         functools.partial(gate_kernel, dp_n),
         grid=(steps,),
         in_specs=[
-            rows(width), whole(rows_z), whole(rows_out),
-            pl.BlockSpec((4, span, quarter), lambda i: (0, i, 0)), rows(inner), whole(vec),
+            rows(width), whole(rows_z.shape), whole(rows_out.shape),
+            pl.BlockSpec((4, span, quarter), lambda i: (0, i, 0)), rows(inner), whole(vec.shape),
         ],
         out_specs=[
-            rows(inner), rows(inner), pl.BlockSpec((width, span), lambda i: (0, i)),
-            pl.BlockSpec((2, blocks, chunk), lambda i: (0, 0, 0)),
+            rows(inner), rows(inner), whole((2, blocks, chunk)), whole((count, inner)), whole(halves), whole(halves),
         ],
         out_shape=[
-            sds((count, inner), F32), sds((count, inner), F32), sds((width, count), BF), sds((2, blocks, chunk), F32),
+            sds((count, inner), F32), sds((count, inner), F32), sds((2, blocks, chunk), F32), sds((count, inner), BF),
+            sds(halves, BF), sds(halves, F32),
         ],
         scratch_shapes=[
             pltpu.VMEM((2, blocks, chunk), F32), pltpu.VMEM((3, 2, blocks, chunk), F32),
+            pltpu.VMEM((count, inner), F32), pltpu.VMEM((width, count), BF),
             pltpu.SemaphoreType.DMA((3,)), pltpu.SemaphoreType.DMA((3,)),
         ],
         compiler_params=pltpu.CompilerParams(
-            collective_id=4, has_side_effects=True, vmem_limit_bytes=48 * 2**20
+            collective_id=4, has_side_effects=True, vmem_limit_bytes=58 * 2**20
         ),
         name="gate",
     )(normed, rows_z, rows_out, parts, y, vec)
 
 
+def sums_beside_scan(
+    dp_n, gn, rows_out, tokens, y_send, g_in, block_out, g_out,
+    sib_send, sib_recv, x_send, x_recv, part, held, y_recv, z_send, z_recv, g_own,
+    s_sib, r_sib, s_x, r_x, s_y, r_y, s_z, r_z,
+):
+    i = pl.program_id(0)
+    blocks = pl.num_programs(0)
+    who = peers(dp_n)
+    lines = who["lines"]
+    chunk = gn.shape[0]
+    quarter = tokens.shape[1]
+    block = g_out.shape[0]
+    half = g_out.shape[1] // 2
+
+    def copy_sib(k):
+        return push(sib_send.at[k], sib_recv.at[k], s_sib.at[k], r_sib.at[k], who["sib"])
+
+    def copy_x(k):
+        return push(x_send.at[k], x_recv.at[k], s_x.at[k], r_x.at[k], who["xn"])
+
+    def copy_y(v):
+        return push(y_send.at[v], y_recv.at[v], s_y.at[v], r_y.at[v], who["yn"])
+
+    def copy_z(v, k):
+        to = (who["line_index"] + k) % lines
+        return push(
+            z_send.at[v, pl.ds(pl.multiple_of(to * block, block), block)],
+            z_recv.at[v, k - 1], s_z.at[v, k - 1], r_z.at[v, k - 1], who["line"](k),
+        )
+
+    @pl.when(i == 0)
+    def _():
+        meet(who)
+        for v in range(2):
+            copy_y(v).start()
+
+    def first(k):
+        for n, q in enumerate(("sib_mine", "sib_other", "mine", "other")):
+            cols = pl.ds(pl.multiple_of(who[q] * quarter, quarter), quarter)
+            p = nt(gn[...], rows_out[cols, :])
+            if n < 2:
+                sib_send[k, n] = p.astype(BF)
+            else:
+                part[k % 2, n - 2] = p
+        copy_sib(k).start()
+
+    def second(k):
+        copy_sib(k).wait()
+        x_send[k] = (part[k % 2, 1] + sib_recv[k, 1].astype(F32)).astype(BF)
+        copy_x(k).start()
+        held[k] = part[k % 2, 0] + sib_recv[k, 0].astype(F32)
+
+    def third(k):
+        copy_x(k).wait()
+        at = pl.ds(pl.multiple_of((blocks - 1 - k) * chunk, chunk), chunk)
+        block_out[at, :] = (tokens[at, :].astype(F32) + held[k] + x_recv[k].astype(F32)).astype(BF)
+
+    def grad_b(v):
+        copy_y(v).wait()
+        g_own[v] = g_in[v] + y_recv[v].astype(F32)
+        z_send[v] = g_own[v].astype(BF)
+        loop_line(lines, lambda k: copy_z(v, k).start())
+
+    def grad_c(v):
+        loop_line(lines, lambda k: copy_z(v, k).wait())
+        total = g_own[v, pl.ds(pl.multiple_of(who["line_index"] * block, block), block), :]
+        for k in range(lines - 1):
+            total = total + z_recv[v, k].astype(F32)
+        g_out[:, v * half : (v + 1) * half] = total
+
+    for v, at in ((0, 4), (1, 7)):
+
+        @pl.when(i == at)
+        def _(v=v):
+            grad_b(v)
+
+    @pl.when(i >= 1)
+    def _():
+        second(i - 1)
+
+    @pl.when(i >= 4)
+    def _():
+        third(i - 4)
+
+    first(i)
+
+    def finish():
+        last = blocks - 1
+        second(last)
+        for v in range(2):
+            grad_c(v)
+        for k in range(3, -1, -1):
+            third(last - k)
+
+    return finish
+
+
 def scan_bwd_kernel(
-    heads, total_inner, taps_n, bc, ggn, y, pz, px, px_halo, pbd, pbd_halo, sin, rows, vec,
-    lpx, lpz, lpbd, gn, acc, dstate, extx, extb, dux, dub, acc_x, acc_bc, acc_s, upper, spread, gather, ones_h,
+    heads, total_inner, taps_n, bc, dp_n, ggn, y, pz, px, px_halo, pbd, pbd_halo, sin, rows, vec, gn, rows_out, tokens,
+    y_send, g_in,
+    lpx, lpz, lpbd, acc, block_out, g_out, dstate, extx, extb, dux, dub, acc_x, acc_bc, acc_s, upper, spread, gather, ones_h,
+    *beside,
 ):
+    finish = sums_beside_scan(dp_n, gn, rows_out, tokens, y_send, g_in, block_out, g_out, *beside)
     i = pl.program_id(0)
     blocks = pl.num_programs(0)
     c = blocks - 1 - i
@@ -301,7 +426,6 @@
     d_gated = inv * (g * gain) - gated * coef
     lpz[...] = (d_gated * yv * (sz * (1.0 + z * (1.0 - sz)))).astype(BF)
     dy = d_gated * silu_z
-    gn[...] = (gated * inv * gain).astype(BF)
     acc_x[taps_n : taps_n + 1, :] += jnp.sum(g * gated * inv, axis=0, keepdims=True)
 
     extx[0:8, :] = jnp.where(keep, px_halo[...], 0.0)
@@ -432,40 +556,58 @@
         three = jnp.concatenate(split3(acc_x[taps_n + 1 : taps_n + 2, :]) + (jnp.zeros((5, inner), F32),), axis=0)
         skips = jnp.sum(nn(three.astype(BF), gather[2]), axis=0, keepdims=True)
         acc[5:6, 0:chunk] = per_head + skips
-
-
-def scan_backward(ggn, y, pz, px, pbd, sin, rows, vec, heads, taps, bc, total_inner):
-    tokens, inner = px.shape
+        finish()
+
+
+def scan_backward(
+    dp_n, ggn, y, pz, px, pbd, sin, rows, vec, gn, rows_out, tokens, y_send, g_own, heads, taps, bc, total_inner
+):
+    count, inner = px.shape
     blocks = sin.shape[0]
-    chunk = tokens // blocks
+    chunk = count // blocks
     whole = lambda a: pl.BlockSpec(a.shape, lambda i: (0,) * a.ndim)
     back = lambda w: pl.BlockSpec((chunk, w), lambda i: (blocks - 1 - i, 0))
     halo = lambda w: pl.BlockSpec((8, w), lambda i: (jnp.maximum((blocks - 1 - i) * (chunk // 8) - 1, 0), 0))
     width = pbd.shape[1]
+    lines = dp_n // 2
+    more = max(lines - 1, 1)
+    block = rows_out.shape[0] // dp_n
+    quarter = tokens.shape[1]
+    dma = pltpu.SemaphoreType.DMA
     vm, sds = pltpu.VMEM, jax.ShapeDtypeStruct
     return pl.pallas_call(
-        functools.partial(scan_bwd_kernel, heads, total_inner, taps, bc),
+        functools.partial(scan_bwd_kernel, heads, total_inner, taps, bc, dp_n),
         grid=(blocks,),
         in_specs=[
             back(inner), back(inner), back(inner), back(inner), halo(inner), back(width), halo(width),
             pl.BlockSpec((1, bc // 2, inner), lambda i: (blocks - 1 - i, 0, 0)), whole(rows), whole(vec),
+            back(inner), whole(rows_out), whole(tokens), whole(y_send), whole(g_own),
         ],
         out_specs=[
-            back(inner), back(inner), back(width), back(inner), pl.BlockSpec((8, vec.shape[1]), lambda i: (0, 0)),
+            back(inner), back(inner), back(width), pl.BlockSpec((8, vec.shape[1]), lambda i: (0, 0)),
+            whole(tokens), pl.BlockSpec((block, inner), lambda i: (0, 0)),
         ],
         scratch_shapes=[
             vm((bc // 2, inner), F32), vm((chunk + 8, inner), F32), vm((chunk + 8, bc), F32),
             vm((chunk + 8, inner), F32), vm((chunk + 8, bc), F32),
             vm((8, inner), F32), vm((8, bc), F32), vm((2 * heads, chunk), F32),
             vm((chunk, chunk), BF), vm((chunk, 3 * inner), BF), vm((3, inner, chunk), BF), vm((heads * chunk, chunk), BF),
+            vm((blocks, 2, chunk, quarter), BF), vm((blocks, 2, chunk, quarter), BF),
+            vm((blocks, chunk, quarter), BF), vm((blocks, chunk, quarter), BF),
+            vm((2, 2, chunk, quarter), F32), vm((blocks, chunk, quarter), F32),
+            vm(y_send.shape, BF), vm(y_send.shape, BF), vm((2, more, block, inner // 2), BF), vm(y_send.shape, F32),
+            dma((blocks,)), dma((blocks,)), dma((blocks,)), dma((blocks,)), dma((2,)), dma((2,)),
+            dma((2, more)), dma((2, more)),
         ],
         out_shape=[
-            sds((tokens, inner), BF), sds((tokens, inner), BF), sds((tokens, width), BF), sds((tokens, inner), BF),
-            sds((8, vec.shape[1]), F32),
+            sds((count, inner), BF), sds((count, inner), BF), sds((count, width), BF),
+            sds((8, vec.shape[1]), F32), sds(tokens.shape, BF), sds((block, inner), F32),
         ],
-        compiler_params=pltpu.CompilerParams(vmem_limit_bytes=48 * 2**20),
+        compiler_params=pltpu.CompilerParams(
+            collective_id=3, has_side_effects=True, vmem_limit_bytes=58 * 2**20
+        ),
         name="scan_backward",
-    )(ggn, y, pz, px, px, pbd, pbd, sin, rows, vec)
+    )(ggn, y, pz, px, px, pbd, pbd, sin, rows, vec, gn, rows_out, tokens, y_send, g_own)
 def peers(dp_n):
     dp, hm = lax.axis_index("dp"), lax.axis_index("heads")
     across, core = hm // 2, hm % 2
@@ -505,21 +647,20 @@
 
 def tail_kernel(
     dp_n, units,
-    grad_t_in, gn_in, rows_out_in, normed_t_in, lpz_in, rows_z_in, lpx_in, rows_x_in, lpbd_in, rows_bd_in, normed_in,
+    normed_t_in, lpz_in, rows_z_in, lpx_in, rows_x_in, lpbd_in, rows_bd_in, normed_in,
     tokens, acc, cot, q_wide, vec,
-    block_out, grad_tokens, g_x, g_z, g_out, g_bc, small_out,
+    grad_tokens, g_x, g_z, g_bc, small_out,
     sib_send, sib_recv, x_send, x_recv, part, held,
     y_send, y_recv, z_send, z_recv, g_own, yb_send, yb_recv, zb_send, zb_recv, gb_own, bh_send, bh_recv,
     bx_send, bx_recv, bs_recv, h_send, h_recv, sy_send, sy_recv, sz_send, sz_recv, dy_send, dy_recv, dz_send, dz_recv, row_sums,
-    grad_t, gn, rows_out, normed_t, lpz, rows_z, lpx, rows_x, lpbd, rows_bd, normed,
+    normed_t, lpz, rows_z, lpx, rows_x, lpbd, rows_bd, normed,
     s_in, s_sib, r_sib, s_x, r_x, s_y, r_y, s_z, r_z, s_m, r_m, s_sl, r_sl,
 ):
     loads = [
         pltpu.make_async_copy(src, dst, s_in.at[i])
         for i, (src, dst) in enumerate((
-            (grad_t_in, grad_t), (gn_in, gn), (rows_out_in, rows_out), (normed_t_in, normed_t), (lpz_in, lpz),
-            (rows_z_in, rows_z), (lpx_in, lpx), (rows_x_in, rows_x), (lpbd_in, lpbd), (rows_bd_in, rows_bd),
-            (normed_in, normed),
+            (normed_t_in, normed_t), (lpz_in, lpz), (rows_z_in, rows_z), (lpx_in, lpx), (rows_x_in, rows_x),
+            (lpbd_in, lpbd), (rows_bd_in, rows_bd), (normed_in, normed),
         ))
     ]
     for load in loads:
@@ -543,24 +684,21 @@
 
     def product(u, q):
         cols = pl.ds(pl.multiple_of(q * quarter, quarter), quarter)
-        if u < units:
-            return nt(gn[u * span : (u + 1) * span, :], rows_out[cols, :])
-        at = slice((u - units) * span, (u - units + 1) * span)
+        at = slice(u * span, (u + 1) * span)
         return nt(lpx[at, :], rows_x[cols, :]) + nt(lpz[at, :], rows_z[cols, :]) + nt(lpbd[at, :], rows_bd[cols, :])
 
     def head_a(u):
         for k, q in enumerate(("sib_mine", "sib_other", "mine", "other")):
             p = product(u, who[q])
-            if u >= units:
-                at = slice((u - units) * span, (u - units + 1) * span)
-                cols = pl.ds(pl.multiple_of(who[q] * quarter, quarter), quarter)
-                inner_p = p * normed[at, cols].astype(F32)
-                h_send[0:1, cols] += jnp.sum(inner_p, axis=0, keepdims=True)
-                first = (u - units) * span
-                lanes = slice(first % width, first % width + span)
-                h_send[2 + first // width : 3 + first // width, lanes] += nt(
-                    jnp.ones((8, quarter), BF), inner_p.astype(BF)
-                )[0:1]
+            at = slice(u * span, (u + 1) * span)
+            cols = pl.ds(pl.multiple_of(who[q] * quarter, quarter), quarter)
+            inner_p = p * normed[at, cols].astype(F32)
+            h_send[0:1, cols] += jnp.sum(inner_p, axis=0, keepdims=True)
+            first = u * span
+            lanes = slice(first % width, first % width + span)
+            h_send[2 + first // width : 3 + first // width, lanes] += nt(
+                jnp.ones((8, quarter), BF), inner_p.astype(BF)
+            )[0:1]
             if k < 2:
                 sib_send[u, k] = p.astype(BF)
             else:
@@ -576,30 +714,26 @@
     def head_c(u):
         copy_x(u).wait()
         total = held[u] + x_recv[u].astype(F32)
-        if u < units:
-            at = slice(u * span, (u + 1) * span)
-            block_out[at, :] = (tokens[at, :].astype(F32) + total).astype(BF)
-        else:
-            first = (u - units) * span
-            lanes = q_wide.shape[1]
-            cols = pl.ds(pl.multiple_of(who["mine"] * quarter, quarter), quarter)
-            for j in range(span // lanes):
-                at = slice(first + j * lanes, first + (j + 1) * lanes)
-                row, lane = (first + j * lanes) // width, (first + j * lanes) % width
-                dots = jnp.transpose(jnp.broadcast_to(row_sums[row : row + 1, lane : lane + lanes], (lanes, lanes)))
-                q = q_wide[at, :]
-                coef = q * q * (dots / width)
-                grad_tokens[at, :] = (
-                    cot[at, :].astype(F32)
-                    + q[:, 0:1] * vec[6:7, cols] * total[j * lanes : (j + 1) * lanes]
-                    - tokens[at, :].astype(F32) * coef[:, 0:1]
-                )
+        first = u * span
+        lanes = q_wide.shape[1]
+        cols = pl.ds(pl.multiple_of(who["mine"] * quarter, quarter), quarter)
+        for j in range(span // lanes):
+            at = slice(first + j * lanes, first + (j + 1) * lanes)
+            row, lane = (first + j * lanes) // width, (first + j * lanes) % width
+            dots = jnp.transpose(jnp.broadcast_to(row_sums[row : row + 1, lane : lane + lanes], (lanes, lanes)))
+            q = q_wide[at, :]
+            coef = q * q * (dots / width)
+            grad_tokens[at, :] = (
+                cot[at, :].astype(F32)
+                + q[:, 0:1] * vec[6:7, cols] * total[j * lanes : (j + 1) * lanes]
+                - tokens[at, :].astype(F32) * coef[:, 0:1]
+            )
 
     def rows_of(line, pair):
         return pl.ds(pl.multiple_of((2 * line + pair) * block, block), block)
 
     def grad_a(v):
-        left, right = ((grad_t, gn), (normed_t, lpz), (normed_t, lpx))[v // 2]
+        left, right = ((normed_t, lpz), (normed_t, lpx))[v // 2]
         cols = slice((v % 2) * (inner // 2), (v % 2 + 1) * (inner // 2))
         for side in (0, 1):
             pair = (1 - who["pair"]) if side == 0 else who["pair"]
@@ -643,7 +777,7 @@
         for k in range(lines - 1):
             total = total + z_recv[v, k].astype(F32)
         cols = slice((v % 2) * (inner // 2), (v % 2 + 1) * (inner // 2))
-        (g_out, g_z, g_x)[v // 2][:, cols] = total
+        (g_z, g_x)[v // 2][:, cols] = total
 
     half = bc // 2
 
@@ -788,21 +922,14 @@
 
     load(0, 1)
     seq((grad_a, 0), (grad_a, 1))
-    load(2)
-    seq((head_a, 0), (head_a, 1), (head_b, 0), (head_a, 2), (head_b, 1), (head_a, 3), (head_b, 2))
-    load(3, 8)
-    seq((bc_a,), (head_b, 3))
-    load(4)
-    seq((grad_a, 2), (bc_b,), (grad_a, 3))
-    load(5, 6, 7, 9, 10)
-    seq((grad_b, 0), (head_a, 4), (dt_a,), (grad_b, 1), (grad_a, 4), (head_b, 4), (head_a, 5), (bc_c,), (head_b, 5))
-    seq((grad_a, 5), (head_a, 6), (grad_b, 2), (head_b, 6), (head_a, 7), (small_a,), (grad_b, 3), (head_b, 7))
-    seq((dt_b,), (small_b,), (head_c, 0), (head_c, 1), (head_c, 2), (head_c, 3), (bc_d,), (grad_c, 0), (grad_c, 1))
-    seq((grad_b, 4), (small_c,), (grad_b, 5), (dt_c,), (bc_e,), (head_c, 4), (head_c, 5), (grad_c, 2), (grad_c, 3))
-    seq((small_d,), (head_c, 6), (grad_c, 4), (bc_f,), (head_c, 7), (grad_c, 5))
-
-
-def tail(dp_n, units, normed_t, normed, grad_t, gn, lpx, lpz, lpbd, rows_x, rows_z, rows_bd, rows_out, tokens, acc, cot, q_wide, vec, bc):
+    load(2, 3, 4, 5, 6, 7)
+    seq((head_a, 0), (bc_a,), (head_a, 1), (head_b, 0), (grad_a, 2), (bc_b,), (head_b, 1), (grad_b, 0), (head_a, 2))
+    seq((grad_a, 3), (head_b, 2), (dt_a,), (grad_b, 1), (head_a, 3), (small_a,), (bc_c,), (head_b, 3), (dt_b,))
+    seq((small_b,), (grad_b, 2), (grad_c, 0), (small_c,), (bc_d,), (dt_c,), (head_c, 0), (grad_b, 3), (grad_c, 1))
+    seq((bc_e,), (head_c, 1), (small_d,), (head_c, 2), (grad_c, 2), (bc_f,), (head_c, 3), (grad_c, 3))
+
+
+def tail(dp_n, units, normed_t, normed, lpx, lpz, lpbd, rows_x, rows_z, rows_bd, tokens, acc, cot, q_wide, vec, bc):
     count, width = normed.shape
     inner = lpx.shape[1]
     quarter = width // 4
@@ -814,26 +941,25 @@
     vm = pltpu.VMEM
     dma = pltpu.SemaphoreType.DMA
     operands = (
-        grad_t, gn, rows_out, normed_t, lpz, rows_z, lpx, rows_x, lpbd, rows_bd, normed, tokens, acc, cot, q_wide, vec,
+        normed_t, lpz, rows_z, lpx, rows_x, lpbd, rows_bd, normed, tokens, acc, cot, q_wide, vec,
     )
     sds = jax.ShapeDtypeStruct
     spec = pl.BlockSpec(memory_space=pltpu.VMEM)
     return pl.pallas_call(
         functools.partial(tail_kernel, dp_n, units),
         out_shape=[
-            sds((count, quarter), BF), sds((count, quarter), F32),
-            sds((block, inner), F32), sds((block, inner), F32), sds((block, inner), F32), sds((block, bc), F32),
+            sds((count, quarter), F32), sds((block, inner), F32), sds((block, inner), F32), sds((block, bc), F32),
             sds((24, width), F32),
         ],
-        in_specs=[pl.BlockSpec(memory_space=pl.ANY)] * 11 + [spec] * 5,
-        out_specs=[spec] * 7,
+        in_specs=[pl.BlockSpec(memory_space=pl.ANY)] * 8 + [spec] * 5,
+        out_specs=[spec] * 5,
         scratch_shapes=[
-            vm((2 * units, 2, span, quarter), BF), vm((2 * units, 2, span, quarter), BF),
-            vm((2 * units, span, quarter), BF), vm((2 * units, span, quarter), BF),
-            vm((2, 2, span, quarter), F32), vm((2 * units, span, quarter), F32),
-            vm((6, half_rows, inner // 2), BF), vm((6, half_rows, inner // 2), BF),
-            vm((6, half_rows, inner // 2), BF), vm((6, more, block, inner // 2), BF),
-            vm((6, half_rows, inner // 2), F32),
+            vm((units, 2, span, quarter), BF), vm((units, 2, span, quarter), BF),
+            vm((units, span, quarter), BF), vm((units, span, quarter), BF),
+            vm((2, 2, span, quarter), F32), vm((units, span, quarter), F32),
+            vm((4, half_rows, inner // 2), BF), vm((4, half_rows, inner // 2), BF),
+            vm((4, half_rows, inner // 2), BF), vm((4, more, block, inner // 2), BF),
+            vm((4, half_rows, inner // 2), F32),
             vm((half_rows, bc // 2), BF), vm((half_rows, bc // 2), BF),
             vm((half_rows, bc // 2), BF), vm((more, block, bc // 2), BF),
             vm((2 * half_rows, bc // 2), F32),
@@ -844,10 +970,10 @@
             vm((16, width), BF), vm((16, width), BF), vm((16, width), BF), vm((more, 16, width), BF),
             vm((8, width), F32),
         ]
-        + [vm(a.shape, a.dtype) for a in operands[:11]]
+        + [vm(a.shape, a.dtype) for a in operands[:8]]
         + [
-            dma((11,)), dma((2 * units,)), dma((2 * units,)), dma((2 * units,)), dma((2 * units,)),
-            dma((6,)), dma((6,)), dma((6, more)), dma((6, more)), dma((9,)), dma((9,)),
+            dma((8,)), dma((units,)), dma((units,)), dma((units,)), dma((units,)),
+            dma((4,)), dma((4,)), dma((4, more)), dma((4, more)), dma((9,)), dma((9,)),
             dma((3, more)), dma((3, more)),
         ],
         compiler_params=pltpu.CompilerParams(
@@ -1206,13 +1332,13 @@
         dp_n, tokens, cotangent, w_x, w_bc, w_z, w_out, w_dt, conv_x, conv_bc, norm_gain, gate_gain, dt_bias, a_log,
         skip, starts, fill,
     )
-    pz, ggn, grad_t, sums = gate(dp_n, blocks, normed, rows_z, rows_out, parts, y, vec)
-    lpx, lpz, lpbd, gn, acc = scan_backward(
-        ggn, y, pz, px, pbd, sin, sums, vec, heads, taps, bc, inner * heads_n
-    )
-    block_out, grad_tokens, grad_w_x, grad_w_z, grad_w_out, grad_w_bc, small = tail(
-        dp_n, 4, normed_t, normed, grad_t, gn, lpx, lpz, lpbd, rows_x, rows_z, rows_bd, rows_out,
-        tokens, acc, cotangent, q_wide, vec, bc,
+    pz, ggn, sums, gn, y_send, g_own = gate(dp_n, blocks, normed, rows_z, rows_out, parts, y, vec)
+    lpx, lpz, lpbd, acc, block_out, grad_w_out = scan_backward(
+        dp_n, ggn, y, pz, px, pbd, sin, sums, vec, gn, rows_out, tokens, y_send, g_own, heads, taps, bc,
+        inner * heads_n,
+    )
+    grad_tokens, grad_w_x, grad_w_z, grad_w_bc, small = tail(
+        dp_n, 4, normed_t, normed, lpx, lpz, lpbd, rows_x, rows_z, rows_bd, tokens, acc, cotangent, q_wide, vec, bc,
     )
     block = width // dp_n
     own_gain = lax.dynamic_slice_in_dim(norm_gain, head_index * columns, columns, 0)

time: 225 us -> 220 us (0.978)
  local copies, waits for them, and re-layouts: 24.1 us -> 13.5 us
  Pallas kernels: 198 us -> 204 us
    pallas_call x1, Pallas kernels: 40.7 us -> 58.3 us  [scan_backward(): pl.pallas_call(functools.partial(scan_bwd_kernel, heads, total_inner, tap...]
    pallas_call x1, Pallas kernels: 71 us -> 56.4 us  [tail(): pl.pallas_call(functools.partial(tail_kernel, dp_n, units), out_shape=[sd...]
    unnamed x29 -> x19, local copies, waits for them, and re-layouts: 17.3 us -> 6.48 us
    pallas_call x1, Pallas kernels: 17.4 us -> 20.7 us  [gate(): pl.pallas_call(functools.partial(gate_kernel, dp_n), grid=(steps,), in_sp...]
where the time goes in v6:
time: 220 us
  Pallas kernels  204 us (93%)
  local copies, waits for them, and re-layouts  13.5 us (6%)
    pallas_call x1, Pallas kernels, front(): pl.pallas_call(functools.partial(front_kernel, dp_n, heads, units, taps,...  68.8 us
    pallas_call x1, Pallas kernels, scan_backward(): pl.pallas_call(functools.partial(scan_bwd_kernel, heads, total_inner, tap...  58.3 us
    pallas_call x1, Pallas kernels, tail(): pl.pallas_call(functools.partial(tail_kernel, dp_n, units), out_shape=[sd...  56.4 us
    pallas_call x1, Pallas kernels, gate(): pl.pallas_call(functools.partial(gate_kernel, dp_n), grid=(steps,), in_sp...  20.7 us
    unnamed x19, local copies, waits for them, and re-layouts  6.48 us

profile of v6, /device:TPU:0, one launch (start us, length us, event | category | flops | bytes accessed | tf_op | source)
XLA Modules:
  0.0 219.7 jit_solution(3300785763665239862)
XLA Ops:
  0.6 1.4 copy.30.w_dt
  2.0 68.8 %front.1 = (f32[40,1024]{1,0:T(8,128)}, f32[2048,512]{1,0:T(8,128)}, f32[2048,384]{1,0:T(8,128)}, bf16[2048,1024]{1,0:T(8,128)(2,1)}, bf16[1024,2048]{1,0:T(8,12...) custom-call(bf16[2048,256]{1,0:T(8,128)(2,1)} %tokens.5, ...), custom_call_target="tpu_custom_call" | custom-call | tf_op jit(solution)/shard_map/front/pallas_call | solution.py:1290
  70.8 20.7 %gate.1 = (f32[2048,512]{1,0:T(8,128)}, f32[2048,512]{1,0:T(8,128)}, f32[2,16,128]{2,1,0:T(8,128)}, bf16[2048,512]{1,0:T(8,128)(2,1)}, bf16[2,512,256]{2,1,0:T(8,128)(2,1)}, /*index=5*/f32[2,512,256]{2,1,0:T(8,128)}) custom-call(bf16[2048,1024]{1,0:T(8,128)(2,1)} %get-tuple-element.44.normed.normed_in, bf16[1024,512]{1,0:T(8,128)(2,1)} %get-tuple-element.45.rows_z.rows_z_in, ...), custom_call_target="tpu_custom_call" | custom-call | tf_op jit(solution)/shard_map/gate/pallas_call | solution.py:266
  91.6 58.3 %scan_backward.1 = (bf16[2048,512]{1,0:T(8,128)(2,1)}, bf16[2048,512]{1,0:T(8,128)(2,1)}, bf16[2048,384]{1,0:T(8,128)(2,1)}, f32[8,1024]{1,0:T(8,128)}, bf16[2048,256]{1,0:T(8,128)(2,1)}, /*index=5*/f32[128,512]{1,0:T(8,128)}) custom-call(f32[2048,512]{1,0:T(8,128)} %get-tuple-element.50.ggn, f32[2048,512]{1,0:T(8,128)} %get-tuple-element.48.y, ...), custom_call_target="tpu_custom_call" | custom-call | tf_op jit(solution)/shard_map/scan_backward/pallas_call | solution.py:578
  149.8 0.0 copy-start.1
  149.8 56.4 %tail.1 = (f32[2048,256]{1,0:T(8,128)}, f32[128,512]{1,0:T(8,128)}, f32[128,512]{1,0:T(8,128)}, f32[128,256]{1,0:T(8,128)}, f32[24,1024]{1,0:T(8,128)}) custom-call(bf16[1024,2048]{1,0:T(8,128)(2,1)} %get-tuple-element.60.normed_t_in, bf16[2048,512]{1,0:T(8,128)(2,1)} %get-tuple-element.61.lpz_in, bf16[1024,512]{1,0:T(8,128)(2,1)} %get-tuple-element.45.rows_z.rows_z_in, ...), custom_call_target="tpu_custom_call" | custom-call | tf_op jit(solution)/shard_map/tail/pallas_call | solution.py:948
  206.2 0.0 copy-start
  206.2 0.9 slice.25
  207.1 0.6 dynamic-slice_bitcast_fusion
  207.7 0.8 slice_reduce_fusion
  208.6 1.3 dynamic-slice_divide_fusion
  209.9 0.8 slice.26
  210.7 0.6 reshape.32
  211.3 0.6 reshape_squeeze.3
  211.9 1.3 slice.31
  213.2 1.4 slice_bitcast_fusion
  214.6 0.0 copy-done.1
  214.6 0.0 copy-start.4
  214.6 0.0 copy-start.3
  214.6 1.0 copy.37
  215.6 0.0 copy-done
  215.6 0.0 copy-start.5
  215.6 0.0 copy-start.2
  215.6 1.3 copy.38
  216.9 0.0 copy-done.4
  216.9 0.7 copy.39
  217.6 0.0 copy-done.3
  217.6 0.7 copy.40
  218.3 0.0 copy-done.5
  218.3 0.7 copy.41
  219.0 0.0 copy-done.2
  219.0 0.7 copy.42
  (1 shorter events, 0.0 us)
Async XLA Ops:
  149.8 64.7 %copy-start.1 = (bf16[2048,256]{1,0:T(8,128)(2,1)S(1)}, bf16[2048,256]{1,0:T(8,128)(2,1)}, u32[]{:S(2)}) copy-start(bf16[2048,256]{1,0:T(8,128)(2,1)} %get-tuple-element.93) | copy-start | bytes 3145732
  206.2 9.4 %copy-start = (f32[2048,256]{1,0:T(8,128)S(1)}, f32[2048,256]{1,0:T(8,128)}, u32[]{:S(2)}) copy-start(f32[2048,256]{1,0:T(8,128)} %get-tuple-element.94) | copy-start | bytes 6291460
  214.6 2.3 %copy-start.4 = (f32[128,512]{1,0:T(8,128)S(1)}, f32[128,512]{1,0:T(8,128)}, u32[]{:S(2)}) copy-start(f32[128,512]{1,0:T(8,128)} %get-tuple-element.96) | copy-start | bytes 786436
  214.6 3.0 %copy-start.3 = (f32[128,512]{1,0:T(8,128)S(1)}, f32[128,512]{1,0:T(8,128)}, u32[]{:S(2)}) copy-start(f32[128,512]{1,0:T(8,128)} %get-tuple-element.97) | copy-start | bytes 786436
  215.6 2.7 %copy-start.5 = (f32[128,256]{1,0:T(8,128)S(1)}, f32[128,256]{1,0:T(8,128)}, u32[]{:S(2)}) copy-start(f32[128,256]{1,0:T(8,128)} %get-tuple-element.99) | copy-start | bytes 393220
  215.6 3.4 %copy-start.2 = (f32[128,512]{1,0:T(8,128)S(1)}, f32[128,512]{1,0:T(8,128)}, u32[]{:S(2)}) copy-start(f32[128,512]{1,0:T(8,128)} %get-tuple-element.106) | copy-start | bytes 786436

commit v7 on v6

--- a/solution.py
+++ b/solution.py
@@ -295,11 +295,9 @@
     s_sib, r_sib, s_x, r_x, s_y, r_y, s_z, r_z,
 ):
     i = pl.program_id(0)
-    blocks = pl.num_programs(0)
     who = peers(dp_n)
     lines = who["lines"]
-    chunk = gn.shape[0]
-    quarter = tokens.shape[1]
+    units, span, quarter = held.shape
     block = g_out.shape[0]
     half = g_out.shape[1] // 2
 
@@ -328,22 +326,22 @@
     def first(k):
         for n, q in enumerate(("sib_mine", "sib_other", "mine", "other")):
             cols = pl.ds(pl.multiple_of(who[q] * quarter, quarter), quarter)
-            p = nt(gn[...], rows_out[cols, :])
+            p = nt(gn[k * span : (k + 1) * span, :], rows_out[cols, :])
             if n < 2:
                 sib_send[k, n] = p.astype(BF)
             else:
-                part[k % 2, n - 2] = p
+                part[n - 2] = p
         copy_sib(k).start()
 
     def second(k):
         copy_sib(k).wait()
-        x_send[k] = (part[k % 2, 1] + sib_recv[k, 1].astype(F32)).astype(BF)
+        x_send[k] = (part[1] + sib_recv[k, 1].astype(F32)).astype(BF)
         copy_x(k).start()
-        held[k] = part[k % 2, 0] + sib_recv[k, 0].astype(F32)
+        held[k] = part[0] + sib_recv[k, 0].astype(F32)
 
     def third(k):
         copy_x(k).wait()
-        at = pl.ds(pl.multiple_of((blocks - 1 - k) * chunk, chunk), chunk)
+        at = slice(k * span, (k + 1) * span)
         block_out[at, :] = (tokens[at, :].astype(F32) + held[k] + x_recv[k].astype(F32)).astype(BF)
 
     def grad_b(v):
@@ -359,29 +357,20 @@
             total = total + z_recv[v, k].astype(F32)
         g_out[:, v * half : (v + 1) * half] = total
 
-    for v, at in ((0, 4), (1, 7)):
+    events = [(grad_b, 0, 4), (grad_b, 1, 7)]
+    for k in range(units):
+        events += [(first, k, 2 * k), (second, k, 2 * k + 1), (third, k, 2 * k + 6)]
+    for at in sorted({e[2] for e in events}):
 
         @pl.when(i == at)
-        def _(v=v):
-            grad_b(v)
-
-    @pl.when(i >= 1)
-    def _():
-        second(i - 1)
-
-    @pl.when(i >= 4)
-    def _():
-        third(i - 4)
-
-    first(i)
+        def _(at=at):
+            for fn, k, when in events:
+                if when == at:
+                    fn(k)
 
     def finish():
-        last = blocks - 1
-        second(last)
         for v in range(2):
             grad_c(v)
-        for k in range(3, -1, -1):
-            third(last - k)
 
     return finish
 
@@ -573,6 +562,8 @@
     more = max(lines - 1, 1)
     block = rows_out.shape[0] // dp_n
     quarter = tokens.shape[1]
+    units = 4
+    span = count // units
     dma = pltpu.SemaphoreType.DMA
     vm, sds = pltpu.VMEM, jax.ShapeDtypeStruct
     return pl.pallas_call(
@@ -581,7 +572,7 @@
         in_specs=[
             back(inner), back(inner), back(inner), back(inner), halo(inner), back(width), halo(width),
             pl.BlockSpec((1, bc // 2, inner), lambda i: (blocks - 1 - i, 0, 0)), whole(rows), whole(vec),
-            back(inner), whole(rows_out), whole(tokens), whole(y_send), whole(g_own),
+            whole(gn), whole(rows_out), whole(tokens), whole(y_send), whole(g_own),
         ],
         out_specs=[
             back(inner), back(inner), back(width), pl.BlockSpec((8, vec.shape[1]), lambda i: (0, 0)),
@@ -592,11 +583,11 @@
             vm((chunk + 8, inner), F32), vm((chunk + 8, bc), F32),
             vm((8, inner), F32), vm((8, bc), F32), vm((2 * heads, chunk), F32),
             vm((chunk, chunk), BF), vm((chunk, 3 * inner), BF), vm((3, inner, chunk), BF), vm((heads * chunk, chunk), BF),
-            vm((blocks, 2, chunk, quarter), BF), vm((blocks, 2, chunk, quarter), BF),
-            vm((blocks, chunk, quarter), BF), vm((blocks, chunk, quarter), BF),
-            vm((2, 2, chunk, quarter), F32), vm((blocks, chunk, quarter), F32),
+            vm((units, 2, span, quarter), BF), vm((units, 2, span, quarter), BF),
+            vm((units, span, quarter), BF), vm((units, span, quarter), BF),
+            vm((2, span, quarter), F32), vm((units, span, quarter), F32),
             vm(y_send.shape, BF), vm(y_send.shape, BF), vm((2, more, block, inner // 2), BF), vm(y_send.shape, F32),
-            dma((blocks,)), dma((blocks,)), dma((blocks,)), dma((blocks,)), dma((2,)), dma((2,)),
+            dma((units,)), dma((units,)), dma((units,)), dma((units,)), dma((2,)), dma((2,)),
             dma((2, more)), dma((2, more)),
         ],
         out_shape=[
@@ -1002,6 +993,90 @@
     return own, along, onward
 
 
+def chain(ref_in, block_of, width, send, recv, y_send, y_recv, who):
+    rows = ref_in.shape[0]
+    lines, line, pair, dp = who["lines"], who["line_index"], who["pair"], who["dp"]
+
+    def at(index):
+        return block_of.at[pl.ds(pl.multiple_of((2 * index + pair) * rows, rows), rows), width]
+
+    def hand(sign, j):
+        index = line - sign * j
+        source = ref_in.at[:, width] if isinstance(j, int) and j == 0 else at(index)
+        slot = j + 1 if sign > 0 else lines + j
+        to = (2 * (line + sign) + pair, who["mine"])
+        return push(source, at(index), send.at[slot], recv.at[slot], to)
+
+    def to_pair(sign, j):
+        slot = j if sign > 0 else lines - 1 + j
+        index = line - sign * j
+        source = ref_in.at[:, width] if isinstance(j, int) and j == 0 else at(index)
+        return push(source, at(index), y_send.at[slot], y_recv.at[slot], who["yn"])
+
+    def arrived(sign, j):
+        slot = j if sign > 0 else lines - 1 + j
+        block = at(line - sign * j)
+        return push(block, block, send.at[slot], recv.at[slot], who["yn"])
+
+    def inside(index):
+        return jnp.logical_and(index >= 0, index < lines)
+
+    def both(fn):
+        for sign in (1, -1):
+            fn(sign)
+
+    def begin():
+        def one(sign):
+            @pl.when(inside(line + sign))
+            def _():
+                hand(sign, 0).start()
+
+        both(one)
+
+    def begin_pair():
+        to_pair(1, 0).start()
+
+    def hop(j):
+        def one(sign):
+            @pl.when(inside(line - sign * j))
+            def _():
+                arrived(sign, j).wait_recv()
+
+                @pl.when(inside(line + sign))
+                def _():
+                    hand(sign, j).start()
+
+                to_pair(sign, j).start()
+
+        both(one)
+
+    def end():
+        to_pair(1, 0).wait()
+
+        def one(sign):
+            @pl.when(inside(line + sign))
+            def _():
+                hand(sign, 0).wait_send()
+
+        both(one)
+
+        def later(j):
+            def one(sign):
+                @pl.when(inside(line - sign * j))
+                def _():
+                    to_pair(sign, j).wait()
+
+                    @pl.when(inside(line + sign))
+                    def _():
+                        hand(sign, j).wait_send()
+
+            both(one)
+
+        loop_line(lines, later)
+
+    return begin, begin_pair, hop, end
+
+
 def loop_line(lines, fn):
     def step(k, carry):
         fn(k)
@@ -1015,7 +1090,7 @@
     tokens, cot, w_x, w_bc, w_z, w_out, w_dt, conv_x, conv_bc, norm_gain, gate_gain, dt_bias, a_log, skip, starts, fill,
     vec, px_out, pbd_out, normed_out, normed_t_out, q_out, y_out, sin_out, parts, rows_x, rows_bd, rows_z, rows_out,
     own_dt, tok, wx, wbd, px, pbd, normed, normed_t, q, y, sin, own_w, own_cot, state, extx, extb, upper, spread,
-    s_loc, s_sib, r_sib, s_x, r_x, s_f, r_f, s_cx, r_cx, s_cf, r_cf, s_w, r_w, s_out, s_y,
+    s_loc, s_sib, r_sib, s_x, r_x, s_f, r_f, s_cx, r_cx, s_cf, r_cf, s_w, r_w, s_c, r_c, s_cy, r_cy, s_out, s_y,
 ):
     who = peers(dp_n)
     count, quarter = tokens.shape
@@ -1080,9 +1155,12 @@
         shares(ref, to, dp_n, cols, s_w.at[n], r_w.at[n], who)
         for n, (ref, to, cols) in enumerate((
             (w_x, wx, pl.ds(0, half)), (w_x, wx, pl.ds(half, half)), (w_bc, wbd, own_half), (own_dt, wbd, dt_cols),
-            (w_z, rows_z, pl.ds(0, half)), (w_z, rows_z, pl.ds(half, half)),
-            (w_out, rows_out, pl.ds(0, half)), (w_out, rows_out, pl.ds(half, half)),
         ))
+    ]
+    chains = [
+        chain(ref, to, pl.ds(h * half, half), s_c.at[2 * n + h], r_c.at[2 * n + h], s_cy.at[2 * n + h], r_cy.at[2 * n + h], who)
+        for n, (ref, to) in enumerate(((w_z, rows_z), (w_out, rows_out)))
+        for h in (0, 1)
     ]
 
     def offer(n):
@@ -1120,8 +1198,8 @@
         offer(n)
     for j in range(pieces):
         cot_x(j).start()
-    for n in (4, 5, 6, 7):
-        offer(n)
+    for begin, begin_pair, hop, end in chains:
+        begin()
     pack_vec(vec, conv_x, conv_bc, norm_gain, gate_gain, dt_bias, a_log, skip, starts, fill, chunk)
     set_upper(upper)
     set_spread(spread, heads)
@@ -1209,8 +1287,14 @@
 
     events = {1: [(last_tokens, units - 1)], 2: [(last_norm, units - 1)]}
     late = []
-    plan = [(pass_rows, 4, 3), (pass_rows, 5, 7), (pass_rows, 6, 11)]
-    plan += [(pass_cot, j, 5 + 2 * j) for j in range(pieces)] + [(pass_rows, 7, 15)]
+    plan = []
+    for n, (begin, begin_pair, hop, end) in enumerate(chains):
+        plan.append((lambda k, fn=begin_pair: fn(), 0, 1 + 2 * n))
+        for j in range(1, min(lines, 4)):
+            plan.append((hop, j, 1 + 2 * n + j))
+        if lines > 4:
+            plan.append((lambda k, fn=hop: lax.fori_loop(4, lines, lambda j, a: (fn(j), a)[1], 0), 0, 5 + 2 * n))
+    plan += [(pass_cot, j, 5 + 2 * j) for j in range(pieces)]
     for fn, k, at in plan:
         if at < blocks:
             events.setdefault(at, []).append((fn, k))
@@ -1264,8 +1348,8 @@
     cot_sib().wait()
     for j in range(pieces):
         cot_forward(j).wait()
-    for n in (4, 5, 6, 7):
-        have(n)
+    for begin, begin_pair, hop, end in chains:
+        end()
 
 
 def front(dp_n, tokens, cot, w_x, w_bc, w_z, w_out, w_dt, conv_x, conv_bc, norm_gain, gate_gain, *scalars):
@@ -1302,7 +1386,8 @@
             vm((chunk, chunk), BF), vm((chunk, 3 * inner), BF),
             dma((11,)), dma((3,)), dma((3,)), dma((units,)), dma((units,)), dma((units,)), dma((units,)),
             dma((pieces,)), dma((pieces,)), dma((pieces,)), dma((pieces,)),
-            dma((8, ways)), dma((8, ways)), dma((5, units)), dma((2, blocks)),
+            dma((4, ways)), dma((4, ways)), dma((4, ways + 1)), dma((4, ways + 1)), dma((4, ways)), dma((4, ways)),
+            dma((5, units)), dma((2, blocks)),
         ],
         compiler_params=pltpu.CompilerParams(
             collective_id=2, has_side_effects=True, vmem_limit_bytes=58 * 2**20
@@ -1311,6 +1396,46 @@
     )(
         tokens, cot, w_x, w_bc, w_z, w_out, w_dt, conv_x, conv_bc, norm_gain[None, :], gate_gain[None, :], *scalars
     )
+def finish_kernel(heads, taps, bc, bo, gt, gx, gz, go, gb, small, own, o_bo, o_gt, o_gx, o_gz, o_go, o_gb, o_gain, o_cx, o_cb, o_bias, o_alog, o_skip, o_gate):
+    o_bo[...] = bo[...]
+    o_gt[...] = gt[...]
+
+    @pl.when(pl.program_id(0) == 0)
+    def _():
+        for src, dst in ((gx, o_gx), (gz, o_gz), (go, o_go), (gb, o_gb)):
+            dst[...] = src[...]
+        inner = o_cx.shape[1]
+        per = small.shape[1] // inner
+        for k in range(taps):
+            o_cx[k : k + 1, :] = small[2 + k // per : 3 + k // per, (k % per) * inner : (k % per + 1) * inner]
+            o_cb[k : k + 1, :] = small[1:2, k * bc : (k + 1) * bc]
+        scalars = small[5:6, :128]
+        o_bias[...] = scalars[0, :heads]
+        o_alog[...] = scalars[0, heads : 2 * heads]
+        o_skip[...] = scalars[0, 2 * heads : 3 * heads]
+        o_gate[...] = small[4, :inner]
+        columns = o_gain.shape[0]
+        at = pl.ds(pl.multiple_of(lax.axis_index("heads") * columns, columns), columns)
+        o_gain[...] = (small[0:1, at] / own[:, at])[0]
+
+
+def finish(bo, gt, gx, gz, go, gb, small, norm_gain, heads, taps, bc):
+    steps = 4
+    sds = jax.ShapeDtypeStruct
+    count, quarter = bo.shape
+    inner = gx.shape[1]
+    rows = pl.BlockSpec((count // steps, quarter), lambda i: (i, 0))
+    whole = lambda shape: pl.BlockSpec(shape, lambda i: (0,) * len(shape))
+    smalls = [(quarter,), (taps, inner), (taps, bc), (heads,), (heads,), (heads,), (inner,)]
+    operands = (bo, gt, gx, gz, go, gb, small, norm_gain[None, :])
+    return pl.pallas_call(
+        functools.partial(finish_kernel, heads, taps, bc),
+        grid=(steps,),
+        in_specs=[rows, rows] + [whole(a.shape) for a in operands[2:]],
+        out_specs=[rows, rows] + [whole(a.shape) for a in operands[2:6]] + [whole(s) for s in smalls],
+        out_shape=[sds(a.shape, a.dtype) for a in operands[:6]] + [sds(s, F32) for s in smalls],
+        name="finish",
+    )(*operands)
 
 
 def body(
@@ -1319,7 +1444,6 @@
 ):
     heads_n = lax.axis_size("heads")
     dp_n = lax.axis_size("dp")
-    head_index = lax.axis_index("heads")
     dp_index = lax.axis_index("dp")
     count, columns = tokens.shape
     width = columns * heads_n
@@ -1341,13 +1465,16 @@
         dp_n, 4, normed_t, normed, lpx, lpz, lpbd, rows_x, rows_z, rows_bd, tokens, acc, cotangent, q_wide, vec, bc,
     )
     block = width // dp_n
-    own_gain = lax.dynamic_slice_in_dim(norm_gain, head_index * columns, columns, 0)
-    gain_sum = lax.dynamic_slice_in_dim(small[0], head_index * columns, columns, 0)
     grad_w_dt = lax.dynamic_slice_in_dim(small[8 : 8 + heads], dp_index * block, block, 1).T
+    (
+        block_out, grad_tokens, grad_w_x, grad_w_z, grad_w_out, grad_w_bc, grad_norm_gain, grad_conv_x, grad_conv_bc,
+        grad_dt_bias, grad_a_log, grad_skip, grad_gate_gain,
+    ) = finish(
+        block_out, grad_tokens, grad_w_x, grad_w_z, grad_w_out, grad_w_bc, small, norm_gain, heads, taps, bc
+    )
     return (
-        block_out, grad_tokens, gain_sum / own_gain, grad_w_x, grad_w_z, grad_w_dt, grad_w_bc,
-        small[2:4].reshape(taps, inner), small[1].reshape(taps, bc), small[5, :heads], small[5, heads : 2 * heads],
-        small[5, 2 * heads : 3 * heads], small[4, :inner], grad_w_out,
+        block_out, grad_tokens, grad_norm_gain, grad_w_x, grad_w_z, grad_w_dt, grad_w_bc, grad_conv_x, grad_conv_bc,
+        grad_dt_bias, grad_a_log, grad_skip, grad_gate_gain, grad_w_out,
     )
 
 

time: 220 us -> 209 us (0.950)
  local copies, waits for them, and re-layouts: 13.5 us -> 2.75 us
    pallas_call x1, Pallas kernels: 58.3 us -> 51.7 us  [scan_backward(): pl.pallas_call(functools.partial(scan_bwd_kernel, heads, total_inner, tap...]
    unnamed x19 -> x1, local copies, waits for them, and re-layouts: 6.48 us -> 1.4 us
    pallas_call x0 -> x1, Pallas kernels: none -> 4.93 us  [finish(): pl.pallas_call(functools.partial(finish_kernel, heads, taps, bc), grid=(s...]
    slice x3 -> x0, local copies, waits for them, and re-layouts: 2.91 us -> none  [the longest x1 1.3 us: body(): small[4, :inner]]
    pallas_call x1, Pallas kernels: 68.8 us -> 71.5 us  [front(): pl.pallas_call(functools.partial(front_kernel, dp_n, heads, units, taps,...]
where the time goes in v7:
time: 209 us; the launch traced here: 208 us
  Pallas kernels  205 us (98%)
  local copies, waits for them, and re-layouts  2.75 us (1%)
    pallas_call x1, Pallas kernels, front(): pl.pallas_call(functools.partial(front_kernel, dp_n, heads, units, taps,...  71.5 us
    pallas_call x1, Pallas kernels, tail(): pl.pallas_call(functools.partial(tail_kernel, dp_n, units), out_shape=[sd...  56.9 us
    pallas_call x1, Pallas kernels, scan_backward(): pl.pallas_call(functools.partial(scan_bwd_kernel, heads, total_inner, tap...  51.7 us
    pallas_call x1, Pallas kernels, gate(): pl.pallas_call(functools.partial(gate_kernel, dp_n), grid=(steps,), in_sp...  19.5 us
    pallas_call x1, Pallas kernels, finish(): pl.pallas_call(functools.partial(finish_kernel, heads, taps, bc), grid=(s...  4.93 us

profile of v7, /device:TPU:0, one launch (start us, length us, event | category | flops | bytes accessed | tf_op | source)
XLA Modules:
  0.0 208.0 jit_solution(10973574613550407503)
XLA Ops:
  0.6 1.4 copy.30.w_dt
  2.0 71.5 %front.1 = (f32[40,1024]{1,0:T(8,128)}, f32[2048,512]{1,0:T(8,128)}, f32[2048,384]{1,0:T(8,128)}, bf16[2048,1024]{1,0:T(8,128)(2,1)}, bf16[1024,2048]{1,0:T(8,12...) custom-call(bf16[2048,256]{1,0:T(8,128)(2,1)} %tokens.5, ...), custom_call_target="tpu_custom_call" | custom-call | tf_op jit(solution)/shard_map/front/pallas_call | solution.py:1374
  73.6 19.5 %gate.1 = (f32[2048,512]{1,0:T(8,128)}, f32[2048,512]{1,0:T(8,128)}, f32[2,16,128]{2,1,0:T(8,128)}, bf16[2048,512]{1,0:T(8,128)(2,1)}, bf16[2,512,256]{2,1,0:T(8,128)(2,1)}, /*index=5*/f32[2,512,256]{2,1,0:T(8,128)}) custom-call(bf16[2048,1024]{1,0:T(8,128)(2,1)} %get-tuple-element.57.normed.normed_in, bf16[1024,512]{1,0:T(8,128)(2,1)} %get-tuple-element.58.rows_z.rows_z_in, ...), custom_call_target="tpu_custom_call" | custom-call | tf_op jit(solution)/shard_map/gate/pallas_call | solution.py:266
  93.1 51.7 %scan_backward.1 = (bf16[2048,512]{1,0:T(8,128)(2,1)}, bf16[2048,512]{1,0:T(8,128)(2,1)}, bf16[2048,384]{1,0:T(8,128)(2,1)}, f32[8,1024]{1,0:T(8,128)}, bf16[2048,256]{1,0:T(8,128)(2,1)}, /*index=5*/f32[128,512]{1,0:T(8,128)}) custom-call(f32[2048,512]{1,0:T(8,128)} %get-tuple-element.63.ggn, f32[2048,512]{1,0:T(8,128)} %get-tuple-element.61.y, ...), custom_call_target="tpu_custom_call" | custom-call | tf_op jit(solution)/shard_map/scan_backward/pallas_call | solution.py:569
  144.8 56.9 %tail.1 = (f32[2048,256]{1,0:T(8,128)}, f32[128,512]{1,0:T(8,128)}, f32[128,512]{1,0:T(8,128)}, f32[128,256]{1,0:T(8,128)}, f32[24,1024]{1,0:T(8,128)}) custom-call(bf16[1024,2048]{1,0:T(8,128)(2,1)} %get-tuple-element.73.normed_t_in, bf16[2048,512]{1,0:T(8,128)(2,1)} %get-tuple-element.74.lpz_in, bf16[1024,512]{1,0:T(8,128)(2,1)} %get-tuple-element.58.rows_z.rows_z_in, ...), custom_call_target="tpu_custom_call" | custom-call | tf_op jit(solution)/shard_map/tail/pallas_call | solution.py:939
  201.7 4.9 %finish.1 = (bf16[2048,256]{1,0:T(8,128)(2,1)}, f32[2048,256]{1,0:T(8,128)}, f32[128,512]{1,0:T(8,128)}, f32[128,512]{1,0:T(8,128)}, f32[128,512]{1,0:T(8,128)},...) custom-call(bf16[2048,256]{1,0:T(8,128)(2,1)} %get-tuple-element.72., ...), custom_call_target="tpu_custom_call" | custom-call | tf_op jit(solution)/shard_map/finish/pallas_call | solution.py:1431
  206.7 0.8 slice.3
  207.4 0.6 dynamic-slice_bitcast_fusion

commit v8 on v7

--- a/solution.py
+++ b/solution.py
@@ -195,8 +195,8 @@
 
 
 def gate_kernel(
-    dp_n, normed, rows_z, rows_out, parts, y, vec, pz, ggn, sums, gn, y_send, g_own,
-    h_send, h_recv, gated_all, grad_t, s_h, r_h,
+    dp_n, normed, rows_z, rows_out, parts, y, vec, normed_t_in, dy_out, lpz, gn, y_send, g_own, gain_grad,
+    h_send, h_recv, z_all, g_all, y_all, grad_t, normed_t, s_h, r_h, s_in,
 ):
     i = pl.program_id(0)
     who = peers(dp_n)
@@ -206,22 +206,24 @@
     blocks, chunk = h_send.shape[1:]
     inner = y.shape[1]
     here = pl.ds(pl.multiple_of(i * span, span), span)
+    load = pltpu.make_async_copy(normed_t_in, normed_t, s_in.at[0])
 
     @pl.when(i == 0)
     def _():
+        load.start()
         for name in names:
             pl.semaphore_signal(barrier, inc=1, device_id=who[name], device_id_type=MESH)
 
     z = nn(normed[...], rows_z[...])
-    pz[...] = z
+    z_all[here, :] = z
+    y_all[here, :] = y[...]
     g = nn(parts[0], rows_out[0:quarter, :])
     for k in range(1, 4):
         g = g + nn(parts[k], rows_out[k * quarter : (k + 1) * quarter, :])
-    ggn[...] = g
+    g_all[here, :] = g
     for k in range(4):
         grad_t[k * quarter : (k + 1) * quarter, here] = jnp.transpose(parts[k])
     gated = y[...] * (z * sigmoid(z))
-    gated_all[here, :] = gated
     ones = jnp.ones((8, inner), BF)
     for k, value in enumerate((gated * gated, gated * vec[5:6, :inner] * g)):
         row = nt(ones, value.astype(BF))
@@ -236,23 +238,36 @@
             copy.start()
         for copy in copies:
             copy.wait()
-        sums[...] = h_send[...] + h_recv[0] + h_recv[1] + h_recv[2]
+        sums = h_send[...] + h_recv[0] + h_recv[1] + h_recv[2]
         gain = vec[5:6, :inner]
-        squares = jnp.transpose(
-            jnp.concatenate([sums[0], jnp.zeros((chunk - blocks, chunk), F32)], axis=0)
-        )
-        inv = lax.rsqrt(squares / (4 * inner) + EPS)
+        below = jnp.zeros((chunk - blocks, chunk), F32)
+        inv = lax.rsqrt(jnp.transpose(jnp.concatenate([sums[0], below], axis=0)) / (4 * inner) + EPS)
+        dots = jnp.transpose(jnp.concatenate([sums[1], below], axis=0))
+        coef = inv * inv * inv * (dots / (4 * inner))
+        gain_grad[...] = jnp.zeros_like(gain_grad)
         for b in range(blocks):
             at = slice(b * chunk, (b + 1) * chunk)
-            gn[at, :] = (gated_all[at, :] * inv[:, b : b + 1] * gain).astype(BF)
+            zb, yb, gb = z_all[at, :], y_all[at, :], g_all[at, :]
+            sz = sigmoid(zb)
+            silu_z = zb * sz
+            gated_b = yb * silu_z
+            inv_b = inv[:, b : b + 1]
+            scaled = gated_b * inv_b
+            gn[at, :] = (scaled * gain).astype(BF)
+            gain_grad[0:1, :] += jnp.sum(gb * scaled, axis=0, keepdims=True)
+            d_gated = inv_b * (gb * gain) - gated_b * coef[:, b : b + 1]
+            lpz[at, :] = (d_gated * yb * (sz * (1.0 + zb * (1.0 - sz)))).astype(BF)
+            dy_out[at, :] = d_gated * silu_z
+        load.wait()
         block = grad_t.shape[0] // dp_n
-        for v in range(2):
-            cols = slice(v * (inner // 2), (v + 1) * (inner // 2))
-            y_send[v] = nn(pair_rows(dp_n, block, 1 - who["pair"], grad_t), gn[:, cols]).astype(BF)
-            g_own[v] = nn(pair_rows(dp_n, block, who["pair"], grad_t), gn[:, cols])
-
-
-def gate(dp_n, blocks, normed, rows_z, rows_out, parts, y, vec):
+        for v in range(4):
+            left, right = ((grad_t, gn), (normed_t, lpz))[v // 2]
+            cols = slice((v % 2) * (inner // 2), (v % 2 + 1) * (inner // 2))
+            y_send[v] = nn(pair_rows(dp_n, block, 1 - who["pair"], left), right[:, cols]).astype(BF)
+            g_own[v] = nn(pair_rows(dp_n, block, who["pair"], left), right[:, cols])
+
+
+def gate(dp_n, blocks, normed, normed_t, rows_z, rows_out, parts, y, vec):
     count, width = normed.shape
     inner = y.shape[1]
     chunk = count // blocks
@@ -262,36 +277,36 @@
     sds = jax.ShapeDtypeStruct
     rows = lambda w: pl.BlockSpec((span, w), lambda i: (i, 0))
     whole = lambda shape: pl.BlockSpec(shape, lambda i: (0,) * len(shape))
-    halves = (2, width // 2, inner // 2)
+    halves = (4, width // 2, inner // 2)
     return pl.pallas_call(
         functools.partial(gate_kernel, dp_n),
         grid=(steps,),
         in_specs=[
             rows(width), whole(rows_z.shape), whole(rows_out.shape),
             pl.BlockSpec((4, span, quarter), lambda i: (0, i, 0)), rows(inner), whole(vec.shape),
+            pl.BlockSpec(memory_space=pl.ANY),
         ],
-        out_specs=[
-            rows(inner), rows(inner), whole((2, blocks, chunk)), whole((count, inner)), whole(halves), whole(halves),
-        ],
+        out_specs=[whole((count, inner))] * 3 + [whole(halves), whole(halves), whole((8, inner))],
         out_shape=[
-            sds((count, inner), F32), sds((count, inner), F32), sds((2, blocks, chunk), F32), sds((count, inner), BF),
-            sds(halves, BF), sds(halves, F32),
+            sds((count, inner), F32), sds((count, inner), BF), sds((count, inner), BF), sds(halves, BF),
+            sds(halves, F32), sds((8, inner), F32),
         ],
         scratch_shapes=[
             pltpu.VMEM((2, blocks, chunk), F32), pltpu.VMEM((3, 2, blocks, chunk), F32),
-            pltpu.VMEM((count, inner), F32), pltpu.VMEM((width, count), BF),
-            pltpu.SemaphoreType.DMA((3,)), pltpu.SemaphoreType.DMA((3,)),
+            pltpu.VMEM((count, inner), F32), pltpu.VMEM((count, inner), F32), pltpu.VMEM((count, inner), F32),
+            pltpu.VMEM((width, count), BF), pltpu.VMEM((width, count), BF),
+            pltpu.SemaphoreType.DMA((3,)), pltpu.SemaphoreType.DMA((3,)), pltpu.SemaphoreType.DMA((1,)),
         ],
         compiler_params=pltpu.CompilerParams(
             collective_id=4, has_side_effects=True, vmem_limit_bytes=58 * 2**20
         ),
         name="gate",
-    )(normed, rows_z, rows_out, parts, y, vec)
+    )(normed, rows_z, rows_out, parts, y, vec, normed_t)
 
 
 def sums_beside_scan(
-    dp_n, gn, rows_out, tokens, y_send, g_in, block_out, g_out,
-    sib_send, sib_recv, x_send, x_recv, part, held, y_recv, z_send, z_recv, g_own,
+    dp_n, gn_in, rows_out_in, tokens_in, y_send_in, g_in_in, block_out, g_out, g_z,
+    gn, rows_out, tokens, y_send, g_in, s_in, sib_send, sib_recv, x_send, x_recv, part, held, y_recv, z_send, z_recv, g_own,
     s_sib, r_sib, s_x, r_x, s_y, r_y, s_z, r_z,
 ):
     i = pl.program_id(0)
@@ -317,11 +332,26 @@
             z_recv.at[v, k - 1], s_z.at[v, k - 1], r_z.at[v, k - 1], who["line"](k),
         )
 
+    loads = [
+        pltpu.make_async_copy(src, dst, s_in.at[n])
+        for n, (src, dst) in enumerate((
+            (y_send_in, y_send), (rows_out_in, rows_out), (gn_in, gn), (tokens_in, tokens), (g_in_in, g_in),
+        ))
+    ]
+
     @pl.when(i == 0)
     def _():
+        for load in loads:
+            load.start()
         meet(who)
-        for v in range(2):
+        loads[0].wait()
+        for v in range(4):
             copy_y(v).start()
+
+    @pl.when(i == 1)
+    def _():
+        for load in loads[1:]:
+            load.wait()
 
     def first(k):
         for n, q in enumerate(("sib_mine", "sib_other", "mine", "other")):
@@ -355,11 +385,11 @@
         total = g_own[v, pl.ds(pl.multiple_of(who["line_index"] * block, block), block), :]
         for k in range(lines - 1):
             total = total + z_recv[v, k].astype(F32)
-        g_out[:, v * half : (v + 1) * half] = total
-
-    events = [(grad_b, 0, 4), (grad_b, 1, 7)]
+        (g_out, g_z)[v // 2][:, (v % 2) * half : (v % 2 + 1) * half] = total
+
+    events = [(grad_b, 0, 3), (grad_b, 1, 6), (grad_b, 2, 8), (grad_b, 3, 11)]
     for k in range(units):
-        events += [(first, k, 2 * k), (second, k, 2 * k + 1), (third, k, 2 * k + 6)]
+        events += [(first, k, 2 * k + 1), (second, k, 2 * k + 2), (third, k, 2 * k + 7)]
     for at in sorted({e[2] for e in events}):
 
         @pl.when(i == at)
@@ -369,19 +399,19 @@
                     fn(k)
 
     def finish():
-        for v in range(2):
+        for v in range(4):
             grad_c(v)
 
     return finish
 
 
 def scan_bwd_kernel(
-    heads, total_inner, taps_n, bc, dp_n, ggn, y, pz, px, px_halo, pbd, pbd_halo, sin, rows, vec, gn, rows_out, tokens,
+    heads, taps_n, bc, dp_n, dy_in, px, px_halo, pbd, pbd_halo, sin, gain_grad, vec, gn, rows_out, tokens,
     y_send, g_in,
-    lpx, lpz, lpbd, acc, block_out, g_out, dstate, extx, extb, dux, dub, acc_x, acc_bc, acc_s, upper, spread, gather, ones_h,
+    lpx, lpbd, acc, block_out, g_out, g_z, dstate, extx, extb, dux, dub, acc_x, acc_bc, acc_s, upper, spread, gather, ones_h,
     *beside,
 ):
-    finish = sums_beside_scan(dp_n, gn, rows_out, tokens, y_send, g_in, block_out, g_out, *beside)
+    finish = sums_beside_scan(dp_n, gn, rows_out, tokens, y_send, g_in, block_out, g_out, g_z, *beside)
     i = pl.program_id(0)
     blocks = pl.num_programs(0)
     c = blocks - 1 - i
@@ -389,33 +419,18 @@
     ns = bc // 2
     par = read_vec(vec, heads, chunk, inner, bc, taps_n)
     keep, n_live, keep_next = read_block(vec, c, chunk)
-    taps, taps_b, bias, rate, skip, gain = (par[k] for k in ("convx", "convbc", "bias", "rate", "skip", "gain"))
+    taps, taps_b, bias, rate, skip = (par[k] for k in ("convx", "convbc", "bias", "rate", "skip"))
 
     @pl.when(i == 0)
     def _():
         for ref in (dstate, dux, dub, acc_x, acc_bc, acc_s):
             ref[...] = jnp.zeros_like(ref)
+        acc_x[taps_n : taps_n + 1, :] = gain_grad[0:1, :]
         set_upper(upper)
         set_spread(spread, heads)
         set_gather(gather, ones_h, heads)
 
-    moved = jnp.transpose(
-        jnp.concatenate(
-            [rows[0, pl.ds(c, 1), :], rows[1, pl.ds(c, 1), :], jnp.zeros((chunk - 2, chunk), F32)], axis=0
-        )
-    )
-    inv = lax.rsqrt(moved[:, 0:1] / total_inner + EPS)
-    coef = inv * inv * inv * (moved[:, 1:2] / total_inner)
-    z = pz[...]
-    sz = sigmoid(z)
-    silu_z = z * sz
-    yv = y[...]
-    gated = yv * silu_z
-    g = ggn[...]
-    d_gated = inv * (g * gain) - gated * coef
-    lpz[...] = (d_gated * yv * (sz * (1.0 + z * (1.0 - sz)))).astype(BF)
-    dy = d_gated * silu_z
-    acc_x[taps_n : taps_n + 1, :] += jnp.sum(g * gated * inv, axis=0, keepdims=True)
+    dy = dy_in[...]
 
     extx[0:8, :] = jnp.where(keep, px_halo[...], 0.0)
     extb[0:8, :] = jnp.where(keep, pbd_halo[:, :bc], 0.0)
@@ -549,7 +564,7 @@
 
 
 def scan_backward(
-    dp_n, ggn, y, pz, px, pbd, sin, rows, vec, gn, rows_out, tokens, y_send, g_own, heads, taps, bc, total_inner
+    dp_n, dy, px, pbd, sin, gain_grad, vec, gn, rows_out, tokens, y_send, g_own, heads, taps, bc
 ):
     count, inner = px.shape
     blocks = sin.shape[0]
@@ -567,38 +582,41 @@
     dma = pltpu.SemaphoreType.DMA
     vm, sds = pltpu.VMEM, jax.ShapeDtypeStruct
     return pl.pallas_call(
-        functools.partial(scan_bwd_kernel, heads, total_inner, taps, bc, dp_n),
+        functools.partial(scan_bwd_kernel, heads, taps, bc, dp_n),
         grid=(blocks,),
         in_specs=[
-            back(inner), back(inner), back(inner), back(inner), halo(inner), back(width), halo(width),
-            pl.BlockSpec((1, bc // 2, inner), lambda i: (blocks - 1 - i, 0, 0)), whole(rows), whole(vec),
-            whole(gn), whole(rows_out), whole(tokens), whole(y_send), whole(g_own),
-        ],
+            back(inner), back(inner), halo(inner), back(width), halo(width),
+            pl.BlockSpec((1, bc // 2, inner), lambda i: (blocks - 1 - i, 0, 0)), whole(gain_grad), whole(vec),
+        ]
+        + [pl.BlockSpec(memory_space=pl.ANY)] * 5,
         out_specs=[
-            back(inner), back(inner), back(width), pl.BlockSpec((8, vec.shape[1]), lambda i: (0, 0)),
-            whole(tokens), pl.BlockSpec((block, inner), lambda i: (0, 0)),
+            back(inner), back(width), pl.BlockSpec((8, vec.shape[1]), lambda i: (0, 0)),
+            whole(tokens), pl.BlockSpec((block, inner), lambda i: (0, 0)), pl.BlockSpec((block, inner), lambda i: (0, 0)),
         ],
         scratch_shapes=[
             vm((bc // 2, inner), F32), vm((chunk + 8, inner), F32), vm((chunk + 8, bc), F32),
             vm((chunk + 8, inner), F32), vm((chunk + 8, bc), F32),
             vm((8, inner), F32), vm((8, bc), F32), vm((2 * heads, chunk), F32),
             vm((chunk, chunk), BF), vm((chunk, 3 * inner), BF), vm((3, inner, chunk), BF), vm((heads * chunk, chunk), BF),
+            vm(gn.shape, BF), vm(rows_out.shape, BF), vm(tokens.shape, BF), vm(y_send.shape, BF), vm(g_own.shape, F32),
+            dma((5,)),
             vm((units, 2, span, quarter), BF), vm((units, 2, span, quarter), BF),
             vm((units, span, quarter), BF), vm((units, span, quarter), BF),
             vm((2, span, quarter), F32), vm((units, span, quarter), F32),
-            vm(y_send.shape, BF), vm(y_send.shape, BF), vm((2, more, block, inner // 2), BF), vm(y_send.shape, F32),
-            dma((units,)), dma((units,)), dma((units,)), dma((units,)), dma((2,)), dma((2,)),
-            dma((2, more)), dma((2, more)),
+            vm(y_send.shape, BF), vm(y_send.shape, BF), vm((4, more, block, inner // 2), BF), vm(y_send.shape, F32),
+            dma((units,)), dma((units,)), dma((units,)), dma((units,)), dma((4,)), dma((4,)),
+            dma((4, more)), dma((4, more)),
         ],
         out_shape=[
-            sds((count, inner), BF), sds((count, inner), BF), sds((count, width), BF),
+            sds((count, inner), BF), sds((count, width), BF),
             sds((8, vec.shape[1]), F32), sds(tokens.shape, BF), sds((block, inner), F32),
+            sds((block, inner), F32),
         ],
         compiler_params=pltpu.CompilerParams(
             collective_id=3, has_side_effects=True, vmem_limit_bytes=58 * 2**20
         ),
         name="scan_backward",
-    )(ggn, y, pz, px, px, pbd, pbd, sin, rows, vec, gn, rows_out, tokens, y_send, g_own)
+    )(dy, px, px, pbd, pbd, sin, gain_grad, vec, gn, rows_out, tokens, y_send, g_own)
 def peers(dp_n):
     dp, hm = lax.axis_index("dp"), lax.axis_index("heads")
     across, core = hm // 2, hm % 2
@@ -638,19 +656,19 @@
 
 def tail_kernel(
     dp_n, units,
-    normed_t_in, lpz_in, rows_z_in, lpx_in, rows_x_in, lpbd_in, rows_bd_in, normed_in,
+    normed_t_in, lpx_in, rows_z_in, lpz_in, rows_x_in, lpbd_in, rows_bd_in, normed_in,
     tokens, acc, cot, q_wide, vec,
-    grad_tokens, g_x, g_z, g_bc, small_out,
+    grad_tokens, g_x, g_bc, small_out,
     sib_send, sib_recv, x_send, x_recv, part, held,
     y_send, y_recv, z_send, z_recv, g_own, yb_send, yb_recv, zb_send, zb_recv, gb_own, bh_send, bh_recv,
     bx_send, bx_recv, bs_recv, h_send, h_recv, sy_send, sy_recv, sz_send, sz_recv, dy_send, dy_recv, dz_send, dz_recv, row_sums,
-    normed_t, lpz, rows_z, lpx, rows_x, lpbd, rows_bd, normed,
+    normed_t, lpx, rows_z, lpz, rows_x, lpbd, rows_bd, normed,
     s_in, s_sib, r_sib, s_x, r_x, s_y, r_y, s_z, r_z, s_m, r_m, s_sl, r_sl,
 ):
     loads = [
         pltpu.make_async_copy(src, dst, s_in.at[i])
         for i, (src, dst) in enumerate((
-            (normed_t_in, normed_t), (lpz_in, lpz), (rows_z_in, rows_z), (lpx_in, lpx), (rows_x_in, rows_x),
+            (normed_t_in, normed_t), (lpx_in, lpx), (rows_z_in, rows_z), (lpz_in, lpz), (rows_x_in, rows_x),
             (lpbd_in, lpbd), (rows_bd_in, rows_bd), (normed_in, normed),
         ))
     ]
@@ -724,7 +742,7 @@
         return pl.ds(pl.multiple_of((2 * line + pair) * block, block), block)
 
     def grad_a(v):
-        left, right = ((normed_t, lpz), (normed_t, lpx))[v // 2]
+        left, right = (normed_t, lpx)
         cols = slice((v % 2) * (inner // 2), (v % 2 + 1) * (inner // 2))
         for side in (0, 1):
             pair = (1 - who["pair"]) if side == 0 else who["pair"]
@@ -768,7 +786,7 @@
         for k in range(lines - 1):
             total = total + z_recv[v, k].astype(F32)
         cols = slice((v % 2) * (inner // 2), (v % 2 + 1) * (inner // 2))
-        (g_z, g_x)[v // 2][:, cols] = total
+        g_x[:, cols] = total
 
     half = bc // 2
 
@@ -912,12 +930,12 @@
             loads[i].wait()
 
     load(0, 1)
-    seq((grad_a, 0), (grad_a, 1))
+    grad_a(0)
     load(2, 3, 4, 5, 6, 7)
-    seq((head_a, 0), (bc_a,), (head_a, 1), (head_b, 0), (grad_a, 2), (bc_b,), (head_b, 1), (grad_b, 0), (head_a, 2))
-    seq((grad_a, 3), (head_b, 2), (dt_a,), (grad_b, 1), (head_a, 3), (small_a,), (bc_c,), (head_b, 3), (dt_b,))
-    seq((small_b,), (grad_b, 2), (grad_c, 0), (small_c,), (bc_d,), (dt_c,), (head_c, 0), (grad_b, 3), (grad_c, 1))
-    seq((bc_e,), (head_c, 1), (small_d,), (head_c, 2), (grad_c, 2), (bc_f,), (head_c, 3), (grad_c, 3))
+    seq((head_a, 0), (bc_a,), (head_b, 0), (head_a, 1), (bc_b,), (grad_a, 1), (head_b, 1), (grad_b, 0), (head_a, 2))
+    seq((dt_a,), (head_b, 2), (head_a, 3), (small_a,), (bc_c,), (head_b, 3), (grad_b, 1), (dt_b,), (small_b,))
+    seq((bc_d,), (head_c, 0), (small_c,), (grad_c, 0), (dt_c,), (head_c, 1), (bc_e,), (small_d,), (bc_f,), (head_c, 2))
+    seq((grad_c, 1), (head_c, 3))
 
 
 def tail(dp_n, units, normed_t, normed, lpx, lpz, lpbd, rows_x, rows_z, rows_bd, tokens, acc, cot, q_wide, vec, bc):
@@ -932,25 +950,25 @@
     vm = pltpu.VMEM
     dma = pltpu.SemaphoreType.DMA
     operands = (
-        normed_t, lpz, rows_z, lpx, rows_x, lpbd, rows_bd, normed, tokens, acc, cot, q_wide, vec,
+        normed_t, lpx, rows_z, lpz, rows_x, lpbd, rows_bd, normed, tokens, acc, cot, q_wide, vec,
     )
     sds = jax.ShapeDtypeStruct
     spec = pl.BlockSpec(memory_space=pltpu.VMEM)
     return pl.pallas_call(
         functools.partial(tail_kernel, dp_n, units),
         out_shape=[
-            sds((count, quarter), F32), sds((block, inner), F32), sds((block, inner), F32), sds((block, bc), F32),
+            sds((count, quarter), F32), sds((block, inner), F32), sds((block, bc), F32),
             sds((24, width), F32),
         ],
         in_specs=[pl.BlockSpec(memory_space=pl.ANY)] * 8 + [spec] * 5,
-        out_specs=[spec] * 5,
+        out_specs=[spec] * 4,
         scratch_shapes=[
             vm((units, 2, span, quarter), BF), vm((units, 2, span, quarter), BF),
             vm((units, span, quarter), BF), vm((units, span, quarter), BF),
             vm((2, 2, span, quarter), F32), vm((units, span, quarter), F32),
-            vm((4, half_rows, inner // 2), BF), vm((4, half_rows, inner // 2), BF),
-            vm((4, half_rows, inner // 2), BF), vm((4, more, block, inner // 2), BF),
-            vm((4, half_rows, inner // 2), F32),
+            vm((2, half_rows, inner // 2), BF), vm((2, half_rows, inner // 2), BF),
+            vm((2, half_rows, inner // 2), BF), vm((2, more, block, inner // 2), BF),
+            vm((2, half_rows, inner // 2), F32),
             vm((half_rows, bc // 2), BF), vm((half_rows, bc // 2), BF),
             vm((half_rows, bc // 2), BF), vm((more, block, bc // 2), BF),
             vm((2 * half_rows, bc // 2), F32),
@@ -964,7 +982,7 @@
         + [vm(a.shape, a.dtype) for a in operands[:8]]
         + [
             dma((8,)), dma((units,)), dma((units,)), dma((units,)), dma((units,)),
-            dma((4,)), dma((4,)), dma((4, more)), dma((4, more)), dma((9,)), dma((9,)),
+            dma((2,)), dma((2,)), dma((2, more)), dma((2, more)), dma((9,)), dma((9,)),
             dma((3, more)), dma((3, more)),
         ],
         compiler_params=pltpu.CompilerParams(
@@ -972,37 +990,17 @@
         ),
         name="tail",
     )(*operands)
-def shares(ref_in, block_of, dp_n, width, send, recv, who):
-    rows = ref_in.shape[0]
-    lines = who["lines"]
-    source = ref_in.at[:, width] if ref_in.shape[1] != width.size else ref_in
-
-    def at(dp):
-        return block_of.at[pl.ds(pl.multiple_of(dp * rows, rows), rows), width]
-
-    def own():
-        return push(source, at(who["dp"]), send.at[0], recv.at[0], who["yn"])
-
-    def along(k):
-        return push(source, at(who["dp"]), send.at[k], recv.at[k], who["line"](k))
-
-    def onward(k):
-        there = at(2 * ((who["line_index"] - k + lines) % lines) + who["pair"])
-        return push(there, there, send.at[lines - 1 + k], recv.at[lines - 1 + k], who["yn"])
-
-    return own, along, onward
-
-
 def chain(ref_in, block_of, width, send, recv, y_send, y_recv, who):
     rows = ref_in.shape[0]
-    lines, line, pair, dp = who["lines"], who["line_index"], who["pair"], who["dp"]
+    lines, line, pair = who["lines"], who["line_index"], who["pair"]
+    own = ref_in.at[:, width] if ref_in.shape[1] != width.size else ref_in
 
     def at(index):
         return block_of.at[pl.ds(pl.multiple_of((2 * index + pair) * rows, rows), rows), width]
 
     def hand(sign, j):
         index = line - sign * j
-        source = ref_in.at[:, width] if isinstance(j, int) and j == 0 else at(index)
+        source = own if isinstance(j, int) and j == 0 else at(index)
         slot = j + 1 if sign > 0 else lines + j
         to = (2 * (line + sign) + pair, who["mine"])
         return push(source, at(index), send.at[slot], recv.at[slot], to)
@@ -1010,7 +1008,7 @@
     def to_pair(sign, j):
         slot = j if sign > 0 else lines - 1 + j
         index = line - sign * j
-        source = ref_in.at[:, width] if isinstance(j, int) and j == 0 else at(index)
+        source = own if isinstance(j, int) and j == 0 else at(index)
         return push(source, at(index), y_send.at[slot], y_recv.at[slot], who["yn"])
 
     def arrived(sign, j):
@@ -1090,7 +1088,7 @@
     tokens, cot, w_x, w_bc, w_z, w_out, w_dt, conv_x, conv_bc, norm_gain, gate_gain, dt_bias, a_log, skip, starts, fill,
     vec, px_out, pbd_out, normed_out, normed_t_out, q_out, y_out, sin_out, parts, rows_x, rows_bd, rows_z, rows_out,
     own_dt, tok, wx, wbd, px, pbd, normed, normed_t, q, y, sin, own_w, own_cot, state, extx, extb, upper, spread,
-    s_loc, s_sib, r_sib, s_x, r_x, s_f, r_f, s_cx, r_cx, s_cf, r_cf, s_w, r_w, s_c, r_c, s_cy, r_cy, s_out, s_y,
+    s_loc, s_sib, r_sib, s_x, r_x, s_f, r_f, s_cx, r_cx, s_cf, r_cf, s_w, r_w, s_wy, r_wy, s_c, r_c, s_cy, r_cy, s_out, s_y,
 ):
     who = peers(dp_n)
     count, quarter = tokens.shape
@@ -1152,7 +1150,7 @@
 
     half = inner // 2
     cuts = [
-        shares(ref, to, dp_n, cols, s_w.at[n], r_w.at[n], who)
+        chain(ref, to, cols, s_w.at[n], r_w.at[n], s_wy.at[n], r_wy.at[n], who)
         for n, (ref, to, cols) in enumerate((
             (w_x, wx, pl.ds(0, half)), (w_x, wx, pl.ds(half, half)), (w_bc, wbd, own_half), (own_dt, wbd, dt_cols),
         ))
@@ -1164,26 +1162,19 @@
     ]
 
     def offer(n):
-        loop_line(lines, lambda k: cuts[n][1](k).start())
+        cuts[n][0]()
 
     def other_half():
         cols = wbd.at[:, own_half]
         return push(cols, cols, s_sib.at[2], r_sib.at[2], who["sib"])
 
     def pass_rows(n):
-        own, along, onward = cuts[n]
-        own().start()
-
-        def one(k):
-            along(k).wait()
-            onward(k).start()
-
-        loop_line(lines, one)
+        begin, begin_pair, hop, end = cuts[n]
+        begin_pair()
+        loop_line(lines, hop)
 
     def have(n):
-        own, along, onward = cuts[n]
-        own().wait()
-        loop_line(lines, lambda k: onward(k).wait())
+        cuts[n][3]()
 
     def pass_cot(j):
         cot_x(j).wait()
@@ -1386,7 +1377,7 @@
             vm((chunk, chunk), BF), vm((chunk, 3 * inner), BF),
             dma((11,)), dma((3,)), dma((3,)), dma((units,)), dma((units,)), dma((units,)), dma((units,)),
             dma((pieces,)), dma((pieces,)), dma((pieces,)), dma((pieces,)),
-            dma((4, ways)), dma((4, ways)), dma((4, ways + 1)), dma((4, ways + 1)), dma((4, ways)), dma((4, ways)),
+            dma((4, ways + 1)), dma((4, ways + 1)), dma((4, ways)), dma((4, ways)), dma((4, ways + 1)), dma((4, ways + 1)), dma((4, ways)), dma((4, ways)),
             dma((5, units)), dma((2, blocks)),
         ],
         compiler_params=pltpu.CompilerParams(
@@ -1456,12 +1447,11 @@
         dp_n, tokens, cotangent, w_x, w_bc, w_z, w_out, w_dt, conv_x, conv_bc, norm_gain, gate_gain, dt_bias, a_log,
         skip, starts, fill,
     )
-    pz, ggn, sums, gn, y_send, g_own = gate(dp_n, blocks, normed, rows_z, rows_out, parts, y, vec)
-    lpx, lpz, lpbd, acc, block_out, grad_w_out = scan_backward(
-        dp_n, ggn, y, pz, px, pbd, sin, sums, vec, gn, rows_out, tokens, y_send, g_own, heads, taps, bc,
-        inner * heads_n,
+    dy, lpz, gn, y_send, g_own, gain_grad = gate(dp_n, blocks, normed, normed_t, rows_z, rows_out, parts, y, vec)
+    lpx, lpbd, acc, block_out, grad_w_out, grad_w_z = scan_backward(
+        dp_n, dy, px, pbd, sin, gain_grad, vec, gn, rows_out, tokens, y_send, g_own, heads, taps, bc
     )
-    grad_tokens, grad_w_x, grad_w_z, grad_w_bc, small = tail(
+    grad_tokens, grad_w_x, grad_w_bc, small = tail(
         dp_n, 4, normed_t, normed, lpx, lpz, lpbd, rows_x, rows_z, rows_bd, tokens, acc, cotangent, q_wide, vec, bc,
     )
     block = width // dp_n

time: 209 us -> 203 us (0.971)
  Pallas kernels: 205 us -> 199 us
    pallas_call x1, Pallas kernels: 56.9 us -> 48.8 us  [tail(): pl.pallas_call(functools.partial(tail_kernel, dp_n, units), out_shape=[sd...]
    pallas_call x1, Pallas kernels: 19.5 us -> 26 us  [gate(): pl.pallas_call(functools.partial(gate_kernel, dp_n), grid=(steps,), in_sp...]
    pallas_call x1, Pallas kernels: 51.7 us -> 46.6 us  [scan_backward(): pl.pallas_call(functools.partial(scan_bwd_kernel, heads, taps, bc, dp_n),...]
where the time goes in v8:
time: 203 us
  Pallas kernels  199 us (98%)
  local copies, waits for them, and re-layouts  2.75 us (1%)
    pallas_call x1, Pallas kernels, front(): pl.pallas_call(functools.partial(front_kernel, dp_n, heads, units, taps,...  73.2 us
    pallas_call x1, Pallas kernels, tail(): pl.pallas_call(functools.partial(tail_kernel, dp_n, units), out_shape=[sd...  48.8 us
    pallas_call x1, Pallas kernels, scan_backward(): pl.pallas_call(functools.partial(scan_bwd_kernel, heads, taps, bc, dp_n),...  46.6 us
    pallas_call x1, Pallas kernels, gate(): pl.pallas_call(functools.partial(gate_kernel, dp_n), grid=(steps,), in_sp...  26 us
    pallas_call x1, Pallas kernels, finish(): pl.pallas_call(functools.partial(finish_kernel, heads, taps, bc), grid=(s...  4.93 us

profile of v8, /device:TPU:0, one launch (start us, length us, event | category | flops | bytes accessed | tf_op | source)
XLA Modules:
  0.0 202.9 jit_solution(15814159854607843973)
XLA Ops:
  0.6 1.4 copy.30.w_dt
  2.0 73.2 %front.1 = (f32[40,1024]{1,0:T(8,128)}, f32[2048,512]{1,0:T(8,128)}, f32[2048,384]{1,0:T(8,128)}, bf16[2048,1024]{1,0:T(8,128)(2,1)}, bf16[1024,2048]{1,0:T(8,12...) custom-call(bf16[2048,256]{1,0:T(8,128)(2,1)} %tokens.5, ...), custom_call_target="tpu_custom_call" | custom-call | tf_op jit(solution)/shard_map/front/pallas_call | solution.py:1365
  75.2 26.0 %gate.1 = (f32[2048,512]{1,0:T(8,128)}, bf16[2048,512]{1,0:T(8,128)(2,1)}, bf16[2048,512]{1,0:T(8,128)(2,1)}, bf16[4,512,256]{2,1,0:T(8,128)(2,1)}, f32[4,512,256]{2,1,0:T(8,128)}, /*index=5*/f32[8,512]{1,0:T(8,128)}) custom-call(bf16[2048,1024]{1,0:T(8,128)(2,1)} %get-tuple-element.56.normed.normed_in, ...), custom_call_target="tpu_custom_call" | custom-call | tf_op jit(solution)/shard_map/gate/pallas_call | solution.py:281
  101.2 46.6 %scan_backward.1 = (bf16[2048,512]{1,0:T(8,128)(2,1)}, bf16[2048,384]{1,0:T(8,128)(2,1)}, f32[8,1024]{1,0:T(8,128)}, bf16[2048,256]{1,0:T(8,128)(2,1)}, f32[128,512]{1,0:T(8,128)}, /*index=5*/f32[128,512]{1,0:T(8,128)}) custom-call(f32[2048,512]{1,0:T(8,128)} %get-tuple-element.63.dy_in, f32[2048,512]{1,0:T(8,128)} %get-tuple-element.64.px.px_halo, ...), custom_call_target="tpu_custom_call" | custom-call | tf_op jit(solution)/shard_map/scan_backward/pallas_call | solution.py:584
  147.8 48.8 %tail.1 = (f32[2048,256]{1,0:T(8,128)}, f32[128,512]{1,0:T(8,128)}, f32[128,256]{1,0:T(8,128)}, f32[24,1024]{1,0:T(8,128)}) custom-call(bf16[1024,2048]{1,0:T(8,128)(2,1)} %get-tuple-element.62.normed_t_in, bf16[2048,512]{1,0:T(8,128)(2,1)} %get-tuple-element.72.lpx_in, bf16[1024,512]{1,0:T(8,128)(2,1)} %get-tuple-element.57.rows_z.rows_z_in, ...), custom_call_target="tpu_custom_call" | custom-call | tf_op jit(solution)/shard_map/tail/pallas_call | solution.py:957
  196.6 4.9 %finish.1 = (bf16[2048,256]{1,0:T(8,128)(2,1)}, f32[2048,256]{1,0:T(8,128)}, f32[128,512]{1,0:T(8,128)}, f32[128,512]{1,0:T(8,128)}, f32[128,512]{1,0:T(8,128)},...) custom-call(bf16[2048,256]{1,0:T(8,128)(2,1)} %get-tuple-element.71., ...), custom_call_target="tpu_custom_call" | custom-call | tf_op jit(solution)/shard_map/finish/pallas_call | solution.py:1422
  201.5 0.8 slice.3
  202.3 0.6 dynamic-slice_bitcast_fusion

commit v9 on v8

--- a/solution.py
+++ b/solution.py
@@ -1161,18 +1161,10 @@
         for h in (0, 1)
     ]
 
-    def offer(n):
-        cuts[n][0]()
-
     def other_half():
         cols = wbd.at[:, own_half]
         return push(cols, cols, s_sib.at[2], r_sib.at[2], who["sib"])
 
-    def pass_rows(n):
-        begin, begin_pair, hop, end = cuts[n]
-        begin_pair()
-        loop_line(lines, hop)
-
     def have(n):
         cuts[n][3]()
 
@@ -1181,16 +1173,14 @@
         cot_forward(j).start()
 
     to_x(0).start()
-    offer(0)
+    for begin, begin_pair, hop, end in cuts:
+        begin()
+        begin_pair()
     for s in range(1, units):
         to_x(s).start()
     to_sib().start()
-    for n in (1, 2, 3):
-        offer(n)
     for j in range(pieces):
         cot_x(j).start()
-    for begin, begin_pair, hop, end in chains:
-        begin()
     pack_vec(vec, conv_x, conv_bc, norm_gain, gate_gain, dt_bias, a_log, skip, starts, fill, chunk)
     set_upper(upper)
     set_spread(spread, heads)
@@ -1232,20 +1222,31 @@
         for copy in out_copies(s)[3:]:
             copy.start()
 
+    def hops(group, j):
+        if j < lines:
+            for begin, begin_pair, hop, end in group:
+                hop(j)
+
     local[0].wait()
+    hops(cuts, 1)
     to_x(0).wait()
     forward(0).start()
-    pass_rows(0)
+    hops(cuts, 2)
+    for begin, begin_pair, hop, end in chains:
+        begin()
     to_sib().wait()
     forward(0).wait()
     norm(0)
     to_x(1).wait()
     forward(1).start()
-    pass_rows(1)
+    hops(cuts, 3)
+    if lines > 4:
+        for begin, begin_pair, hop, end in cuts:
+            lax.fori_loop(4, lines, lambda j, a, fn=hop: (fn(j), a)[1], 0)
+    for begin, begin_pair, hop, end in chains:
+        begin_pair()
     forward(1).wait()
     norm(1)
-    pass_rows(2)
-    pass_rows(3)
     have(2)
     local[2].wait()
     other_half().start()
@@ -1262,6 +1263,7 @@
     for n in (0, 1, 3):
         have(n)
     other_half().wait()
+    hops(chains, 1)
     keep_rows = [
         pltpu.make_async_copy(wx, rows_x, s_loc.at[6]), pltpu.make_async_copy(wbd, rows_bd, s_loc.at[7]),
     ]
@@ -1280,11 +1282,12 @@
     late = []
     plan = []
     for n, (begin, begin_pair, hop, end) in enumerate(chains):
-        plan.append((lambda k, fn=begin_pair: fn(), 0, 1 + 2 * n))
-        for j in range(1, min(lines, 4)):
-            plan.append((hop, j, 1 + 2 * n + j))
+        if lines > 2:
+            plan.append((hop, 2, 1 + n // 2))
+        if lines > 3:
+            plan.append((hop, 3, 3 + n))
         if lines > 4:
-            plan.append((lambda k, fn=hop: lax.fori_loop(4, lines, lambda j, a: (fn(j), a)[1], 0), 0, 5 + 2 * n))
+            plan.append((lambda k, fn=hop: lax.fori_loop(4, lines, lambda j, a: (fn(j), a)[1], 0), 0, 7 + n))
     plan += [(pass_cot, j, 5 + 2 * j) for j in range(pieces)]
     for fn, k, at in plan:
         if at < blocks:

time: 203 us -> 192 us (0.946)
  Pallas kernels: 199 us -> 188 us
    pallas_call x1, Pallas kernels: 73.2 us -> 60.8 us  [front(): pl.pallas_call(functools.partial(front_kernel, dp_n, heads, units, taps,...]
where the time goes in v9:
time: 192 us; the launch traced here: 191 us
  Pallas kernels  188 us (98%)
  local copies, waits for them, and re-layouts  2.75 us (1%)
    pallas_call x1, Pallas kernels, front(): pl.pallas_call(functools.partial(front_kernel, dp_n, heads, units, taps,...  60.8 us
    pallas_call x1, Pallas kernels, tail(): pl.pallas_call(functools.partial(tail_kernel, dp_n, units), out_shape=[sd...  49.6 us
    pallas_call x1, Pallas kernels, scan_backward(): pl.pallas_call(functools.partial(scan_bwd_kernel, heads, taps, bc, dp_n),...  45.8 us
    pallas_call x1, Pallas kernels, gate(): pl.pallas_call(functools.partial(gate_kernel, dp_n), grid=(steps,), in_sp...  27 us
    pallas_call x1, Pallas kernels, finish(): pl.pallas_call(functools.partial(finish_kernel, heads, taps, bc), grid=(s...  4.93 us

profile of v9, /device:TPU:0, one launch (start us, length us, event | category | flops | bytes accessed | tf_op | source)
XLA Modules:
  0.0 191.5 jit_solution(18209057764149853804)
XLA Ops:
  0.6 1.4 copy.30.w_dt
  2.0 60.8 %front.1 = (f32[40,1024]{1,0:T(8,128)}, f32[2048,512]{1,0:T(8,128)}, f32[2048,384]{1,0:T(8,128)}, bf16[2048,1024]{1,0:T(8,128)(2,1)}, bf16[1024,2048]{1,0:T(8,12...) custom-call(bf16[2048,256]{1,0:T(8,128)(2,1)} %tokens.5, ...), custom_call_target="tpu_custom_call" | custom-call | tf_op jit(solution)/shard_map/front/pallas_call | solution.py:1368
  62.8 27.0 %gate.1 = (f32[2048,512]{1,0:T(8,128)}, bf16[2048,512]{1,0:T(8,128)(2,1)}, bf16[2048,512]{1,0:T(8,128)(2,1)}, bf16[4,512,256]{2,1,0:T(8,128)(2,1)}, f32[4,512,256]{2,1,0:T(8,128)}, /*index=5*/f32[8,512]{1,0:T(8,128)}) custom-call(bf16[2048,1024]{1,0:T(8,128)(2,1)} %get-tuple-element.56.normed.normed_in, ...), custom_call_target="tpu_custom_call" | custom-call | tf_op jit(solution)/shard_map/gate/pallas_call | solution.py:281
  89.8 45.8 %scan_backward.1 = (bf16[2048,512]{1,0:T(8,128)(2,1)}, bf16[2048,384]{1,0:T(8,128)(2,1)}, f32[8,1024]{1,0:T(8,128)}, bf16[2048,256]{1,0:T(8,128)(2,1)}, f32[128,512]{1,0:T(8,128)}, /*index=5*/f32[128,512]{1,0:T(8,128)}) custom-call(f32[2048,512]{1,0:T(8,128)} %get-tuple-element.63.dy_in, f32[2048,512]{1,0:T(8,128)} %get-tuple-element.64.px.px_halo, ...), custom_call_target="tpu_custom_call" | custom-call | tf_op jit(solution)/shard_map/scan_backward/pallas_call | solution.py:584
  135.6 49.6 %tail.1 = (f32[2048,256]{1,0:T(8,128)}, f32[128,512]{1,0:T(8,128)}, f32[128,256]{1,0:T(8,128)}, f32[24,1024]{1,0:T(8,128)}) custom-call(bf16[1024,2048]{1,0:T(8,128)(2,1)} %get-tuple-element.62.normed_t_in, bf16[2048,512]{1,0:T(8,128)(2,1)} %get-tuple-element.72.lpx_in, bf16[1024,512]{1,0:T(8,128)(2,1)} %get-tuple-element.57.rows_z.rows_z_in, ...), custom_call_target="tpu_custom_call" | custom-call | tf_op jit(solution)/shard_map/tail/pallas_call | solution.py:957
  185.2 4.9 %finish.1 = (bf16[2048,256]{1,0:T(8,128)(2,1)}, f32[2048,256]{1,0:T(8,128)}, f32[128,512]{1,0:T(8,128)}, f32[128,512]{1,0:T(8,128)}, f32[128,512]{1,0:T(8,128)},...) custom-call(bf16[2048,256]{1,0:T(8,128)(2,1)} %get-tuple-element.71., ...), custom_call_target="tpu_custom_call" | custom-call | tf_op jit(solution)/shard_map/finish/pallas_call | solution.py:1425
  190.1 0.8 slice.3
  190.9 0.6 dynamic-slice_bitcast_fusion

commit v10 on v9

--- a/solution.py
+++ b/solution.py
@@ -75,10 +75,11 @@
 
 def conv_from(ext, taps, rows, halo):
     n = taps.shape[0]
-    out = taps[n - 1 : n, :] * ext[pl.ds(halo, rows), :]
+    moved = [ext[pl.ds(halo - k, rows), :] for k in range(n)]
+    out = taps[n - 1 : n, :] * moved[0]
     for k in range(1, n):
-        out = out + taps[n - 1 - k : n - k, :] * ext[pl.ds(halo - k, rows), :]
-    return out
+        out = out + taps[n - 1 - k : n - k, :] * moved[k]
+    return out, moved
 
 
 def dt_rows(pdt, bias, rate, fill, heads, upper):
@@ -158,9 +159,9 @@
     extx[8 : chunk + 8, :] = px[...]
     extb[8 : chunk + 8, :] = pbd[:, :bc]
 
-    u = conv_from(extx, par["convx"], chunk, 8)
+    u, _ = conv_from(extx, par["convx"], chunk, 8)
     x = u * sigmoid(u) * (iota2(chunk, inner, 0).astype(F32) < n_live).astype(F32)
-    ub = conv_from(extb, par["convbc"], chunk, 8)
+    ub, _ = conv_from(extb, par["convbc"], chunk, 8)
     act = (ub * sigmoid(ub) * (iota2(chunk, bc, 0).astype(F32) < n_live).astype(F32)).astype(BF)
     b, cc = act[:, :ns], act[:, ns:]
 
@@ -260,11 +261,13 @@
             dy_out[at, :] = d_gated * silu_z
         load.wait()
         block = grad_t.shape[0] // dp_n
-        for v in range(4):
-            left, right = ((grad_t, gn), (normed_t, lpz))[v // 2]
-            cols = slice((v % 2) * (inner // 2), (v % 2 + 1) * (inner // 2))
-            y_send[v] = nn(pair_rows(dp_n, block, 1 - who["pair"], left), right[:, cols]).astype(BF)
-            g_own[v] = nn(pair_rows(dp_n, block, who["pair"], left), right[:, cols])
+        for v, (left, right) in enumerate(((grad_t, gn), (normed_t, lpz))):
+            theirs = nn(pair_rows(dp_n, block, 1 - who["pair"], left), right[...])
+            ours = nn(pair_rows(dp_n, block, who["pair"], left), right[...])
+            for h in (0, 1):
+                cols = slice(h * (inner // 2), (h + 1) * (inner // 2))
+                y_send[2 * v + h] = theirs[:, cols].astype(BF)
+                g_own[2 * v + h] = ours[:, cols]
 
 
 def gate(dp_n, blocks, normed, normed_t, rows_z, rows_out, parts, y, vec):
@@ -438,11 +441,11 @@
     extb[8 : chunk + 8, :] = pbd[:, :bc]
     live_x = (iota2(chunk, inner, 0).astype(F32) < n_live).astype(F32)
     live_b = (iota2(chunk, bc, 0).astype(F32) < n_live).astype(F32)
-    u = conv_from(extx, taps, chunk, 8)
+    u, moved_x = conv_from(extx, taps, chunk, 8)
     su = sigmoid(u)
     x = u * su * live_x
     dx_du = su * (1.0 + u * (1.0 - su)) * live_x
-    ub = conv_from(extb, taps_b, chunk, 8)
+    ub, moved_b = conv_from(extb, taps_b, chunk, 8)
     sb = sigmoid(ub)
     act = (ub * sb * live_b).astype(BF)
     db_du = sb * (1.0 + ub * (1.0 - sb)) * live_b
@@ -525,23 +528,21 @@
     acc_s[0:heads, :] += d_pre
     acc_s[heads : 2 * heads, :] += d_a * dt * rate
 
-    def conv_back(d_u, du_ref, ext_ref, tap_values, acc):
+    def conv_back(d_u, du_ref, moved, tap_values, acc):
         du_ref[chunk : chunk + 8, :] = jnp.where(keep_next, du_ref[0:8, :], 0.0)
         du_ref[0:chunk, :] = d_u
         out = tap_values[taps_n - 1 : taps_n, :] * d_u
-        acc[taps_n - 1 : taps_n, :] += jnp.sum(d_u * ext_ref[8 : chunk + 8, :], axis=0, keepdims=True)
+        acc[taps_n - 1 : taps_n, :] += jnp.sum(d_u * moved[0], axis=0, keepdims=True)
         for k in range(1, taps_n):
             row = taps_n - 1 - k
             out = out + tap_values[row : row + 1, :] * du_ref[pl.ds(k, chunk), :]
-            acc[row : row + 1, :] += jnp.sum(
-                d_u * ext_ref[pl.ds(8 - k, chunk), :], axis=0, keepdims=True
-            )
+            acc[row : row + 1, :] += jnp.sum(d_u * moved[k], axis=0, keepdims=True)
         return out
 
     d_x = d_xd * dt_w + skip * dy
-    lpx[...] = conv_back(d_x * dx_du, dux, extx, taps, acc_x).astype(BF)
+    lpx[...] = conv_back(d_x * dx_du, dux, moved_x, taps, acc_x).astype(BF)
     d_act = jnp.concatenate([d_b, d_cb], axis=1)
-    lpbd[:, :bc] = conv_back(d_act * db_du, dub, extb, taps_b, acc_bc).astype(BF)
+    lpbd[:, :bc] = conv_back(d_act * db_du, dub, moved_b, taps_b, acc_bc).astype(BF)
     pad = jnp.concatenate([d_pre, jnp.zeros((chunk - heads, chunk), F32)], axis=0)
     lpbd[:, bc:] = jnp.transpose(pad).astype(BF)
 

time: 192 us -> 192 us (level)
  no operation moved by 1% of the time
where the time goes in v10:
time: 192 us; the launch traced here: 191 us
  Pallas kernels  188 us (98%)
  local copies, waits for them, and re-layouts  2.75 us (1%)
    pallas_call x1, Pallas kernels, front(): pl.pallas_call(functools.partial(front_kernel, dp_n, heads, units, taps,...  60.8 us
    pallas_call x1, Pallas kernels, tail(): pl.pallas_call(functools.partial(tail_kernel, dp_n, units), out_shape=[sd...  49.6 us
    pallas_call x1, Pallas kernels, scan_backward(): pl.pallas_call(functools.partial(scan_bwd_kernel, heads, taps, bc, dp_n),...  45.5 us
    pallas_call x1, Pallas kernels, gate(): pl.pallas_call(functools.partial(gate_kernel, dp_n), grid=(steps,), in_sp...  27 us
    pallas_call x1, Pallas kernels, finish(): pl.pallas_call(functools.partial(finish_kernel, heads, taps, bc), grid=(s...  4.93 us

profile of v10, /device:TPU:0, one launch (start us, length us, event | category | flops | bytes accessed | tf_op | source)
XLA Modules:
  0.0 191.2 jit_solution(2691202248634763629)
XLA Ops:
  0.6 1.4 copy.30.w_dt
  2.0 60.8 %front.1 = (f32[40,1024]{1,0:T(8,128)}, f32[2048,512]{1,0:T(8,128)}, f32[2048,384]{1,0:T(8,128)}, bf16[2048,1024]{1,0:T(8,128)(2,1)}, bf16[1024,2048]{1,0:T(8,12...) custom-call(bf16[2048,256]{1,0:T(8,128)(2,1)} %tokens.5, ...), custom_call_target="tpu_custom_call" | custom-call | tf_op jit(solution)/shard_map/front/pallas_call | solution.py:1369
  62.8 27.0 %gate.1 = (f32[2048,512]{1,0:T(8,128)}, bf16[2048,512]{1,0:T(8,128)(2,1)}, bf16[2048,512]{1,0:T(8,128)(2,1)}, bf16[4,512,256]{2,1,0:T(8,128)(2,1)}, f32[4,512,256]{2,1,0:T(8,128)}, /*index=5*/f32[8,512]{1,0:T(8,128)}) custom-call(bf16[2048,1024]{1,0:T(8,128)(2,1)} %get-tuple-element.56.normed.normed_in, ...), custom_call_target="tpu_custom_call" | custom-call | tf_op jit(solution)/shard_map/gate/pallas_call | solution.py:284
  89.8 45.5 %scan_backward.1 = (bf16[2048,512]{1,0:T(8,128)(2,1)}, bf16[2048,384]{1,0:T(8,128)(2,1)}, f32[8,1024]{1,0:T(8,128)}, bf16[2048,256]{1,0:T(8,128)(2,1)}, f32[128,512]{1,0:T(8,128)}, /*index=5*/f32[128,512]{1,0:T(8,128)}) custom-call(f32[2048,512]{1,0:T(8,128)} %get-tuple-element.63.dy_in, f32[2048,512]{1,0:T(8,128)} %get-tuple-element.64.px.px_halo, ...), custom_call_target="tpu_custom_call" | custom-call | tf_op jit(solution)/shard_map/scan_backward/pallas_call | solution.py:585
  135.3 49.6 %tail.1 = (f32[2048,256]{1,0:T(8,128)}, f32[128,512]{1,0:T(8,128)}, f32[128,256]{1,0:T(8,128)}, f32[24,1024]{1,0:T(8,128)}) custom-call(bf16[1024,2048]{1,0:T(8,128)(2,1)} %get-tuple-element.62.normed_t_in, bf16[2048,512]{1,0:T(8,128)(2,1)} %get-tuple-element.72.lpx_in, bf16[1024,512]{1,0:T(8,128)(2,1)} %get-tuple-element.57.rows_z.rows_z_in, ...), custom_call_target="tpu_custom_call" | custom-call | tf_op jit(solution)/shard_map/tail/pallas_call | solution.py:958
  184.9 4.9 %finish.1 = (bf16[2048,256]{1,0:T(8,128)(2,1)}, f32[2048,256]{1,0:T(8,128)}, f32[128,512]{1,0:T(8,128)}, f32[128,512]{1,0:T(8,128)}, f32[128,512]{1,0:T(8,128)},...) custom-call(bf16[2048,256]{1,0:T(8,128)(2,1)} %get-tuple-element.71., ...), custom_call_target="tpu_custom_call" | custom-call | tf_op jit(solution)/shard_map/finish/pallas_call | solution.py:1426
  189.9 0.8 slice.3
  190.6 0.6 dynamic-slice_bitcast_fusion

commit v11 on v10

--- a/solution.py
+++ b/solution.py
@@ -274,7 +274,7 @@
     count, width = normed.shape
     inner = y.shape[1]
     chunk = count // blocks
-    steps = 8
+    steps = 4
     span = count // steps
     quarter = width // 4
     sds = jax.ShapeDtypeStruct

time: 192 us -> 190 us (0.990)
  Pallas kernels: 188 us -> 186 us
where the time goes in v11:
time: 190 us; the launch traced here: 189 us
  Pallas kernels  186 us (98%)
  local copies, waits for them, and re-layouts  2.75 us (1%)
    pallas_call x1, Pallas kernels, front(): pl.pallas_call(functools.partial(front_kernel, dp_n, heads, units, taps,...  60.8 us
    pallas_call x1, Pallas kernels, tail(): pl.pallas_call(functools.partial(tail_kernel, dp_n, units), out_shape=[sd...  49.6 us
    pallas_call x1, Pallas kernels, scan_backward(): pl.pallas_call(functools.partial(scan_bwd_kernel, heads, taps, bc, dp_n),...  45.6 us
    pallas_call x1, Pallas kernels, gate(): pl.pallas_call(functools.partial(gate_kernel, dp_n), grid=(steps,), in_sp...  25.2 us
    pallas_call x1, Pallas kernels, finish(): pl.pallas_call(functools.partial(finish_kernel, heads, taps, bc), grid=(s...  4.93 us

profile of v11, /device:TPU:0, one launch (start us, length us, event | category | flops | bytes accessed | tf_op | source)
XLA Modules:
  0.0 189.5 jit_solution(15956724558173076606)
XLA Ops:
  0.6 1.4 copy.30.w_dt
  2.0 60.8 %front.1 = (f32[40,1024]{1,0:T(8,128)}, f32[2048,512]{1,0:T(8,128)}, f32[2048,384]{1,0:T(8,128)}, bf16[2048,1024]{1,0:T(8,128)(2,1)}, bf16[1024,2048]{1,0:T(8,12...) custom-call(bf16[2048,256]{1,0:T(8,128)(2,1)} %tokens.5, ...), custom_call_target="tpu_custom_call" | custom-call | tf_op jit(solution)/shard_map/front/pallas_call | solution.py:1369
  62.8 25.2 %gate.1 = (f32[2048,512]{1,0:T(8,128)}, bf16[2048,512]{1,0:T(8,128)(2,1)}, bf16[2048,512]{1,0:T(8,128)(2,1)}, bf16[4,512,256]{2,1,0:T(8,128)(2,1)}, f32[4,512,256]{2,1,0:T(8,128)}, /*index=5*/f32[8,512]{1,0:T(8,128)}) custom-call(bf16[2048,1024]{1,0:T(8,128)(2,1)} %get-tuple-element.56.normed.normed_in, ...), custom_call_target="tpu_custom_call" | custom-call | tf_op jit(solution)/shard_map/gate/pallas_call | solution.py:284
  88.0 45.6 %scan_backward.1 = (bf16[2048,512]{1,0:T(8,128)(2,1)}, bf16[2048,384]{1,0:T(8,128)(2,1)}, f32[8,1024]{1,0:T(8,128)}, bf16[2048,256]{1,0:T(8,128)(2,1)}, f32[128,512]{1,0:T(8,128)}, /*index=5*/f32[128,512]{1,0:T(8,128)}) custom-call(f32[2048,512]{1,0:T(8,128)} %get-tuple-element.63.dy_in, f32[2048,512]{1,0:T(8,128)} %get-tuple-element.64.px.px_halo, ...), custom_call_target="tpu_custom_call" | custom-call | tf_op jit(solution)/shard_map/scan_backward/pallas_call | solution.py:585
  133.6 49.6 %tail.1 = (f32[2048,256]{1,0:T(8,128)}, f32[128,512]{1,0:T(8,128)}, f32[128,256]{1,0:T(8,128)}, f32[24,1024]{1,0:T(8,128)}) custom-call(bf16[1024,2048]{1,0:T(8,128)(2,1)} %get-tuple-element.62.normed_t_in, bf16[2048,512]{1,0:T(8,128)(2,1)} %get-tuple-element.72.lpx_in, bf16[1024,512]{1,0:T(8,128)(2,1)} %get-tuple-element.57.rows_z.rows_z_in, ...), custom_call_target="tpu_custom_call" | custom-call | tf_op jit(solution)/shard_map/tail/pallas_call | solution.py:958
  183.2 4.9 %finish.1 = (bf16[2048,256]{1,0:T(8,128)(2,1)}, f32[2048,256]{1,0:T(8,128)}, f32[128,512]{1,0:T(8,128)}, f32[128,512]{1,0:T(8,128)}, f32[128,512]{1,0:T(8,128)},...) custom-call(bf16[2048,256]{1,0:T(8,128)(2,1)} %get-tuple-element.71., ...), custom_call_target="tpu_custom_call" | custom-call | tf_op jit(solution)/shard_map/finish/pallas_call | solution.py:1426
  188.1 0.8 slice.3
  188.9 0.6 dynamic-slice_bitcast_fusion
